TPU v7x, 256 devices: a whole 4x4x8 slice. The times are simulated.
256 devices in a mesh: seq: 128 (over z, y, x_lo, core), cfg: 2 (over x_hi).
Axes of the slice: x: 4 (x_hi: 2, x_lo: 2; x = x_hi * 2 + x_lo), y: 4, z: 8, core: 2. Of those that a mesh axis runs over, the one named last changes fastest.
Arguments:
- queries: bfloat16 [65536, 2560], P(('cfg', 'seq')), parts along dimension 0, may hold values from -40 to 40
- latent_keys: bfloat16 [65536, 2560], P(('cfg', 'seq')), parts along dimension 0, may hold values from -6 to 6
- latent_values: bfloat16 [65536, 2560], P(('cfg', 'seq')), parts along dimension 0, may hold values from -6 to 6
- prompt_keyvals: bfloat16 [2, 2048, 2560], P(None, ('cfg', 'seq')), parts along dimension 1, may hold values from -9 to 9
- block_lists: int32 [256, 8], P('seq'), may hold values from -1 to 255, as said below
- tile_segment: int32 [128], P('seq'), may hold values from 0 to 3
Outputs:
- attended: bfloat16 [65536, 2560], P(('cfg', 'seq')), parts along dimension 0
There are 2 independent parts, one for each index of `cfg`. A program takes and returns all parts, laid end to end along the dimension named above; an argument that names none is the same for every part. Nothing has to cross between parts.
Inputs may be any that keep to these rules, and one draw needn't show every extreme that they name: `block_lists`: row b lists distinct key blocks, all held by indices of seq at most 3 away from the one holding query block b (each index holds 2 blocks in order); b itself comes first, used entries precede the -1 entries, and some row fills all 8.
All inputs are finite; a program needn't handle non-finite values.
Results may differ from a plain program's by a relative error of at most 0.0035.
Values may be sent and summed in bfloat16 or wider, within the bound.
No kernel may reach another device: no remote copies, remote signals or barrier semaphores. Data moves between devices by JAX's collectives and lax.ppermute only.
A program may use at most 128 MiB of HBM per device.

v0:
```python
import math

import jax
import jax.numpy as jnp
from jax import lax
from jax.sharding import PartitionSpec as P

HD = 128
BLK = 128
REACH = 3
TXT = 256


def from_behind(block, axis, distance):
    devices = range(lax.axis_size(axis))
    route = [(i - distance, i) for i in devices if i - distance in devices]
    return lax.ppermute(block, axis, route)


def on_device(queries, latent_keys, latent_values, prompt_keyvals, block_lists, tile_segment):
    tok_rows, width = queries.shape
    heads = width // HD
    per_device = tok_rows // BLK
    window_blocks = (2 * REACH + 1) * per_device
    scale = 1.0 / math.sqrt(HD)
    device = lax.axis_index("seq")
    own_pair = jnp.stack([latent_keys, latent_values])
    lower_tiles = []
    upper_tiles = []
    moving_up = own_pair
    moving_down = own_pair
    for travel in range(REACH):
        moving_up = from_behind(moving_up, "seq", 1)
        lower_tiles.append(moving_up)
        moving_down = from_behind(moving_down, "seq", -1)
        upper_tiles.append(moving_down)
    window = jnp.concatenate(lower_tiles[::-1] + [own_pair] + upper_tiles, axis=1)
    whole_text = lax.all_gather(prompt_keyvals, "seq", axis=1, tiled=True)
    segment = tile_segment[0]
    own_text = lax.dynamic_slice_in_dim(whole_text, segment * TXT, TXT, 1)
    first_block = (device - REACH) * per_device
    empty = jnp.zeros((tok_rows, width), jnp.bfloat16)
    numbers = first_block + jnp.arange(window_blocks, dtype=jnp.int32)
    listed = (block_lists[:, :, None] == numbers[None, None, :]) & (block_lists[:, :, None] >= 0)
    block_mask = jnp.any(listed, axis=1)
    row_mask = jnp.repeat(jnp.repeat(block_mask, BLK, axis=0), BLK, axis=1)
    allowed = jnp.concatenate([row_mask, jnp.ones((tok_rows, TXT), dtype=bool)], axis=1)
    all_keys = jnp.concatenate([window[0], own_text[0]], axis=0)
    all_values = jnp.concatenate([window[1], own_text[1]], axis=0)

    def attend_head(head_index, result):
        start = head_index * HD
        head_query = lax.dynamic_slice_in_dim(queries, start, HD, 1)
        head_keys = lax.dynamic_slice_in_dim(all_keys, start, HD, 1)
        head_values = lax.dynamic_slice_in_dim(all_values, start, HD, 1)
        scores = (
            jnp.einsum("qd,kd->qk", head_query, head_keys, preferred_element_type=jnp.float32)
            * scale
        )
        top = jnp.max(jnp.where(allowed, scores, -jnp.inf), axis=1, keepdims=True)
        weights = jnp.where(allowed, jnp.exp(scores - top), 0.0)
        total = jnp.sum(weights, axis=1, keepdims=True)
        mixed = (
            jnp.dot(weights.astype(jnp.bfloat16), head_values, preferred_element_type=jnp.float32)
            / total
        )
        return lax.dynamic_update_slice_in_dim(result, mixed.astype(jnp.bfloat16), start, 1)

    attended = lax.fori_loop(0, heads, attend_head, empty)
    return attended


def solution(mesh):
    in_specs = (
        P(("cfg", "seq"), None),
        P(("cfg", "seq"), None),
        P(("cfg", "seq"), None),
        P(None, ("cfg", "seq"), None),
        P("seq", None),
        P("seq"),
    )
    out_specs = P(("cfg", "seq"), None)
    return jax.shard_map(
        on_device, mesh=mesh, in_specs=in_specs, out_specs=out_specs, check_vma=False
    )
```

profile of v0, /device:TPU:4, one launch (start us, length us, event | category | flops | bytes accessed | tf_op | source)
XLA Modules:
  0.0 437.0 jit_solution(2258392231643403699)
XLA Ops:
  7.3 2.0 pad_maximum_fusion.2
  9.2 1.9 collective-permute-start
  12.4 3.1 collective-permute-done
  15.5 98.6 %collective-permute-start.1 = (bf16[2,256,2560]{2,1,0:T(8,128)(2,1)S(1)}, bf16[2,256,2560]{2,1,0:T(8,128)(2,1)}, u32[]{:S(2)}, u32[]{:S(2)}) collective-permute-start(bf16[2,256,2560]{2,1,0:T(8,128)(2,1)S(1)} %collective-permute-done), channel_id=1, source_target_pairs={{0,2},{2,4},{4,6},{6,8},{8,10},{10,12},{12,14},{14,16},{16,18},{18... | collective-permute-start | bytes 7864328 | tf_op jit(solution)/shard_map/ppermute | solution.py:17
  115.4 1.9 collective-permute-done.1
  117.3 64.8 %collective-permute-start.2 = (bf16[2,256,2560]{2,1,0:T(8,128)(2,1)}, bf16[2,256,2560]{2,1,0:T(8,128)(2,1)}, u32[]{:S(2)}, u32[]{:S(2)}) collective-permute-start(bf16[2,256,2560]{2,1,0:T(8,128)(2,1)} %collective-permute-done.1), channel_id=1, source_target_pairs={{0,2},{2,4},{4,6},{6,8},{8,10},{10,12},{12,14},{14,16},{16,18},{18... | collective-permute-start | bytes 7864328 | tf_op jit(solution)/shard_map/ppermute | solution.py:17
  187.2 1.9 constant_dynamic-update-slice_fusion.6
  189.1 2.1 constant_dynamic-update-slice_fusion.5
  193.8 1.9 constant_dynamic-update-slice_fusion.1
  195.7 2.0 constant_dynamic-update-slice_fusion
  197.7 6.8 %slice_bitcast_fusion = (bf16[1792,2560]{1,0:T(8,128)(2,1)}, bf16[1792,2560]{1,0:T(8,128)(2,1)}) fusion(bf16[2,1792,2560]{2,1,0:T(8,128)(2,1)S(1)} %constant_dynamic-update-slice_fusion), kind=kLoop, calls=%fused_computation.18 | loop fusion | bytes 36700160 | tf_op jit(solution)/shard_map/squeeze | solution.py:49
  204.5 126.9 %all-gather.2.cloned.1.call-done = bf16[2,1024,2560]{2,1,0:T(8,128)(2,1)} async-done(((bf16[2,8,2560]{2,1,0:T(8,128)(2,1)}), bf16[2,1024,2560]{2,1,0:T(8,128)(2,1)}) %all-gather.2.cloned.1.call-update) | async-done | bytes 10485776 | tf_op jit(solution)/shard_map/all_gather | solution.py:38
  331.3 1.9 dynamic-slice_bitcast_fusion
  333.2 14.7 %pad_maximum_fusion = (bf16[2048,2560]{1,0:T(8,128)(2,1)}, bf16[2048,2560]{1,0:T(8,128)(2,1)}) fusion(bf16[256,2560]{1,0:T(8,128)(2,1)S(1)} %get-tuple-element.150, bf16[1792,2560]{1,0:T(8,128)(2,1)} %get-tuple-element.148, bf16[256,2560]{1,0:T(8,128)(2,1)S(1)} %get-tuple-element.149, bf16[1792,2560]{1,0:T(8,128)(2,1)} %get-tuple-element.147), kind=kLoop, calls=%fused_computation.16 | loop fusion | flops 41943040 | bytes 41943040 | tf_op jit(solution)/shard_map/concatenate | solution.py:48
  348.1 81.0 %while.13 = (s32[]{:T(128)}, bf16[256,2560]{1,0:T(8,128)(2,1)S(1)}, bf16[256,2560]{1,0:T(8,128)(2,1)}, bf16[2048,2560]{1,0:T(8,128)(2,1)}, pred[256,2048]{1,0:T(...) while((s32[]{:T(128)}, bf16[256,2560]{1,0:T(8,128)(2,1)S(1)}, ...), condition=%wide.region_4.5_spmd, body=%wide.region_1.4_spmd.sunk | while | flops 273219072 | bytes 9051283 | solution.py:69
  350.4 1.7 fusion.20
  354.4 1.7 fusion.20
  358.5 1.7 fusion.20
  362.5 1.7 fusion.20
  366.6 1.7 fusion.20
  370.6 1.7 fusion.20
  374.7 1.7 fusion.20
  378.7 1.7 fusion.20
  382.8 1.7 fusion.20
  386.8 1.7 fusion.20
  390.9 1.7 fusion.20
  394.9 1.7 fusion.20
  399.0 1.7 fusion.20
  403.0 1.7 fusion.20
  407.1 1.7 fusion.20
  411.1 1.7 fusion.20
  415.2 1.7 fusion.20
  (78 shorter events, 62.6 us)
Async XLA Ops:
  6.5 324.8 %all-gather.2.cloned.1.call-start = ((), (), s32[]{:S(2)}) async-start(), calls=%async_computation | async-start | bytes 10567680 | tf_op jit(solution)/shard_map/all_gather | solution.py:38
  7.3 175.5 %copy-start.5 = (s32[2,8]{1,0:T(2,128)S(1)}, s32[2,8]{1,0:T(2,128)}, u32[]{:S(2)}) copy-start(s32[2,8]{1,0:T(2,128)} %param.12) | copy-start | bytes 196
  9.2 6.3 %collective-permute-start = (bf16[2,256,2560]{2,1,0:T(8,128)(2,1)S(1)}, bf16[2,256,2560]{2,1,0:T(8,128)(2,1)S(1)}, u32[]{:S(2)}, u32[]{:S(2)}) collective-permute-start(bf16[2,256,2560]{2,1,0:T(8,128)(2,1)S(1)} %pad_maximum_fusion.2), channel_id=1, source_target_pairs={{0,2},{2,4},{4,6},{6,8},{8,10},{10,12},{12,14},{14,16},{16,18},{18... | collective-permute-start | bytes 7864328 | tf_op jit(solution)/shard_map/ppermute | solution.py:17
  11.1 103.0 %collective-permute-start.3 = (bf16[2,256,2560]{2,1,0:T(8,128)(2,1)S(1)}, bf16[2,256,2560]{2,1,0:T(8,128)(2,1)S(1)}, u32[]{:S(2)}, u32[]{:S(2)}) collective-permute-start(bf16[2,256,2560]{2,1,0:T(8,128)(2,1)S(1)} %pad_maximum_fusion.2), channel_id=1, source_target_pairs={{2,0},{4,2},{6,4},{8,6},{10,8},{12,10},{14,12},{16,14},{18,16},{20... | collective-permute-start | bytes 7864328 | tf_op jit(solution)/shard_map/ppermute | solution.py:17
  15.5 98.6 %copy-start.2 = (bf16[2,256,2560]{2,1,0:T(8,128)(2,1)}, bf16[2,256,2560]{2,1,0:T(8,128)(2,1)S(1)}, u32[]{:S(2)}) copy-start(bf16[2,256,2560]{2,1,0:T(8,128)(2,1)S(1)} %collective-permute-done) | copy-start | bytes 7864324
  15.5 101.8 %collective-permute-start.1 = (bf16[2,256,2560]{2,1,0:T(8,128)(2,1)S(1)}, bf16[2,256,2560]{2,1,0:T(8,128)(2,1)}, u32[]{:S(2)}, u32[]{:S(2)}) collective-permute-start(bf16[2,256,2560]{2,1,0:T(8,128)(2,1)S(1)} %collective-permute-done), channel_id=1, source_target_pairs={{0,2},{2,4},{4,6},{6,8},{8,10},{10,12},{12,14},{14,16},{16,18},{18... | collective-permute-start | bytes 7864328 | tf_op jit(solution)/shard_map/ppermute | solution.py:17
  114.1 68.9 %collective-permute-start.4 = (bf16[2,256,2560]{2,1,0:T(8,128)(2,1)S(1)}, bf16[2,256,2560]{2,1,0:T(8,128)(2,1)}, u32[]{:S(2)}, u32[]{:S(2)}) collective-permute-start(bf16[2,256,2560]{2,1,0:T(8,128)(2,1)S(1)} %collective-permute-done.3), channel_id=1, source_target_pairs={{2,0},{4,2},{6,4},{8,6},{10,8},{12,10},{14,12},{16,14},{18,16},{20... | collective-permute-start | bytes 7864328 | tf_op jit(solution)/shard_map/ppermute | solution.py:17
  117.3 69.9 %collective-permute-start.2 = (bf16[2,256,2560]{2,1,0:T(8,128)(2,1)}, bf16[2,256,2560]{2,1,0:T(8,128)(2,1)}, u32[]{:S(2)}, u32[]{:S(2)}) collective-permute-start(bf16[2,256,2560]{2,1,0:T(8,128)(2,1)} %collective-permute-done.1), channel_id=1, source_target_pairs={{0,2},{2,4},{4,6},{6,8},{8,10},{10,12},{12,14},{14,16},{16,18},{18... | collective-permute-start | bytes 7864328 | tf_op jit(solution)/shard_map/ppermute | solution.py:17
  183.0 12.7 %collective-permute-start.5 = (bf16[2,256,2560]{2,1,0:T(8,128)(2,1)}, bf16[2,256,2560]{2,1,0:T(8,128)(2,1)}, u32[]{:S(2)}, u32[]{:S(2)}) collective-permute-start(bf16[2,256,2560]{2,1,0:T(8,128)(2,1)} %collective-permute-done.4), channel_id=1, source_target_pairs={{2,0},{4,2},{6,4},{8,6},{10,8},{12,10},{14,12},{16,14},{18,16},{20... | collective-permute-start | bytes 7864328 | tf_op jit(solution)/shard_map/ppermute | solution.py:17
  189.1 2.6 copy-start.3
  191.7 1.3 copy-start
  191.7 1.7 copy-start.1
  429.1 1.1 copy-start.4
Sparse Core Ops, SparseCore 0:
  9.2 322.1 all-gather.1
where the time goes:
time: 439 us; the launch traced here: 437 us
  starting transfers between devices  169 us (38%)
  waiting for transfers between devices  133 us (30%)
  matrix products  67.7 us (15%)
  other arithmetic  29.9 us (7%)
  local copies, waits for them, and re-layouts  23 us (5%)
  between operations  14.2 us (3%)
    ppermute x6, starting transfers between devices, from_behind(): return lax.ppermute(block, axis, route)  169 us
    all_gather x1, waiting for transfers between devices, on_device(): whole_text = lax.all_gather(prompt_keyvals, 'seq', axis=1, tiled=True)  127 us
    dot_general x20, matrix products, attend_head(): jnp.dot(weights.astype(jnp.bfloat16), head_values, preferred_element_type...  34.4 us
    dot_general x20, matrix products, attend_head(): jnp.einsum('qd,kd->qk', head_query, head_keys, preferred_element_type=jnp...  33.3 us
    concatenate x1, other arithmetic, on_device(): all_keys = jnp.concatenate([window[0], own_text[0]], axis=0)  14.7 us
    reduce_sum x20, other arithmetic, attend_head(): total = jnp.sum(weights, axis=1, keepdims=True)  12.9 us
    unnamed x21, local copies, waits for them, and re-layouts  10.8 us
  transfers between devices with their start and end apart: 7, of which 3 were waited for; matrix products, arithmetic and copies ran while one was open for 5% of the time, Pallas kernels for 0%

commit v1 on v0

v1 whole, which is shorter than its diff:
```python
import functools
import math

import jax
import jax.numpy as jnp
from jax import lax
from jax.experimental import pallas as pl
from jax.experimental.pallas import tpu as pltpu
from jax.sharding import PartitionSpec as P

HD = 128
BLK = 128
TOK = 256
ZN, YN, XN, CN = 8, 4, 2, 2
ROWS = ZN * YN
HALF = 10
CHUNKS = (3, 4, 3)
NEG = -1e30
C2 = math.log2(math.e) / math.sqrt(HD)


def place(row, x, core):
    return ((row % ROWS) * XN + x % XN) * CN + core % CN


DEVICES = [(r, x, c) for r in range(ROWS) for x in range(XN) for c in range(CN)]


def route(to):
    return [(place(*d), place(*to(*d))) for d in DEVICES]


ACROSS = route(lambda r, x, c: (r, 1 - x, c))
CORES = route(lambda r, x, c: (r, x, 1 - c))
OUTWARD = route(lambda r, x, c: (r + (1 if c else -1), x, c))
INWARD = route(lambda r, x, c: (r + (-1 if c else 1), x, c))
ZUP = route(lambda r, x, c: (r + YN, x, c))
ZDOWN = route(lambda r, x, c: (r - YN, x, c))
PLANES = [
    [place(z * YN + y, x, c) for y in range(YN) for x in range(XN)]
    for z in range(ZN)
    for c in range(CN)
]


def send(block, to):
    return lax.ppermute(block, "seq", to)


def attend_kernel(
    half_ref, slots_ref, valid_ref, text_at_ref,
    q_own, q_far, k_own, v_own, far, out_own, out_far, mid, cc_fix, cc_part, text, cc_text,
    o_own, o_far, keys, values,
):
    tiles = [
        (k_own, v_own),
        (far.at[0], far.at[1]),
        (out_own.at[0], out_own.at[1]),
        (out_far.at[0], out_far.at[1]),
        (mid.at[0], mid.at[1]),
        (cc_fix.at[0, 0], cc_fix.at[0, 1]),
        (cc_part.at[0, 0], cc_part.at[0, 1]),
        (cc_fix.at[1, 0], cc_fix.at[1, 1]),
        (cc_part.at[1, 0], cc_part.at[1, 1]),
        (cc_part.at[2, 0], cc_part.at[2, 1]),
    ]
    for at, (k, v) in enumerate(tiles):
        keys[at * TOK : (at + 1) * TOK, :] = k[...]
        values[at * TOK : (at + 1) * TOK, :] = v[...]
    for tile, (q_ref, o_ref) in enumerate(((q_own, o_own), (q_far, o_far))):
        first, second = text_at_ref[tile, 0], text_at_ref[tile, 1]
        text_k = [ref[at, 0] for ref in (text, cc_text) for at in (first, second)]
        text_v = [ref[at, 1] for ref in (text, cc_text) for at in (first, second)]
        for block in range(TOK // BLK):
            row = tile * 2 + block
            rows = slice(block * BLK, (block + 1) * BLK)
            starts = [pl.multiple_of(slots_ref[row, s] * BLK, BLK) for s in range(8)]
            all_k = jnp.concatenate([keys[pl.ds(at, BLK), :] for at in starts] + text_k, axis=0)
            all_v = jnp.concatenate([values[pl.ds(at, BLK), :] for at in starts] + text_v, axis=0)
            scores = lax.dot_general(
                q_ref[rows, :], all_k, (((1,), (1,)), ((), ())), preferred_element_type=jnp.float32
            )
            scores = jnp.concatenate(
                [scores[:, :BLK]]
                + [
                    jnp.where(valid_ref[row, s] > 0, scores[:, s * BLK : (s + 1) * BLK], NEG)
                    for s in range(1, 8)
                ]
                + [scores[:, 8 * BLK :]],
                axis=1,
            )
            top = jnp.max(scores, axis=1, keepdims=True)
            weights = jnp.exp2((scores - top) * C2)
            total = jnp.sum(weights, axis=1, keepdims=True)
            mixed = jnp.dot(weights.astype(jnp.bfloat16), all_v, preferred_element_type=jnp.float32)
            o_ref[rows, :] = (mixed / total).astype(jnp.bfloat16)


def attend(first, heads, scalars, q_own, q_far, k_own, v_own, far, out_own, out_far, mid, cc_fix, cc_part, text, cc_text):
    def whole(i, half, *_):
        return (0, half[0] * HALF + first + i)

    def halved(lead):
        return lambda i, *_: (0,) * lead + (first + i,)

    def chunk(lead):
        return lambda i, *_: (0,) * lead + (i,)

    specs = [
        pl.BlockSpec((TOK, HD), whole),
        pl.BlockSpec((TOK, HD), halved(1)),
        pl.BlockSpec((TOK, HD), whole),
        pl.BlockSpec((TOK, HD), whole),
        pl.BlockSpec((2, TOK, HD), chunk(2)),
        pl.BlockSpec((2, TOK, HD), halved(2)),
        pl.BlockSpec((2, TOK, HD), chunk(2)),
        pl.BlockSpec((2, TOK, HD), chunk(2)),
        pl.BlockSpec((2, 2, TOK, HD), halved(3)),
        pl.BlockSpec((3, 2, TOK, HD), chunk(3)),
        pl.BlockSpec((ZN, 2, 64, HD), halved(3)),
        pl.BlockSpec((ZN, 2, 64, HD), halved(3)),
    ]
    out = jax.ShapeDtypeStruct((TOK, heads * HD), jnp.bfloat16)
    return pl.pallas_call(
        attend_kernel,
        out_shape=(out, out),
        grid_spec=pltpu.PrefetchScalarGridSpec(
            num_scalar_prefetch=4,
            grid=(heads,),
            in_specs=specs,
            out_specs=(pl.BlockSpec((TOK, HD), chunk(1)), pl.BlockSpec((TOK, HD), chunk(1))),
            scratch_shapes=[
                pltpu.VMEM((10 * TOK, HD), jnp.bfloat16),
                pltpu.VMEM((10 * TOK, HD), jnp.bfloat16),
            ],
        ),
        compiler_params=pltpu.CompilerParams(vmem_limit_bytes=32 * 1024 * 1024),
        cost_estimate=pl.CostEstimate(
            flops=heads * 4 * 128 * 1280 * 128 * 4,
            bytes_accessed=heads * 2200000,
            transcendentals=heads * 4 * 128 * 1280,
        ),
        name="attend",
    )(*scalars, q_own, q_far, k_own, v_own, far, out_own, out_far, mid, cc_fix, cc_part, text, cc_text)


def on_device(queries, latent_keys, latent_values, prompt_keyvals, block_lists, tile_segment):
    width = HALF * HD
    device = lax.axis_index("seq")
    core, x, row = device % CN, device // CN % XN, device // (CN * XN)
    z = row // YN

    def half_of(array, which):
        return lax.dynamic_slice_in_dim(array, which * width, width, array.ndim - 1)

    own_table = jnp.concatenate(
        [block_lists, jnp.broadcast_to(tile_segment[:, None], (2, 8))], axis=1
    )
    table = jnp.concatenate([own_table, send(own_table, ACROSS)], axis=0)
    lists, segments = table[:, :8], table[::2, 8]

    def held(which):
        side = 2 * which - 1
        return [
            2 * x + which,
            2 * (1 - x) + which,
            2 * x + which - 4 * side,
            2 * (1 - x) + which - 4 * side,
            2 - which + 4 * side,
        ]

    offsets = jnp.stack(held(core) + held(1 - core))
    wanted = lists // 2 - 4 * row
    position = jnp.argmax(wanted[:, :, None] == offsets[None, None, :], axis=2).astype(jnp.int32)
    valid = (lists >= 0).astype(jnp.int32)
    slots = jnp.where(lists >= 0, position * 2 + lists % 2, 0)
    text_at = (2 * segments[:, None] + jnp.arange(2)[None, :] - z) % ZN
    scalars = (x[None].astype(jnp.int32), slots, valid, text_at.astype(jnp.int32))

    halves = jnp.stack([prompt_keyvals[..., :width], prompt_keyvals[..., width:]])
    plane = lax.all_to_all(
        jnp.concatenate([halves] * YN, axis=0), "seq", 0, 0, axis_index_groups=PLANES
    )
    plane = jnp.swapaxes(plane, 0, 1).reshape(2, 64, width)
    ups, downs = [plane], [plane]
    for _ in range(4):
        ups.append(send(ups[-1], ZUP))
    for _ in range(3):
        downs.append(send(downs[-1], ZDOWN))
    text = jnp.stack([plane, downs[1], downs[2], downs[3], ups[4], ups[3], ups[2], ups[1]])
    cc_text = send(text, CORES)

    kv_own = jnp.stack([half_of(latent_keys, x), half_of(latent_values, x)])
    kv_give = jnp.stack([half_of(latent_keys, 1 - x), half_of(latent_values, 1 - x)])
    out_own = send(kv_own, OUTWARD)
    cc_fix = send(jnp.stack([kv_own, out_own]), CORES)
    q_far = send(half_of(queries, 1 - x), ACROSS)
    results = []
    first = 0
    for heads in CHUNKS:
        cols = slice(first * HD, (first + heads) * HD)
        far = send(kv_give[..., cols], ACROSS)
        out_far = send(far, OUTWARD)
        mid = send(jnp.where(x != core, kv_own[..., cols], far), INWARD)
        cc_part = send(jnp.stack([far, out_far, mid]), CORES)
        mine, theirs = attend(
            first, heads, scalars, queries, q_far, latent_keys, latent_values,
            far, out_own, out_far, mid, cc_fix, cc_part, text, cc_text,
        )
        results.append((mine, send(theirs, ACROSS)))
        first += heads
    mine = jnp.concatenate([m for m, _ in results], axis=1)
    back = jnp.concatenate([b for _, b in results], axis=1)
    left, right = jnp.where(x == 0, mine, back), jnp.where(x == 0, back, mine)
    return jnp.concatenate([left, right], axis=1)


def solution(mesh):
    in_specs = (
        P(("cfg", "seq"), None),
        P(("cfg", "seq"), None),
        P(("cfg", "seq"), None),
        P(None, ("cfg", "seq"), None),
        P("seq", None),
        P("seq"),
    )
    out_specs = P(("cfg", "seq"), None)
    return jax.shard_map(
        on_device, mesh=mesh, in_specs=in_specs, out_specs=out_specs, check_vma=False
    )
```

time: 439 us -> 163 us (0.37)
  starting transfers between devices: 169 us -> 47.2 us
  waiting for transfers between devices: 133 us -> 59.9 us
  matrix products: 67.7 us -> 0 us
  Pallas kernels: 0 us -> 25.4 us
  other arithmetic: 29.9 us -> 16 us
  between operations: 14.2 us -> 1.06 us
  local copies, waits for them, and re-layouts: 23 us -> 12.8 us
    all_gather x1 -> x0, waiting for transfers between devices: 127 us -> none  [on_device(): whole_text = lax.all_gather(prompt_keyvals, 'seq', axis=1, tiled=True)]
    ppermute x6 -> x27, starting transfers between devices: 169 us -> 42.4 us  [send(): return lax.ppermute(block, 'seq', to)]
    dot_general x40 -> x0, matrix products: 67.7 us -> none  [the longest x20 34.4 us: attend_head(): jnp.dot(weights.astype(jnp.bfloat16), head_values, preferred_element_type...]
    ppermute x6 -> x27, waiting for transfers between devices: 4.94 us -> 54.4 us  [send(): return lax.ppermute(block, 'seq', to)]
    pallas_call x0 -> x3, Pallas kernels: none -> 25.4 us  [attend(): pl.pallas_call(attend_kernel, out_shape=(out, out), grid_spec=pltpu.Prefe...]
    concatenate x1 -> x2, other arithmetic: 14.7 us -> 1.15 us  [the longest x1 1.15 us: on_device(): return jnp.concatenate([left, right], axis=1)]
    reduce_sum x20 -> x0, other arithmetic: 12.9 us -> none  [attend_head(): total = jnp.sum(weights, axis=1, keepdims=True)]
    another operation x1 -> x7, other arithmetic: 1.96 us -> 10.8 us  [the longest x3 5.49 us: on_device(): cc_part = send(jnp.stack([far, out_far, mid]), CORES)]
  transfers between devices with their start and end apart: 7 -> 28, of which waited for: 3 -> 10; matrix products, arithmetic and copies ran while one was open for 5% -> 14% of each run, Pallas kernels for 0% -> 16%
where the time goes in v1:
time: 163 us; the launch traced here: 162 us
  waiting for transfers between devices  59.9 us (37%)
  starting transfers between devices  47.2 us (29%)
  Pallas kernels  25.4 us (16%)
  other arithmetic  16 us (10%)
  local copies, waits for them, and re-layouts  12.8 us (8%)
    ppermute x27, waiting for transfers between devices, send(): return lax.ppermute(block, 'seq', to)  54.4 us
    ppermute x27, starting transfers between devices, send(): return lax.ppermute(block, 'seq', to)  42.4 us
    pallas_call x3, Pallas kernels, attend(): pl.pallas_call(attend_kernel, out_shape=(out, out), grid_spec=pltpu.Prefe...  25.4 us
    unnamed x56, local copies, waits for them, and re-layouts  6.89 us
    all_to_all x1, waiting for transfers between devices, on_device(): lax.all_to_all(jnp.concatenate([halves] * YN, axis=0), 'seq', 0, 0, axis_...  5.56 us
    another operation x3, other arithmetic, on_device(): cc_part = send(jnp.stack([far, out_far, mid]), CORES)  5.49 us
    all_to_all x1, starting transfers between devices, on_device(): lax.all_to_all(jnp.concatenate([halves] * YN, axis=0), 'seq', 0, 0, axis_...  4.74 us
    another operation x2, other arithmetic, on_device(): cc_fix = send(jnp.stack([kv_own, out_own]), CORES)  3.52 us
  transfers between devices with their start and end apart: 28, of which 10 were waited for; matrix products, arithmetic and copies ran while one was open for 14% of the time, Pallas kernels for 16%

profile of v1, /device:TPU:4, one launch (start us, length us, event | category | flops | bytes accessed | tf_op | source)
XLA Modules:
  0.0 162.4 jit_solution(10208799760719190294)
XLA Ops:
  0.0 1.8 %dynamic-slice_bitcast_fusion = (bf16[1,256,1280]{2,1,0:T(8,128)(2,1)S(1)}, bf16[1,256,1280]{2,1,0:T(8,128)(2,1)S(1)}, bf16[1,256,1280]{2,1,0:T(8,128)(2,1)S(1)}, bf16[1,256,1280]{2,1,0:T(8,128)(2,1)S(1)}) fusion(bf16[256,2560]{1,0:T(8,128)(2,1)} %v_own.5, s32[]{:T(128)S(6)} %select_n.98, s32[]{:T(128)S(6)} %select_n.97, bf16[256,2560]{1,0:T(8,128)(2,1)} %k_own.5), kind=kLoop, calls=%fused_computation.12 | loop fusion | bytes 5242888 | tf_op jit(solution)/shard_map/stack | solution.py:193
  8.9 4.7 %all-to-all-start = ((bf16[8,2,8,1280]{3,2,1,0:T(8,128)(2,1)}), bf16[8,2,8,1280]{3,2,1,0:T(8,128)(2,1)}, u32[]{:S(2)}, u32[]{:S(2)}) async-start(bf16[8,2,8,1280]{3,2,1,0:T(8,128)(2,1)} %constant_dynamic-update-slice_fusion), calls=%async_computation | async-start | bytes 655360 | tf_op jit(solution)/shard_map/all_to_all | solution.py:181
  14.6 2.0 %collective-permute-start.2 = (bf16[2,256,384]{2,1,0:T(8,128)(2,1)}, bf16[2,256,384]{2,1,0:T(8,128)(2,1)S(1)}, u32[]{:S(2)}, u32[]{:S(2)}) collective-permute-start(bf16[2,256,384]{2,1,0:T(8,128)(2,1)} %get-tuple-element.28), channel_id=1, source_target_pairs={{0,4},{2,6},{4,0},{6,2},{8,12},{10,14},{12,8},{14,10},{16,20},{18,... | collective-permute-start | bytes 1179656 | tf_op jit(solution)/shard_map/ppermute | solution.py:47
  16.6 1.7 %fusion.11 = (bf16[1,2,256,1280]{3,2,1,0:T(8,128)(2,1)}, bf16[2,256,1280]{2,1,0:T(8,128)(2,1)}) fusion(bf16[1,256,1280]{2,1,0:T(8,128)(2,1)S(1)} %get-tuple-element.33, bf16[1,256,1280]{2,1,0:T(8,128)(2,1)S(1)} %get-tuple-element.36), kind=kLoop, calls=%fused_computation.71 | loop fusion | flops 655360 | bytes 3932160 | tf_op jit(solution)/shard_map/stack | solution.py:196
  18.3 5.6 %all-to-all-done = bf16[8,2,8,1280]{3,2,1,0:T(8,128)(2,1)} async-done(((bf16[8,2,8,1280]{3,2,1,0:T(8,128)(2,1)}), bf16[8,2,8,1280]{3,2,1,0:T(8,128)(2,1)}, u32[]{:S(2)}, u32[]{:S(2)}) %all-to-all-start) | async-done | bytes 327712 | tf_op jit(solution)/shard_map/all_to_all | solution.py:181
  24.9 5.9 %collective-permute-start.8 = (bf16[2,64,1280]{2,1,0:T(8,128)(2,1)S(1)}, bf16[2,64,1280]{2,1,0:T(8,128)(2,1)S(1)}, u32[]{:S(2)}, u32[]{:S(2)}) collective-permute-start(bf16[2,64,1280]{2,1,0:T(8,128)(2,1)S(1)} %copy_bitcast_fusion), channel_id=1, source_target_pairs={{0,224},{2,226},{4,228},{6,230},{8,232},{10,234},{12,236},{14,238}... | collective-permute-start | bytes 983048 | tf_op jit(solution)/shard_map/ppermute | solution.py:47
  31.9 6.1 %collective-permute-start.3 = (bf16[2,256,1280]{2,1,0:T(8,128)(2,1)}, bf16[2,256,1280]{2,1,0:T(8,128)(2,1)S(1)}, u32[]{:S(2)}, u32[]{:S(2)}) collective-permute-start(bf16[2,256,1280]{2,1,0:T(8,128)(2,1)} %get-tuple-element.30), channel_id=1, source_target_pairs={{0,248},{2,10},{4,252},{6,14},{8,0},{10,18},{12,4},{14,22},{16,8},... | collective-permute-start | bytes 3932168 | tf_op jit(solution)/shard_map/ppermute | solution.py:47
  39.5 5.9 %collective-permute-start.9 = (bf16[2,64,1280]{2,1,0:T(8,128)(2,1)S(1)}, bf16[2,64,1280]{2,1,0:T(8,128)(2,1)S(1)}, u32[]{:S(2)}, u32[]{:S(2)}) collective-permute-start(bf16[2,64,1280]{2,1,0:T(8,128)(2,1)S(1)} %collective-permute-done.8), channel_id=1, source_target_pairs={{0,224},{2,226},{4,228},{6,230},{8,232},{10,234},{12,236},{14,238}... | collective-permute-start | bytes 983048 | tf_op jit(solution)/shard_map/ppermute | solution.py:47
  45.4 19.3 %collective-permute-done.9 = bf16[2,64,1280]{2,1,0:T(8,128)(2,1)S(1)} collective-permute-done((bf16[2,64,1280]{2,1,0:T(8,128)(2,1)S(1)}, bf16[2,64,1280]{2,1,0:T(8,128)(2,1)S(1)}, u32[]{:S(2)}, u32[]{:S(2)}) %collective-permute-start.9) | collective-permute-done | bytes 327712 | tf_op jit(solution)/shard_map/ppermute | solution.py:47
  64.7 3.7 %collective-permute-start.10 = (bf16[2,64,1280]{2,1,0:T(8,128)(2,1)S(1)}, bf16[2,64,1280]{2,1,0:T(8,128)(2,1)S(1)}, u32[]{:S(2)}, u32[]{:S(2)}) collective-permute-start(bf16[2,64,1280]{2,1,0:T(8,128)(2,1)S(1)} %collective-permute-done.9), channel_id=1, source_target_pairs={{0,224},{2,226},{4,228},{6,230},{8,232},{10,234},{12,236},{14,238}... | collective-permute-start | bytes 983048 | tf_op jit(solution)/shard_map/ppermute | solution.py:47
  68.4 9.8 %collective-permute-done.13 = bf16[2,64,1280]{2,1,0:T(8,128)(2,1)S(1)} collective-permute-done((bf16[2,64,1280]{2,1,0:T(8,128)(2,1)S(1)}, bf16[2,64,1280]{2,1,0:T(8,128)(2,1)S(1)}, u32[]{:S(2)}, u32[]{:S(2)}) %collective-permute-start.13) | collective-permute-done | bytes 327712 | tf_op jit(solution)/shard_map/ppermute | solution.py:47
  78.3 1.9 %pad_maximum_fusion = bf16[2,2,256,1280]{3,2,1,0:T(8,128)(2,1)} fusion(bf16[1,2,256,1280]{3,2,1,0:T(8,128)(2,1)S(1)} %bitcast.66, bf16[1,2,256,1280]{3,2,1,0:T(8,128)(2,1)S(1)} %copy-done.16), kind=kLoop, calls=%fused_computation | loop fusion | flops 1310720 | bytes 5242880 | tf_op jit(solution)/shard_map/stack | solution.py:196
  80.2 6.3 %collective-permute-done.14 = bf16[2,64,1280]{2,1,0:T(8,128)(2,1)S(1)} collective-permute-done((bf16[2,64,1280]{2,1,0:T(8,128)(2,1)S(1)}, bf16[2,64,1280]{2,1,0:T(8,128)(2,1)S(1)}, u32[]{:S(2)}, u32[]{:S(2)}) %collective-permute-start.14) | collective-permute-done | bytes 327712 | tf_op jit(solution)/shard_map/ppermute | solution.py:47
  87.4 1.3 collective-permute-start
  88.7 2.0 %fusion.1 = bf16[2,256,512]{2,1,0:T(8,128)(2,1)} fusion(bf16[2,256,512]{2,1,0:T(8,128)(2,1)} %collective-permute-done.16.far, bf16[1,256,1280]{2,1,0:T(8,128)(2,1)S(1)} %copy-done.15, bf16[1,256,1280]{2,1,0:T(8,128)(2,1)S(1)} %copy-done.13, pred[]{:T(512)S(6)} %ne.69), kind=kLoop, calls=%fused_computation.19 | loop fusion | flops 524288 | bytes 2359297 | tf_op jit(solution)/shard_map/jit(_where)/select_n | solution.py:204
  91.1 1.6 collective-permute-start.18
  92.7 3.7 %collective-permute-start.17 = (bf16[2,256,512]{2,1,0:T(8,128)(2,1)}, bf16[2,256,512]{2,1,0:T(8,128)(2,1)}, u32[]{:S(2)}, u32[]{:S(2)}) collective-permute-start(bf16[2,256,512]{2,1,0:T(8,128)(2,1)} %collective-permute-done.16.far), channel_id=1, source_target_pairs={{0,248},{2,10},{4,252},{6,14},{8,0},{10,18},{12,4},{14,22},{16,8},... | collective-permute-start | bytes 1572872 | tf_op jit(solution)/shard_map/ppermute | solution.py:47
  96.5 3.2 %collective-permute-done.4.out_far = bf16[2,256,384]{2,1,0:T(8,128)(2,1)S(1)} collective-permute-done((bf16[2,256,384]{2,1,0:T(8,128)(2,1)S(1)}, bf16[2,256,384]{2,1,0:T(8,128)(2,1)S(1)}, u32[]{:S(2)}, u32[]{:S(2)}) %collective-permute-start.4) | collective-permute-done | bytes 393248 | tf_op jit(solution)/shard_map/ppermute | solution.py:47
  99.8 2.1 %constant_dynamic-slice_fusion = bf16[256,1280]{1,0:T(8,128)(2,1)} fusion(bf16[256,2560]{1,0:T(8,128)(2,1)} %q_own.5, s32[]{:T(128)S(6)} %select_n.97), kind=kLoop, calls=%fused_computation.67 | loop fusion | bytes 1310724 | tf_op jit(solution)/shard_map/dynamic_slice | solution.py:154
  101.9 6.8 %collective-permute-done.18.mid = bf16[2,256,512]{2,1,0:T(8,128)(2,1)} collective-permute-done((bf16[2,256,512]{2,1,0:T(8,128)(2,1)}, bf16[2,256,512]{2,1,0:T(8,128)(2,1)}, u32[]{:S(2)}, u32[]{:S(2)}) %collective-permute-start.18) | collective-permute-done | bytes 524320 | tf_op jit(solution)/shard_map/ppermute | solution.py:47
  108.6 2.5 %collective-permute-done.17.out_far = bf16[2,256,512]{2,1,0:T(8,128)(2,1)} collective-permute-done((bf16[2,256,512]{2,1,0:T(8,128)(2,1)}, bf16[2,256,512]{2,1,0:T(8,128)(2,1)}, u32[]{:S(2)}, u32[]{:S(2)}) %collective-permute-start.17) | collective-permute-done | bytes 524320 | tf_op jit(solution)/shard_map/ppermute | solution.py:47
  111.1 3.8 %collective-permute-start.21 = (bf16[2,256,384]{2,1,0:T(8,128)(2,1)}, bf16[2,256,384]{2,1,0:T(8,128)(2,1)}, u32[]{:S(2)}, u32[]{:S(2)}) collective-permute-start(bf16[2,256,384]{2,1,0:T(8,128)(2,1)} %copy-done.6), channel_id=1, source_target_pairs={{0,248},{2,10},{4,252},{6,14},{8,0},{10,18},{12,4},{14,22},{16,8},... | collective-permute-start | bytes 1179656 | tf_op jit(solution)/shard_map/ppermute | solution.py:47
  114.9 2.7 %pad_maximum_fusion.2 = bf16[3,2,256,512]{3,2,1,0:T(8,128)(2,1)} fusion(bf16[1,2,256,512]{3,2,1,0:T(8,128)(2,1)} %bitcast.35, bf16[1,2,256,512]{3,2,1,0:T(8,128)(2,1)} %bitcast.34, bf16[1,2,256,512]{3,2,1,0:T(8,128)(2,1)} %bitcast.33), kind=kLoop, calls=%fused_computation.8 | loop fusion | flops 1572864 | bytes 3145728 | tf_op jit(solution)/shard_map/stack | solution.py:205
  117.8 1.5 pad_maximum_fusion.4
  120.5 2.0 %collective-permute-start.7 = (bf16[3,2,256,384]{3,2,1,0:T(8,128)(2,1)S(1)}, bf16[3,2,256,384]{3,2,1,0:T(8,128)(2,1)S(1)}, u32[]{:S(2)}, u32[]{:S(2)}) collective-permute-start(bf16[3,2,256,384]{3,2,1,0:T(8,128)(2,1)S(1)} %pad_maximum_fusion.4), channel_id=1, source_target_pairs={{0,2},{2,0},{4,6},{6,4},{8,10},{10,8},{12,14},{14,12},{16,18},{18,... | collective-permute-start | bytes 3538952 | tf_op jit(solution)/shard_map/ppermute | solution.py:47
  124.9 1.3 copy-done.4
  126.2 9.8 %attend.4 = (bf16[256,512]{1,0:T(8,128)(2,1)S(1)}, bf16[256,512]{1,0:T(8,128)(2,1)S(1)}) custom-call(s32[1]{0:T(128)} %bitcast.half_ref, s32[4,8]{1,0:T(4,128)S(1)} %fusion.8.slots_ref, s32[4,8]{1,0:T(4,128)S(1)} %get-tuple-element.19.valid_ref, s32[2,2]{1,0:T(2,128)S(1)} %and_select_fusion.text_at_ref, bf16[256,2560]{1,0:T(8,128)(2,1)S(1)} %copy-done.4, ...), custom_call_target="tpu_custom_call" | custom-call | flops 1342177280 | bytes 8800000 | tf_op jit(solution)/shard_map/attend/pallas_call | solution.py:124
  136.1 1.9 %collective-permute-start.25 = (bf16[256,512]{1,0:T(8,128)(2,1)S(1)}, bf16[256,512]{1,0:T(8,128)(2,1)S(1)}, u32[]{:S(2)}, u32[]{:S(2)}) collective-permute-start(bf16[256,512]{1,0:T(8,128)(2,1)S(1)} %get-tuple-element.17), channel_id=1, source_target_pairs={{0,4},{2,6},{4,0},{6,2},{8,12},{10,14},{12,8},{14,10},{16,20},{18,... | collective-permute-start | bytes 786440 | tf_op jit(solution)/shard_map/ppermute | solution.py:47
  138.1 7.8 %attend.3 = (bf16[256,384]{1,0:T(8,128)(2,1)S(1)}, bf16[256,384]{1,0:T(8,128)(2,1)S(1)}) custom-call(s32[1]{0:T(128)} %bitcast.half_ref, s32[4,8]{1,0:T(4,128)S(1)} %fusion.8.slots_ref, s32[4,8]{1,0:T(4,128)S(1)} %get-tuple-element.19.valid_ref, s32[2,2]{1,0:T(2,128)S(1)} %and_select_fusion.text_at_ref, bf16[256,2560]{1,0:T(8,128)(2,1)S(1)} %copy-done.5, ...), custom_call_target="tpu_custom_call" | custom-call | flops 1006632960 | bytes 6600000 | tf_op jit(solution)/shard_map/attend/pallas_call | solution.py:124
  146.3 7.8 %attend.5 = (bf16[256,384]{1,0:T(8,128)(2,1)S(1)}, bf16[256,384]{1,0:T(8,128)(2,1)S(1)}) custom-call(s32[1]{0:T(128)} %bitcast.half_ref, s32[4,8]{1,0:T(4,128)S(1)} %fusion.8.slots_ref, s32[4,8]{1,0:T(4,128)S(1)} %get-tuple-element.19.valid_ref, s32[2,2]{1,0:T(2,128)S(1)} %and_select_fusion.text_at_ref, bf16[256,2560]{1,0:T(8,128)(2,1)S(1)} %copy-done.5, ...), custom_call_target="tpu_custom_call" | custom-call | flops 1006632960 | bytes 6600000 | tf_op jit(solution)/shard_map/attend/pallas_call | solution.py:124
  154.1 1.9 %collective-permute-start.26 = (bf16[256,384]{1,0:T(8,128)(2,1)S(1)}, bf16[256,384]{1,0:T(8,128)(2,1)S(1)}, u32[]{:S(2)}, u32[]{:S(2)}) collective-permute-start(bf16[256,384]{1,0:T(8,128)(2,1)S(1)} %get-tuple-element.18), channel_id=1, source_target_pairs={{0,4},{2,6},{4,0},{6,2},{8,12},{10,14},{12,8},{14,10},{16,20},{18,... | collective-permute-start | bytes 589832 | tf_op jit(solution)/shard_map/ppermute | solution.py:47
  156.2 4.9 %collective-permute-done.26 = bf16[256,384]{1,0:T(8,128)(2,1)S(1)} collective-permute-done((bf16[256,384]{1,0:T(8,128)(2,1)S(1)}, bf16[256,384]{1,0:T(8,128)(2,1)S(1)}, u32[]{:S(2)}, u32[]{:S(2)}) %collective-permute-start.26) | collective-permute-done | bytes 196640 | tf_op jit(solution)/shard_map/ppermute | solution.py:47
  (111 shorter events, 17.9 us)
Async XLA Ops:
  1.9 14.8 %copy-start.12 = (bf16[1,256,1280]{2,1,0:T(8,128)(2,1)}, bf16[1,256,1280]{2,1,0:T(8,128)(2,1)S(1)}, u32[]{:S(2)}) copy-start(bf16[1,256,1280]{2,1,0:T(8,128)(2,1)S(1)} %get-tuple-element.33) | copy-start | bytes 1966084
  1.9 14.8 %copy-start.14 = (bf16[1,256,1280]{2,1,0:T(8,128)(2,1)}, bf16[1,256,1280]{2,1,0:T(8,128)(2,1)S(1)}, u32[]{:S(2)}) copy-start(bf16[1,256,1280]{2,1,0:T(8,128)(2,1)S(1)} %get-tuple-element.36) | copy-start | bytes 1966084
  2.7 86.0 %collective-permute-start.16 = (bf16[2,256,512]{2,1,0:T(8,128)(2,1)}, bf16[2,256,512]{2,1,0:T(8,128)(2,1)}, u32[]{:S(2)}, u32[]{:S(2)}) collective-permute-start(bf16[2,256,512]{2,1,0:T(8,128)(2,1)} %pad_maximum_fusion.6), channel_id=1, source_target_pairs={{0,4},{2,6},{4,0},{6,2},{8,12},{10,14},{12,8},{14,10},{16,20},{18,... | collective-permute-start | bytes 1572872 | tf_op jit(solution)/shard_map/ppermute | solution.py:47
  8.9 15.0 %all-to-all-start = ((bf16[8,2,8,1280]{3,2,1,0:T(8,128)(2,1)}), bf16[8,2,8,1280]{3,2,1,0:T(8,128)(2,1)}, u32[]{:S(2)}, u32[]{:S(2)}) async-start(bf16[8,2,8,1280]{3,2,1,0:T(8,128)(2,1)} %constant_dynamic-update-slice_fusion), calls=%async_computation | async-start | bytes 655360 | tf_op jit(solution)/shard_map/all_to_all | solution.py:181
  14.6 17.3 %collective-permute-start.2 = (bf16[2,256,384]{2,1,0:T(8,128)(2,1)}, bf16[2,256,384]{2,1,0:T(8,128)(2,1)S(1)}, u32[]{:S(2)}, u32[]{:S(2)}) collective-permute-start(bf16[2,256,384]{2,1,0:T(8,128)(2,1)} %get-tuple-element.28), channel_id=1, source_target_pairs={{0,4},{2,6},{4,0},{6,2},{8,12},{10,14},{12,8},{14,10},{16,20},{18,... | collective-permute-start | bytes 1179656 | tf_op jit(solution)/shard_map/ppermute | solution.py:47
  16.6 21.4 %collective-permute-start.20 = (bf16[2,256,384]{2,1,0:T(8,128)(2,1)}, bf16[2,256,384]{2,1,0:T(8,128)(2,1)S(1)}, u32[]{:S(2)}, u32[]{:S(2)}) collective-permute-start(bf16[2,256,384]{2,1,0:T(8,128)(2,1)} %get-tuple-element.27), channel_id=1, source_target_pairs={{0,4},{2,6},{4,0},{6,2},{8,12},{10,14},{12,8},{14,10},{16,20},{18,... | collective-permute-start | bytes 1179656 | tf_op jit(solution)/shard_map/ppermute | solution.py:47
  24.9 14.6 %collective-permute-start.8 = (bf16[2,64,1280]{2,1,0:T(8,128)(2,1)S(1)}, bf16[2,64,1280]{2,1,0:T(8,128)(2,1)S(1)}, u32[]{:S(2)}, u32[]{:S(2)}) collective-permute-start(bf16[2,64,1280]{2,1,0:T(8,128)(2,1)S(1)} %copy_bitcast_fusion), channel_id=1, source_target_pairs={{0,224},{2,226},{4,228},{6,230},{8,232},{10,234},{12,236},{14,238}... | collective-permute-start | bytes 983048 | tf_op jit(solution)/shard_map/ppermute | solution.py:47
  30.9 14.5 %collective-permute-start.11 = (bf16[2,64,1280]{2,1,0:T(8,128)(2,1)S(1)}, bf16[2,64,1280]{2,1,0:T(8,128)(2,1)S(1)}, u32[]{:S(2)}, u32[]{:S(2)}) collective-permute-start(bf16[2,64,1280]{2,1,0:T(8,128)(2,1)S(1)} %copy_bitcast_fusion), channel_id=1, source_target_pairs={{0,32},{2,34},{4,36},{6,38},{8,40},{10,42},{12,44},{14,46},{16,48}... | collective-permute-start | bytes 983048 | tf_op jit(solution)/shard_map/ppermute | solution.py:47
  31.9 56.8 %copy-start.8 = (bf16[2,256,384]{2,1,0:T(8,128)(2,1)}, bf16[2,256,384]{2,1,0:T(8,128)(2,1)S(1)}, u32[]{:S(2)}) copy-start(bf16[2,256,384]{2,1,0:T(8,128)(2,1)S(1)} %collective-permute-done.2.far) | copy-start | bytes 1179652
  31.9 46.4 %collective-permute-start.3 = (bf16[2,256,1280]{2,1,0:T(8,128)(2,1)}, bf16[2,256,1280]{2,1,0:T(8,128)(2,1)S(1)}, u32[]{:S(2)}, u32[]{:S(2)}) collective-permute-start(bf16[2,256,1280]{2,1,0:T(8,128)(2,1)} %get-tuple-element.30), channel_id=1, source_target_pairs={{0,248},{2,10},{4,252},{6,14},{8,0},{10,18},{12,4},{14,22},{16,8},... | collective-permute-start | bytes 3932168 | tf_op jit(solution)/shard_map/ppermute | solution.py:47
  39.0 39.3 %copy-start.16 = (bf16[1,2,256,1280]{3,2,1,0:T(8,128)(2,1)S(1)}, bf16[1,2,256,1280]{3,2,1,0:T(8,128)(2,1)}, u32[]{:S(2)}) copy-start(bf16[1,2,256,1280]{3,2,1,0:T(8,128)(2,1)} %get-tuple-element.29) | copy-start | bytes 3932164
  39.0 53.7 %collective-permute-start.5 = (bf16[2,256,384]{2,1,0:T(8,128)(2,1)S(1)}, bf16[2,256,384]{2,1,0:T(8,128)(2,1)}, u32[]{:S(2)}, u32[]{:S(2)}) collective-permute-start(bf16[2,256,384]{2,1,0:T(8,128)(2,1)S(1)} %get-tuple-element.26), channel_id=1, source_target_pairs={{0,8},{2,250},{4,12},{6,254},{8,16},{10,2},{12,20},{14,6},{16,24},... | collective-permute-start | bytes 1179656 | tf_op jit(solution)/shard_map/ppermute | solution.py:47
  39.5 25.2 %collective-permute-start.9 = (bf16[2,64,1280]{2,1,0:T(8,128)(2,1)S(1)}, bf16[2,64,1280]{2,1,0:T(8,128)(2,1)S(1)}, u32[]{:S(2)}, u32[]{:S(2)}) collective-permute-start(bf16[2,64,1280]{2,1,0:T(8,128)(2,1)S(1)} %collective-permute-done.8), channel_id=1, source_target_pairs={{0,224},{2,226},{4,228},{6,230},{8,232},{10,234},{12,236},{14,238}... | collective-permute-start | bytes 983048 | tf_op jit(solution)/shard_map/ppermute | solution.py:47
  45.4 23.0 %collective-permute-start.12 = (bf16[2,64,1280]{2,1,0:T(8,128)(2,1)S(1)}, bf16[2,64,1280]{2,1,0:T(8,128)(2,1)S(1)}, u32[]{:S(2)}, u32[]{:S(2)}) collective-permute-start(bf16[2,64,1280]{2,1,0:T(8,128)(2,1)S(1)} %collective-permute-done.11), channel_id=1, source_target_pairs={{0,32},{2,34},{4,36},{6,38},{8,40},{10,42},{12,44},{14,46},{16,48}... | collective-permute-start | bytes 983048 | tf_op jit(solution)/shard_map/ppermute | solution.py:47
  64.7 13.6 %collective-permute-start.10 = (bf16[2,64,1280]{2,1,0:T(8,128)(2,1)S(1)}, bf16[2,64,1280]{2,1,0:T(8,128)(2,1)S(1)}, u32[]{:S(2)}, u32[]{:S(2)}) collective-permute-start(bf16[2,64,1280]{2,1,0:T(8,128)(2,1)S(1)} %collective-permute-done.9), channel_id=1, source_target_pairs={{0,224},{2,226},{4,228},{6,230},{8,232},{10,234},{12,236},{14,238}... | collective-permute-start | bytes 983048 | tf_op jit(solution)/shard_map/ppermute | solution.py:47
  68.4 9.9 %collective-permute-start.13 = (bf16[2,64,1280]{2,1,0:T(8,128)(2,1)S(1)}, bf16[2,64,1280]{2,1,0:T(8,128)(2,1)S(1)}, u32[]{:S(2)}, u32[]{:S(2)}) collective-permute-start(bf16[2,64,1280]{2,1,0:T(8,128)(2,1)S(1)} %collective-permute-done.12), channel_id=1, source_target_pairs={{0,32},{2,34},{4,36},{6,38},{8,40},{10,42},{12,44},{14,46},{16,48}... | collective-permute-start | bytes 983048 | tf_op jit(solution)/shard_map/ppermute | solution.py:47
  78.2 8.3 %collective-permute-start.14 = (bf16[2,64,1280]{2,1,0:T(8,128)(2,1)S(1)}, bf16[2,64,1280]{2,1,0:T(8,128)(2,1)S(1)}, u32[]{:S(2)}, u32[]{:S(2)}) collective-permute-start(bf16[2,64,1280]{2,1,0:T(8,128)(2,1)S(1)} %collective-permute-done.13), channel_id=1, source_target_pairs={{0,32},{2,34},{4,36},{6,38},{8,40},{10,42},{12,44},{14,46},{16,48}... | collective-permute-start | bytes 983048 | tf_op jit(solution)/shard_map/ppermute | solution.py:47
  80.2 44.7 %collective-permute-start.6 = (bf16[2,2,256,1280]{3,2,1,0:T(8,128)(2,1)}, bf16[2,2,256,1280]{3,2,1,0:T(8,128)(2,1)}, u32[]{:S(2)}, u32[]{:S(2)}) collective-permute-start(bf16[2,2,256,1280]{3,2,1,0:T(8,128)(2,1)} %pad_maximum_fusion), channel_id=1, source_target_pairs={{0,2},{2,0},{4,6},{6,4},{8,10},{10,8},{12,14},{14,12},{16,18},{18,... | collective-permute-start | bytes 7864328 | tf_op jit(solution)/shard_map/ppermute | solution.py:47
  86.6 38.2 %collective-permute-start.15 = (bf16[8,2,64,1280]{3,2,1,0:T(8,128)(2,1)S(1)}, bf16[8,2,64,1280]{3,2,1,0:T(8,128)(2,1)}, u32[]{:S(2)}, u32[]{:S(2)}) collective-permute-start(bf16[8,2,64,1280]{3,2,1,0:T(8,128)(2,1)S(1)} %bitcast_dynamic-update-slice_fusion.text), channel_id=1, source_target_pairs={{0,2},{2,0},{4,6},{6,4},{8,10},{10,8},{12,14},{14,12},{16,18},{18,... | collective-permute-start | bytes 7864328 | tf_op jit(solution)/shard_map/ppermute | solution.py:47
  87.4 3.7 %collective-permute-start = (s32[2,16]{1,0:T(2,128)S(1)}, s32[2,16]{1,0:T(2,128)S(1)}, u32[]{:S(2)}, u32[]{:S(2)}) collective-permute-start(s32[2,16]{1,0:T(2,128)S(1)} %concatenate.19), channel_id=1, source_target_pairs={{0,4},{2,6},{4,0},{6,2},{8,12},{10,14},{12,8},{14,10},{16,20},{18,... | collective-permute-start | bytes 392 | tf_op jit(solution)/shard_map/ppermute | solution.py:47
  88.7 11.0 %collective-permute-start.4 = (bf16[2,256,384]{2,1,0:T(8,128)(2,1)S(1)}, bf16[2,256,384]{2,1,0:T(8,128)(2,1)S(1)}, u32[]{:S(2)}, u32[]{:S(2)}) collective-permute-start(bf16[2,256,384]{2,1,0:T(8,128)(2,1)S(1)} %collective-permute-done.2.far), channel_id=1, source_target_pairs={{0,248},{2,10},{4,252},{6,14},{8,0},{10,18},{12,4},{14,22},{16,8},... | collective-permute-start | bytes 1179656 | tf_op jit(solution)/shard_map/ppermute | solution.py:47
  91.1 17.6 %collective-permute-start.18 = (bf16[2,256,512]{2,1,0:T(8,128)(2,1)}, bf16[2,256,512]{2,1,0:T(8,128)(2,1)}, u32[]{:S(2)}, u32[]{:S(2)}) collective-permute-start(bf16[2,256,512]{2,1,0:T(8,128)(2,1)} %fusion.1), channel_id=1, source_target_pairs={{0,8},{2,250},{4,12},{6,254},{8,16},{10,2},{12,20},{14,6},{16,24},... | collective-permute-start | bytes 1572872 | tf_op jit(solution)/shard_map/ppermute | solution.py:47
  92.7 18.4 %collective-permute-start.17 = (bf16[2,256,512]{2,1,0:T(8,128)(2,1)}, bf16[2,256,512]{2,1,0:T(8,128)(2,1)}, u32[]{:S(2)}, u32[]{:S(2)}) collective-permute-start(bf16[2,256,512]{2,1,0:T(8,128)(2,1)} %collective-permute-done.16.far), channel_id=1, source_target_pairs={{0,248},{2,10},{4,252},{6,14},{8,0},{10,18},{12,4},{14,22},{16,8},... | collective-permute-start | bytes 1572872 | tf_op jit(solution)/shard_map/ppermute | solution.py:47
  99.8 17.8 %collective-permute-start.22 = (bf16[2,256,384]{2,1,0:T(8,128)(2,1)}, bf16[2,256,384]{2,1,0:T(8,128)(2,1)}, u32[]{:S(2)}, u32[]{:S(2)}) collective-permute-start(bf16[2,256,384]{2,1,0:T(8,128)(2,1)} %get-tuple-element.25), channel_id=1, source_target_pairs={{0,8},{2,250},{4,12},{6,254},{8,16},{10,2},{12,20},{14,6},{16,24},... | collective-permute-start | bytes 1179656 | tf_op jit(solution)/shard_map/ppermute | solution.py:47
  108.6 15.2 %collective-permute-start.1 = (bf16[256,1280]{1,0:T(8,128)(2,1)}, bf16[256,1280]{1,0:T(8,128)(2,1)S(1)}, u32[]{:S(2)}, u32[]{:S(2)}) collective-permute-start(bf16[256,1280]{1,0:T(8,128)(2,1)} %constant_dynamic-slice_fusion), channel_id=1, source_target_pairs={{0,4},{2,6},{4,0},{6,2},{8,12},{10,14},{12,8},{14,10},{16,20},{18,... | collective-permute-start | bytes 1966088 | tf_op jit(solution)/shard_map/ppermute | solution.py:47
  111.1 9.4 %collective-permute-start.21 = (bf16[2,256,384]{2,1,0:T(8,128)(2,1)}, bf16[2,256,384]{2,1,0:T(8,128)(2,1)}, u32[]{:S(2)}, u32[]{:S(2)}) collective-permute-start(bf16[2,256,384]{2,1,0:T(8,128)(2,1)} %copy-done.6), channel_id=1, source_target_pairs={{0,248},{2,10},{4,252},{6,14},{8,0},{10,18},{12,4},{14,22},{16,8},... | collective-permute-start | bytes 1179656 | tf_op jit(solution)/shard_map/ppermute | solution.py:47
  117.6 7.3 %collective-permute-start.19 = (bf16[3,2,256,512]{3,2,1,0:T(8,128)(2,1)}, bf16[3,2,256,512]{3,2,1,0:T(8,128)(2,1)}, u32[]{:S(2)}, u32[]{:S(2)}) collective-permute-start(bf16[3,2,256,512]{3,2,1,0:T(8,128)(2,1)} %pad_maximum_fusion.2), channel_id=1, source_target_pairs={{0,2},{2,0},{4,6},{6,4},{8,10},{10,8},{12,14},{14,12},{16,18},{18,... | collective-permute-start | bytes 4718600 | tf_op jit(solution)/shard_map/ppermute | solution.py:47
  120.5 17.5 %collective-permute-start.7 = (bf16[3,2,256,384]{3,2,1,0:T(8,128)(2,1)S(1)}, bf16[3,2,256,384]{3,2,1,0:T(8,128)(2,1)S(1)}, u32[]{:S(2)}, u32[]{:S(2)}) collective-permute-start(bf16[3,2,256,384]{3,2,1,0:T(8,128)(2,1)S(1)} %pad_maximum_fusion.4), channel_id=1, source_target_pairs={{0,2},{2,0},{4,6},{6,4},{8,10},{10,8},{12,14},{14,12},{16,18},{18,... | collective-permute-start | bytes 3538952 | tf_op jit(solution)/shard_map/ppermute | solution.py:47
  123.8 22.5 %collective-permute-start.23 = (bf16[3,2,256,384]{3,2,1,0:T(8,128)(2,1)S(1)}, bf16[3,2,256,384]{3,2,1,0:T(8,128)(2,1)S(1)}, u32[]{:S(2)}, u32[]{:S(2)}) collective-permute-start(bf16[3,2,256,384]{3,2,1,0:T(8,128)(2,1)S(1)} %pad_maximum_fusion.5), channel_id=1, source_target_pairs={{0,2},{2,0},{4,6},{6,4},{8,10},{10,8},{12,14},{14,12},{16,18},{18,... | collective-permute-start | bytes 3538952 | tf_op jit(solution)/shard_map/ppermute | solution.py:47
  136.1 20.1 %collective-permute-start.25 = (bf16[256,512]{1,0:T(8,128)(2,1)S(1)}, bf16[256,512]{1,0:T(8,128)(2,1)S(1)}, u32[]{:S(2)}, u32[]{:S(2)}) collective-permute-start(bf16[256,512]{1,0:T(8,128)(2,1)S(1)} %get-tuple-element.17), channel_id=1, source_target_pairs={{0,4},{2,6},{4,0},{6,2},{8,12},{10,14},{12,8},{14,10},{16,20},{18,... | collective-permute-start | bytes 786440 | tf_op jit(solution)/shard_map/ppermute | solution.py:47
  145.8 10.3 %collective-permute-start.24 = (bf16[256,384]{1,0:T(8,128)(2,1)S(1)}, bf16[256,384]{1,0:T(8,128)(2,1)S(1)}, u32[]{:S(2)}, u32[]{:S(2)}) collective-permute-start(bf16[256,384]{1,0:T(8,128)(2,1)S(1)} %get-tuple-element.16), channel_id=1, source_target_pairs={{0,4},{2,6},{4,0},{6,2},{8,12},{10,14},{12,8},{14,10},{16,20},{18,... | collective-permute-start | bytes 589832 | tf_op jit(solution)/shard_map/ppermute | solution.py:47
  154.1 7.0 %collective-permute-start.26 = (bf16[256,384]{1,0:T(8,128)(2,1)S(1)}, bf16[256,384]{1,0:T(8,128)(2,1)S(1)}, u32[]{:S(2)}, u32[]{:S(2)}) collective-permute-start(bf16[256,384]{1,0:T(8,128)(2,1)S(1)} %get-tuple-element.18), channel_id=1, source_target_pairs={{0,4},{2,6},{4,0},{6,2},{8,12},{10,14},{12,8},{14,10},{16,20},{18,... | collective-permute-start | bytes 589832 | tf_op jit(solution)/shard_map/ppermute | solution.py:47
  (15 other events, 110.3 us)

commit v2 on v0

v2 whole, which is shorter than its diff:
```python
import functools
import math

import jax
import jax.numpy as jnp
from jax import lax
from jax.experimental import pallas as pl
from jax.experimental.pallas import tpu as pltpu
from jax.sharding import PartitionSpec as P

HD = 128
BLK = 128
TOK = 256
ZN, YN, XN, CN = 8, 4, 2, 2
ROWS = ZN * YN
HALF = 10
CHUNKS = (6, 4)
NEG = -1e30
C2 = math.log2(math.e) / math.sqrt(HD)


def place(row, x, core):
    return ((row % ROWS) * XN + x % XN) * CN + core % CN


DEVICES = [(r, x, c) for r in range(ROWS) for x in range(XN) for c in range(CN)]


def route(to):
    return [(place(*d), place(*to(*d))) for d in DEVICES]


ACROSS = route(lambda r, x, c: (r, 1 - x, c))
CORES = route(lambda r, x, c: (r, x, 1 - c))
OUTWARD = route(lambda r, x, c: (r + (1 if c else -1), x, c))
INWARD = route(lambda r, x, c: (r + (-1 if c else 1), x, c))
ZUP = route(lambda r, x, c: (r + YN, x, c))
ZDOWN = route(lambda r, x, c: (r - YN, x, c))


def pack_kernel(*refs):
    whole = refs[-1]
    for i, block in enumerate(refs[:-1]):

        @pl.when(pl.program_id(0) == i)
        def _():
            whole[...] = block[...]


def pack(*blocks):
    shape = blocks[0].shape
    zeros = (0,) * len(shape)
    return pl.pallas_call(
        pack_kernel,
        out_shape=jax.ShapeDtypeStruct((len(blocks), *shape), blocks[0].dtype),
        grid=(len(blocks),),
        in_specs=[pl.BlockSpec(shape, lambda i: zeros)] * len(blocks),
        out_specs=pl.BlockSpec((None, *shape), lambda i: (i, *zeros)),
        compiler_params=pltpu.CompilerParams(vmem_limit_bytes=32 * 1024 * 1024),
        name="pack",
    )(*blocks)


def gather_kernel(*refs):
    whole = refs[-1]
    for i, pair in enumerate(refs[:-1]):
        whole[i] = pair[...]


def gather_heads(first, heads, *pairs):
    pair = (2, TOK, HD)

    def spec(width):
        start = first if width == HALF * HD else 0
        return pl.BlockSpec(pair, lambda i: (0, 0, start + i))

    return pl.pallas_call(
        gather_kernel,
        out_shape=jax.ShapeDtypeStruct((len(pairs), 2, TOK, heads * HD), jnp.bfloat16),
        grid=(heads,),
        in_specs=[spec(p.shape[-1]) for p in pairs],
        out_specs=pl.BlockSpec((len(pairs), *pair), lambda i: (0, 0, 0, i)),
        compiler_params=pltpu.CompilerParams(vmem_limit_bytes=32 * 1024 * 1024),
        name="gather_heads",
    )(*pairs)


def softened(parts, top):
    weights = [jnp.exp2((part - top) * C2) for part in parts]
    total = jnp.sum(functools.reduce(jnp.add, weights), axis=1, keepdims=True)
    return jnp.concatenate([w.astype(jnp.bfloat16) for w in weights], axis=1), total


def scored(query, keys):
    return lax.dot_general(query, keys, (((1,), (1,)), ((), ())), preferred_element_type=jnp.float32)


UNITS = [
    (tile, slice(block * BLK, (block + 1) * BLK), tile * 2 + block)
    for tile in range(2)
    for block in range(TOK // BLK)
]


def latent_kernel(
    half_ref, slots_ref, valid_ref, text_at_ref,
    q_own, q_far, k_own, v_own, far, out_own, out_far, mid, cc_part,
    sums, stats, keys, values,
):
    tiles = [
        (k_own, v_own),
        *[(pair.at[0], pair.at[1]) for pair in (far, out_own, out_far, mid)],
        *[(cc_part.at[i, 0], cc_part.at[i, 1]) for i in range(5)],
    ]
    for at, (k, v) in enumerate(tiles):
        keys[at * TOK : (at + 1) * TOK, :] = k[...]
        values[at * TOK : (at + 1) * TOK, :] = v[...]

    def listed(row, store):
        starts = [pl.multiple_of(slots_ref[row, s] * BLK, BLK) for s in range(8)]
        return jnp.concatenate([store[pl.ds(at, BLK), :] for at in starts], axis=0)

    def score(unit):
        tile, rows, row = unit
        scores = scored((q_own, q_far)[tile][rows, :], listed(row, keys))
        parts = [scores[:, s * BLK : (s + 1) * BLK] for s in range(8)]
        for s in range(1, 8):
            parts[s] = jnp.where(valid_ref[row, s] > 0, parts[s], NEG)
        return parts

    left = lax.broadcasted_iota(jnp.int32, (BLK, HD), 1) < HD // 2
    ahead = score(UNITS[0])
    for unit, later in zip(UNITS, UNITS[1:] + [None]):
        parts, ahead = ahead, score(later) if later else None
        tile, rows, row = unit
        top = jnp.max(functools.reduce(jnp.maximum, parts), axis=1, keepdims=True)
        rounded, total = softened(parts, top)
        sums[tile, rows, :] = jnp.dot(
            rounded, listed(row, values), preferred_element_type=jnp.float32
        )
        stats[tile, rows, :] = jnp.where(left, top, total)


def text_kernel(
    half_ref, slots_ref, valid_ref, text_at_ref,
    q_own, q_far, sums, stats, near, last, cc_near, cc_last, o_own, o_far, keys, values,
):
    for core, (most, other) in enumerate(((near, last), (cc_near, cc_last))):
        for at, plane in enumerate([most.at[i] for i in range(7)] + [other]):
            to = at * BLK + core * 64
            keys[to : to + 64, :] = plane[0]
            values[to : to + 64, :] = plane[1]

    def listed(tile, store):
        starts = [pl.multiple_of(text_at_ref[tile, i] * BLK, BLK) for i in range(2)]
        return jnp.concatenate([store[pl.ds(at, BLK), :] for at in starts], axis=0)

    scores = [
        scored((q_own, q_far)[tile][rows, :], listed(tile, keys)) for tile, rows, row in UNITS
    ]
    parts = [[score[:, :BLK], score[:, BLK:]] for score in scores]
    before = [stats[tile, rows, :1] for tile, rows, row in UNITS]
    ends = slice(HD // 2, HD // 2 + 1)
    totals_before = [stats[tile, rows, ends] for tile, rows, row in UNITS]
    tops = [
        jnp.maximum(old, jnp.max(jnp.maximum(*part), axis=1, keepdims=True))
        for old, part in zip(before, parts)
    ]
    softs = [softened(part, top) for part, top in zip(parts, tops)]
    fades = [jnp.exp2((old - top) * C2) for old, top in zip(before, tops)]
    mixes = [
        jnp.dot(rounded, listed(tile, values), preferred_element_type=jnp.float32)
        for (rounded, _), (tile, rows, row) in zip(softs, UNITS)
    ]
    for i, (tile, rows, row) in enumerate(UNITS):
        total = totals_before[i] * fades[i] + softs[i][1]
        mixed = (sums[tile, rows, :] * fades[i] + mixes[i]) / total
        (o_own, o_far)[tile][rows, :] = mixed.astype(jnp.bfloat16)


def specs_of(first):
    def whole(i, half, *_):
        return (0, half[0] * HALF + first + i)

    def halved(lead):
        return lambda i, *_: (0,) * lead + (first + i,)

    def chunk(lead):
        return lambda i, *_: (0,) * lead + (i,)

    return whole, halved, chunk


def call(kernel, name, heads, keys, in_specs, out_shape, out_specs, rows, arguments):
    return pl.pallas_call(
        kernel,
        out_shape=out_shape,
        grid_spec=pltpu.PrefetchScalarGridSpec(
            num_scalar_prefetch=4,
            grid=(heads,),
            in_specs=in_specs,
            out_specs=out_specs,
            scratch_shapes=[pltpu.VMEM((rows, HD), jnp.bfloat16)] * 2,
        ),
        compiler_params=pltpu.CompilerParams(vmem_limit_bytes=56 * 1024 * 1024),
        cost_estimate=pl.CostEstimate(
            flops=heads * 4 * BLK * keys * HD * 4 * 6,
            bytes_accessed=heads * keys * 2000,
            transcendentals=heads * 4 * BLK * keys,
        ),
        name=name,
    )(*arguments)


def latent(first, heads, scalars, *arrays):
    whole, halved, chunk = specs_of(first)
    pair = (2, TOK, HD)
    in_specs = [
        pl.BlockSpec((TOK, HD), whole),
        pl.BlockSpec((TOK, HD), halved(1)),
        pl.BlockSpec((TOK, HD), whole),
        pl.BlockSpec((TOK, HD), whole),
        pl.BlockSpec(pair, chunk(2)),
        pl.BlockSpec(pair, halved(2)),
        pl.BlockSpec(pair, chunk(2)),
        pl.BlockSpec(pair, chunk(2)),
        pl.BlockSpec((5, *pair), chunk(3)),
    ]
    out = jax.ShapeDtypeStruct((2, TOK, heads * HD), jnp.float32)
    out_specs = (pl.BlockSpec(pair, chunk(2)), pl.BlockSpec(pair, chunk(2)))
    return call(
        latent_kernel, "latent", heads, 1024, in_specs, (out, out), out_specs, 10 * TOK,
        (*scalars, *arrays),
    )


def finish(first, heads, scalars, *arrays):
    whole, halved, chunk = specs_of(first)
    in_specs = [
        pl.BlockSpec((TOK, HD), whole),
        pl.BlockSpec((TOK, HD), halved(1)),
        pl.BlockSpec((2, TOK, HD), chunk(2)),
        pl.BlockSpec((2, TOK, HD), chunk(2)),
        *[pl.BlockSpec((7, 2, 64, HD), halved(3)), pl.BlockSpec((2, 64, HD), halved(2))] * 2,
    ]
    out = jax.ShapeDtypeStruct((TOK, heads * HD), jnp.bfloat16)
    out_specs = (pl.BlockSpec((TOK, HD), chunk(1)), pl.BlockSpec((TOK, HD), chunk(1)))
    return call(
        text_kernel, "finish", heads, 256, in_specs, (out, out), out_specs, ZN * BLK,
        (*scalars, *arrays),
    )


PLANES = [
    [place(z * YN + y, x, c) for y in range(YN) for x in range(XN)]
    for z in range(ZN)
    for c in range(CN)
]


def send(what, block, to):
    with jax.named_scope(what):
        return lax.ppermute(block, "seq", to)


def on_device(queries, latent_keys, latent_values, prompt_keyvals, block_lists, tile_segment):
    width = HALF * HD
    device = lax.axis_index("seq")
    core, x, row = device % CN, device // CN % XN, device // (CN * XN)
    z = row // YN

    def half_of(array, which, first=0, heads=HALF):
        start = which * width + first * HD
        return lax.dynamic_slice_in_dim(array, start, heads * HD, array.ndim - 1)

    def pair_of(which, first=0, heads=HALF):
        return jnp.stack([half_of(a, which, first, heads) for a in (latent_keys, latent_values)])

    def whereabouts(*tables):
        table = jnp.concatenate(tables, axis=0)
        lists, segments = table[:, :8], table[::2, 8]

        def held(which):
            side = 2 * which - 1
            return [
                2 * x + which,
                2 * (1 - x) + which,
                2 * x + which - 4 * side,
                2 * (1 - x) + which - 4 * side,
                2 - which + 4 * side,
            ]

        offsets = jnp.stack(held(core) + held(1 - core))
        wanted = lists // 2 - 4 * row
        position = jnp.argmax(wanted[:, :, None] == offsets[None, None, :], axis=2).astype(jnp.int32)
        valid = (lists >= 0).astype(jnp.int32)
        slots = jnp.where(lists >= 0, position * 2 + lists % 2, 0)
        ahead = (2 * segments[:, None] + jnp.arange(2)[None, :] - z) % ZN
        order = (0, 1, 2, 3, 7, 6, 5, 4)
        text_at = sum(jnp.where(ahead == k, at, 0) for k, at in enumerate(order))
        return (x[None].astype(jnp.int32), slots, valid, text_at.astype(jnp.int32))

    firsts = [sum(CHUNKS[:i]) for i in range(len(CHUNKS))]
    gives = [pair_of(1 - x, f, h) for f, h in zip(firsts, CHUNKS)]
    kv_own = pair_of(x)

    own_table = jnp.concatenate(
        [block_lists, jnp.broadcast_to(tile_segment[:, None], (2, 8))], axis=1
    )
    far_table = send("table", own_table, ACROSS)
    halves = jnp.stack([prompt_keyvals[..., :width], prompt_keyvals[..., width:]])
    spread = jnp.broadcast_to(halves[None], (YN, *halves.shape))
    plane = lax.all_to_all(
        spread.reshape(YN * XN, *halves.shape[1:]), "seq", 0, 0, axis_index_groups=PLANES
    )
    plane = jnp.swapaxes(plane, 0, 1).reshape(2, 64, width)
    far1 = send("far", gives[0], ACROSS)
    kv_own, plane, far_table = lax.optimization_barrier((kv_own, plane, far_table))
    scalars = whereabouts(own_table, far_table)
    out_own = send("out_own", kv_own, OUTWARD)
    q_far = send("q_far", half_of(queries, 1 - x), ACROSS)
    up1, down1 = send("text_up", plane, ZUP), send("text_down", plane, ZDOWN)
    give2, up1, down1, far1, out_own, kv_own, q_far, *scalars = lax.optimization_barrier(
        (gives[1], up1, down1, far1, out_own, kv_own, q_far, *scalars)
    )

    def between(first, heads, far):
        return jnp.where(x != core, kv_own[..., first * HD : (first + heads) * HD], far)

    def swapped(i, far, out_far, mid):
        held_here = gather_heads(firsts[i], CHUNKS[i], kv_own, far, out_own, out_far, mid)
        return send("cc_part", held_here, CORES)

    def attended(i, far, out_far, mid, cc_part):
        return latent(
            firsts[i], CHUNKS[i], scalars, queries, q_far, latent_keys, latent_values,
            far, out_own, out_far, mid, cc_part,
        )

    far2 = send("far", give2, ACROSS)
    out_far1 = send("out_far", far1, OUTWARD)
    mid1 = send("mid", between(firsts[0], CHUNKS[0], far1), INWARD)
    up2, down2 = send("text_up", up1, ZUP), send("text_down", down1, ZDOWN)
    far2, out_far1, mid1, up2, down2 = lax.optimization_barrier((far2, out_far1, mid1, up2, down2))

    out_far2 = send("out_far", far2, OUTWARD)
    mid2 = send("mid", between(firsts[1], CHUNKS[1], far2), INWARD)
    up3, down3 = send("text_up", up2, ZUP), send("text_down", down2, ZDOWN)
    sums1 = attended(0, far1, out_far1, mid1, swapped(0, far1, out_far1, mid1))
    out_far2, mid2, up3, down3, *sums1 = lax.optimization_barrier(
        (out_far2, mid2, up3, down3, *sums1)
    )

    up4 = send("text_up", up3, ZUP)
    near = pack(plane, down1, down2, down3, up1, up2, up3)
    cc_near = send("cc_text", near, CORES)
    sums2 = attended(1, far2, out_far2, mid2, swapped(1, far2, out_far2, mid2))
    up4, _, _ = lax.optimization_barrier((up4, *sums2))
    cc_last = send("cc_text", up4, CORES)
    text = (near, up4, cc_near, cc_last)
    results = []
    for first, heads, sums in zip(firsts, CHUNKS, (sums1, sums2)):
        mine, theirs = finish(first, heads, scalars, queries, q_far, *sums, *text)
        results.append((mine, send("back", theirs, ACROSS)))
    mine = jnp.concatenate([m for m, _ in results], axis=1)
    back = jnp.concatenate([b for _, b in results], axis=1)
    left, right = jnp.where(x == 0, mine, back), jnp.where(x == 0, back, mine)
    return jnp.concatenate([left, right], axis=1)


def solution(mesh):
    in_specs = (
        P(("cfg", "seq"), None),
        P(("cfg", "seq"), None),
        P(("cfg", "seq"), None),
        P(None, ("cfg", "seq"), None),
        P("seq", None),
        P("seq"),
    )
    out_specs = P(("cfg", "seq"), None)
    return jax.shard_map(
        on_device, mesh=mesh, in_specs=in_specs, out_specs=out_specs, check_vma=False
    )
```

time: 439 us -> 149 us (0.34)
  starting transfers between devices: 169 us -> 40.8 us
  waiting for transfers between devices: 133 us -> 49.4 us
  matrix products: 67.7 us -> 0 us
  Pallas kernels: 0 us -> 39.3 us
  other arithmetic: 29.9 us -> 6.06 us
  between operations: 14.2 us -> 1.02 us
  local copies, waits for them, and re-layouts: 23 us -> 10.5 us
    ppermute x6 -> x22, starting transfers between devices: 169 us -> 35.7 us  [send(): return lax.ppermute(block, 'seq', to)]
    all_gather x1 -> x0, waiting for transfers between devices: 127 us -> none  [on_device(): whole_text = lax.all_gather(prompt_keyvals, 'seq', axis=1, tiled=True)]
    dot_general x40 -> x0, matrix products: 67.7 us -> none  [the longest x20 34.4 us: attend_head(): jnp.dot(weights.astype(jnp.bfloat16), head_values, preferred_element_type...]
    ppermute x6 -> x22, waiting for transfers between devices: 4.94 us -> 49.4 us  [send(): return lax.ppermute(block, 'seq', to)]
    pallas_call x0 -> x7, Pallas kernels: none -> 39.3 us  [the longest x4 34.6 us: call(): pl.pallas_call(kernel, out_shape=out_shape, grid_spec=pltpu.PrefetchScala...]
    concatenate x1 -> x2, other arithmetic: 14.7 us -> 1.15 us  [the longest x1 1.15 us: on_device(): return jnp.concatenate([left, right], axis=1)]
    reduce_sum x20 -> x0, other arithmetic: 12.9 us -> none  [attend_head(): total = jnp.sum(weights, axis=1, keepdims=True)]
    unnamed x21 -> x46, local copies, waits for them, and re-layouts: 10.8 us -> 1.72 us
  transfers between devices with their start and end apart: 7 -> 23, of which waited for: 3 -> 9; matrix products, arithmetic and copies ran while one was open for 5% -> 8% of each run, Pallas kernels for 0% -> 19%
where the time goes in v2:
time: 149 us; the launch traced here: 147 us
  waiting for transfers between devices  49.4 us (33%)
  starting transfers between devices  40.8 us (27%)
  Pallas kernels  39.3 us (26%)
  local copies, waits for them, and re-layouts  10.5 us (7%)
  other arithmetic  6.06 us (4%)
    ppermute x22, waiting for transfers between devices, send(): return lax.ppermute(block, 'seq', to)  49.4 us
    ppermute x22, starting transfers between devices, send(): return lax.ppermute(block, 'seq', to)  35.7 us
    pallas_call x4, Pallas kernels, call(): pl.pallas_call(kernel, out_shape=out_shape, grid_spec=pltpu.PrefetchScala...  34.6 us
    all_to_all x1, starting transfers between devices, on_device(): lax.all_to_all(spread.reshape(YN * XN, *halves.shape[1:]), 'seq', 0, 0, a...  5.1 us
    another operation x3, local copies, waits for them, and re-layouts, pair_of(): jnp.stack([half_of(a, which, first, heads) for a in (latent_keys, latent_...  3.31 us
    pallas_call x2, Pallas kernels, gather_heads(): pl.pallas_call(gather_kernel, out_shape=jax.ShapeDtypeStruct((len(pairs),...  2.99 us
  transfers between devices with their start and end apart: 23, of which 9 were waited for; matrix products, arithmetic and copies ran while one was open for 8% of the time, Pallas kernels for 19%

profile of v2, /device:TPU:4, one launch (start us, length us, event | category | flops | bytes accessed | tf_op | source)
XLA Modules:
  0.0 147.0 jit_solution(7189702795195425957)
XLA Ops:
  1.7 5.1 %all-to-all-start = ((bf16[8,2,8,1280]{3,2,1,0:T(8,128)(2,1)}), bf16[8,2,8,1280]{3,2,1,0:T(8,128)(2,1)}, u32[]{:S(2)}, u32[]{:S(2)}) async-start(bf16[8,2,8,1280]{3,2,1,0:T(8,128)(2,1)} %bitcast.6), calls=%async_computation | async-start | bytes 655360 | tf_op jit(solution)/shard_map/all_to_all | solution.py:313
  7.4 2.1 %collective-permute-start = (s32[2,16]{1,0:T(2,128)S(1)}, s32[2,16]{1,0:T(2,128)S(1)}, u32[]{:S(2)}, u32[]{:S(2)}) collective-permute-start(s32[2,16]{1,0:T(2,128)S(1)} %concatenate.15), channel_id=1, source_target_pairs={{0,4},{2,6},{4,0},{6,2},{8,12},{10,14},{12,8},{14,10},{16,20},{18,... | collective-permute-start | bytes 392 | tf_op jit(solution)/shard_map/table/ppermute | solution.py:263
  9.6 1.2 dynamic-slice_bitcast_fusion.2
  12.6 2.0 %collective-permute-start.5 = (bf16[256,1280]{1,0:T(8,128)(2,1)}, bf16[256,1280]{1,0:T(8,128)(2,1)}, u32[]{:S(2)}, u32[]{:S(2)}) collective-permute-start(bf16[256,1280]{1,0:T(8,128)(2,1)} %constant_dynamic-slice_fusion), channel_id=1, source_target_pairs={{0,4},{2,6},{4,0},{6,2},{8,12},{10,14},{12,8},{14,10},{16,20},{18,... | collective-permute-start | bytes 1966088 | tf_op jit(solution)/shard_map/q_far/ppermute | solution.py:263
  14.6 1.2 dynamic-slice_bitcast_fusion
  15.8 1.0 dynamic-slice_bitcast_fusion.4
  17.8 1.7 %copy_bitcast_fusion.refs_0_ = bf16[2,64,1280]{2,1,0:T(8,128)(2,1)} fusion(bf16[8,2,8,1280]{3,2,1,0:T(8,128)(2,1)} %all-to-all-done), kind=kLoop, calls=%fused_computation.12 | loop fusion | bytes 655360 | tf_op jit(solution)/shard_map/reshape | solution.py:316
  19.6 1.9 %collective-permute-start.1 = (bf16[2,64,1280]{2,1,0:T(8,128)(2,1)}, bf16[2,64,1280]{2,1,0:T(8,128)(2,1)}, u32[]{:S(2)}, u32[]{:S(2)}) collective-permute-start(bf16[2,64,1280]{2,1,0:T(8,128)(2,1)} %copy_bitcast_fusion.refs_0_), channel_id=1, source_target_pairs={{0,32},{2,34},{4,36},{6,38},{8,40},{10,42},{12,44},{14,46},{16,48}... | collective-permute-start | bytes 983048 | tf_op jit(solution)/shard_map/text_up/ppermute | solution.py:263
  21.5 3.9 %collective-permute-start.2 = (bf16[2,64,1280]{2,1,0:T(8,128)(2,1)}, bf16[2,64,1280]{2,1,0:T(8,128)(2,1)}, u32[]{:S(2)}, u32[]{:S(2)}) collective-permute-start(bf16[2,64,1280]{2,1,0:T(8,128)(2,1)} %copy_bitcast_fusion.refs_0_), channel_id=1, source_target_pairs={{0,224},{2,226},{4,228},{6,230},{8,232},{10,234},{12,236},{14,238}... | collective-permute-start | bytes 983048 | tf_op jit(solution)/shard_map/text_down/ppermute | solution.py:263
  25.4 4.1 %collective-permute-start.4 = (bf16[2,256,1280]{2,1,0:T(8,128)(2,1)S(1)}, bf16[2,256,1280]{2,1,0:T(8,128)(2,1)S(1)}, u32[]{:S(2)}, u32[]{:S(2)}) collective-permute-start(bf16[2,256,1280]{2,1,0:T(8,128)(2,1)S(1)} %pad_maximum_fusion.refs_0_), channel_id=1, source_target_pairs={{0,248},{2,10},{4,252},{6,14},{8,0},{10,18},{12,4},{14,22},{16,8},... | collective-permute-start | bytes 3932168 | tf_op jit(solution)/shard_map/out_own/ppermute | solution.py:263
  32.4 12.0 %collective-permute-done.5.q_far = bf16[256,1280]{1,0:T(8,128)(2,1)} collective-permute-done((bf16[256,1280]{1,0:T(8,128)(2,1)}, bf16[256,1280]{1,0:T(8,128)(2,1)}, u32[]{:S(2)}, u32[]{:S(2)}) %collective-permute-start.5) | collective-permute-done | bytes 655392 | tf_op jit(solution)/shard_map/q_far/ppermute | solution.py:263
  46.1 6.6 %collective-permute-start.7 = (bf16[2,256,768]{2,1,0:T(8,128)(2,1)S(1)}, bf16[2,256,768]{2,1,0:T(8,128)(2,1)S(1)}, u32[]{:S(2)}, u32[]{:S(2)}) collective-permute-start(bf16[2,256,768]{2,1,0:T(8,128)(2,1)S(1)} %collective-permute-done.3.refs_1_.far), channel_id=1, source_target_pairs={{0,248},{2,10},{4,252},{6,14},{8,0},{10,18},{12,4},{14,22},{16,8},... | collective-permute-start | bytes 2359304 | tf_op jit(solution)/shard_map/out_far/ppermute | solution.py:263
  53.3 1.7 %collective-permute-start.10 = (bf16[2,64,1280]{2,1,0:T(8,128)(2,1)}, bf16[2,64,1280]{2,1,0:T(8,128)(2,1)S(1)}, u32[]{:S(2)}, u32[]{:S(2)}) collective-permute-start(bf16[2,64,1280]{2,1,0:T(8,128)(2,1)} %collective-permute-done.2.refs_1_), channel_id=1, source_target_pairs={{0,224},{2,226},{4,228},{6,230},{8,232},{10,234},{12,236},{14,238}... | collective-permute-start | bytes 983048 | tf_op jit(solution)/shard_map/text_down/ppermute | solution.py:263
  55.3 19.5 %collective-permute-done.10.refs_2_ = bf16[2,64,1280]{2,1,0:T(8,128)(2,1)S(1)} collective-permute-done((bf16[2,64,1280]{2,1,0:T(8,128)(2,1)}, bf16[2,64,1280]{2,1,0:T(8,128)(2,1)S(1)}, u32[]{:S(2)}, u32[]{:S(2)}) %collective-permute-start.10) | collective-permute-done | bytes 327712 | tf_op jit(solution)/shard_map/text_down/ppermute | solution.py:263
  74.8 1.8 %gather_heads.2 = bf16[5,2,256,768]{3,2,1,0:T(8,128)(2,1)S(1)} custom-call(bf16[2,256,1280]{2,1,0:T(8,128)(2,1)S(1)} %pad_maximum_fusion.refs_0_, bf16[2,256,768]{2,1,0:T(8,128)(2,1)S(1)} %collective-permute-done.3.refs_1_.far, bf16[2,256,1280]{2,1,0:T(8,128)(2,1)S(1)} %collective-permute-done.4.refs_2_.out_own, ...), custom_call_target="tpu_custom_call" | custom-call | tf_op jit(solution)/shard_map/gather_heads/pallas_call | solution.py:77
  76.8 5.3 %collective-permute-start.11 = (bf16[2,256,512]{2,1,0:T(8,128)(2,1)S(1)}, bf16[2,256,512]{2,1,0:T(8,128)(2,1)S(1)}, u32[]{:S(2)}, u32[]{:S(2)}) collective-permute-start(bf16[2,256,512]{2,1,0:T(8,128)(2,1)S(1)} %collective-permute-done.6.refs_1_.far), channel_id=1, source_target_pairs={{0,248},{2,10},{4,252},{6,14},{8,0},{10,18},{12,4},{14,22},{16,8},... | collective-permute-start | bytes 1572872 | tf_op jit(solution)/shard_map/out_far/ppermute | solution.py:263
  82.5 3.2 %collective-permute-start.14 = (bf16[2,64,1280]{2,1,0:T(8,128)(2,1)S(1)}, bf16[2,64,1280]{2,1,0:T(8,128)(2,1)S(1)}, u32[]{:S(2)}, u32[]{:S(2)}) collective-permute-start(bf16[2,64,1280]{2,1,0:T(8,128)(2,1)S(1)} %collective-permute-done.10.refs_2_), channel_id=1, source_target_pairs={{0,224},{2,226},{4,228},{6,230},{8,232},{10,234},{12,236},{14,238}... | collective-permute-start | bytes 983048 | tf_op jit(solution)/shard_map/text_down/ppermute | solution.py:263
  85.7 10.7 %latent.2 = (f32[2,256,768]{2,1,0:T(8,128)}, f32[2,256,768]{2,1,0:T(8,128)}) custom-call(s32[1]{0:T(128)} %bitcast.12.half_ref, s32[4,8]{1,0:T(4,128)} %fusion.2.slots_ref, s32[4,8]{1,0:T(4,128)} %get-tuple-element.46.valid_ref, s32[2,2]{1,0:T(2,128)} %fusion.9.text_at_ref, bf16[256,2560]{1,0:T(8,128)(2,1)} %q_own.7, ...), custom_call_target="tpu_custom_call" | custom-call | flops 9663676416 | bytes 12288000 | tf_op jit(solution)/shard_map/latent/pallas_call | solution.py:195
  96.4 4.6 %collective-permute-done.14.refs_3_ = bf16[2,64,1280]{2,1,0:T(8,128)(2,1)S(1)} collective-permute-done((bf16[2,64,1280]{2,1,0:T(8,128)(2,1)S(1)}, bf16[2,64,1280]{2,1,0:T(8,128)(2,1)S(1)}, u32[]{:S(2)}, u32[]{:S(2)}) %collective-permute-start.14) | collective-permute-done | bytes 327712 | tf_op jit(solution)/shard_map/text_down/ppermute | solution.py:263
  101.8 1.2 gather_heads.3
  103.3 1.7 %pack.1.near = bf16[7,2,64,1280]{3,2,1,0:T(8,128)(2,1)S(1)} custom-call(bf16[2,64,1280]{2,1,0:T(8,128)(2,1)} %copy_bitcast_fusion.refs_0_, bf16[2,64,1280]{2,1,0:T(8,128)(2,1)} %collective-permute-done.2.refs_1_, bf16[2,64,1280]{2,1,0:T(8,128)(2,1)S(1)} %copy-done.10, bf16[2,64,1280]{2,1,0:T(8,128)(2,1)S(1)} %copy-done.14, ...), custom_call_target="tpu_custom_call" | custom-call | tf_op jit(solution)/shard_map/pack/pallas_call | solution.py:53
  105.5 2.7 %collective-permute-done.17.cc_part = bf16[5,2,256,512]{3,2,1,0:T(8,128)(2,1)} collective-permute-done((bf16[5,2,256,512]{3,2,1,0:T(8,128)(2,1)S(1)}, bf16[5,2,256,512]{3,2,1,0:T(8,128)(2,1)}, u32[]{:S(2)}, u32[]{:S(2)}) %collective-permute-start.17) | collective-permute-done | bytes 2621472 | tf_op jit(solution)/shard_map/cc_part/ppermute | solution.py:263
  108.1 8.0 %latent.3 = (f32[2,256,512]{2,1,0:T(8,128)}, f32[2,256,512]{2,1,0:T(8,128)}) custom-call(s32[1]{0:T(128)} %bitcast.12.half_ref, s32[4,8]{1,0:T(4,128)} %fusion.2.slots_ref, s32[4,8]{1,0:T(4,128)} %get-tuple-element.46.valid_ref, s32[2,2]{1,0:T(2,128)} %fusion.9.text_at_ref, bf16[256,2560]{1,0:T(8,128)(2,1)} %q_own.7, ...), custom_call_target="tpu_custom_call" | custom-call | flops 6442450944 | bytes 8192000 | tf_op jit(solution)/shard_map/latent/pallas_call | solution.py:195
  116.2 1.2 collective-permute-done.16.last
  117.4 1.6 %collective-permute-done.19.cc_last = bf16[2,64,1280]{2,1,0:T(8,128)(2,1)S(1)} collective-permute-done((bf16[2,64,1280]{2,1,0:T(8,128)(2,1)S(1)}, bf16[2,64,1280]{2,1,0:T(8,128)(2,1)S(1)}, u32[]{:S(2)}, u32[]{:S(2)}) %collective-permute-start.19) | collective-permute-done | bytes 327712 | tf_op jit(solution)/shard_map/cc_text/ppermute | solution.py:263
  119.8 9.0 %finish.2 = (bf16[256,768]{1,0:T(8,128)(2,1)}, bf16[256,768]{1,0:T(8,128)(2,1)}) custom-call(s32[1]{0:T(128)} %bitcast.12.half_ref, s32[4,8]{1,0:T(4,128)} %fusion.2.slots_ref, s32[4,8]{1,0:T(4,128)} %get-tuple-element.46.valid_ref, s32[2,2]{1,0:T(2,128)} %fusion.9.text_at_ref, bf16[256,2560]{1,0:T(8,128)(2,1)} %q_own.7, ...), custom_call_target="tpu_custom_call" | custom-call | flops 2415919104 | bytes 3072000 | tf_op jit(solution)/shard_map/finish/pallas_call | solution.py:195
  129.2 6.9 %finish.3 = (bf16[256,512]{1,0:T(8,128)(2,1)}, bf16[256,512]{1,0:T(8,128)(2,1)}) custom-call(s32[1]{0:T(128)} %bitcast.12.half_ref, s32[4,8]{1,0:T(4,128)} %fusion.2.slots_ref, s32[4,8]{1,0:T(4,128)} %get-tuple-element.46.valid_ref, s32[2,2]{1,0:T(2,128)} %fusion.9.text_at_ref, bf16[256,2560]{1,0:T(8,128)(2,1)} %q_own.7, ...), custom_call_target="tpu_custom_call" | custom-call | flops 1610612736 | bytes 2048000 | tf_op jit(solution)/shard_map/finish/pallas_call | solution.py:195
  136.1 1.7 %collective-permute-start.21 = (bf16[256,512]{1,0:T(8,128)(2,1)}, bf16[256,512]{1,0:T(8,128)(2,1)S(1)}, u32[]{:S(2)}, u32[]{:S(2)}) collective-permute-start(bf16[256,512]{1,0:T(8,128)(2,1)} %get-tuple-element.74), channel_id=1, source_target_pairs={{0,4},{2,6},{4,0},{6,2},{8,12},{10,14},{12,8},{14,10},{16,20},{18,... | collective-permute-start | bytes 786440 | tf_op jit(solution)/shard_map/back/ppermute | solution.py:263
  137.8 1.0 constant_dynamic-update-slice_fusion
  138.7 2.2 %collective-permute-done.20 = bf16[256,768]{1,0:T(8,128)(2,1)S(1)} collective-permute-done((bf16[256,768]{1,0:T(8,128)(2,1)}, bf16[256,768]{1,0:T(8,128)(2,1)S(1)}, u32[]{:S(2)}, u32[]{:S(2)}) %collective-permute-start.20) | collective-permute-done | bytes 393248 | tf_op jit(solution)/shard_map/back/ppermute | solution.py:263
  141.0 4.8 %collective-permute-done.21 = bf16[256,512]{1,0:T(8,128)(2,1)S(1)} collective-permute-done((bf16[256,512]{1,0:T(8,128)(2,1)}, bf16[256,512]{1,0:T(8,128)(2,1)S(1)}, u32[]{:S(2)}, u32[]{:S(2)}) %collective-permute-start.21) | collective-permute-done | bytes 262176 | tf_op jit(solution)/shard_map/back/ppermute | solution.py:263
  145.9 1.1 pad_maximum_fusion.1
  (94 shorter events, 13.4 us)
Async XLA Ops:
  0.0 9.5 %copy-start.18 = (bf16[256,2560]{1,0:T(8,128)(2,1)S(1)}, bf16[256,2560]{1,0:T(8,128)(2,1)}, u32[]{:S(2)}) copy-start(bf16[256,2560]{1,0:T(8,128)(2,1)} %k_own.3) | copy-start | bytes 3932164
  1.7 16.2 %all-to-all-start = ((bf16[8,2,8,1280]{3,2,1,0:T(8,128)(2,1)}), bf16[8,2,8,1280]{3,2,1,0:T(8,128)(2,1)}, u32[]{:S(2)}, u32[]{:S(2)}) async-start(bf16[8,2,8,1280]{3,2,1,0:T(8,128)(2,1)} %bitcast.6), calls=%async_computation | async-start | bytes 655360 | tf_op jit(solution)/shard_map/all_to_all | solution.py:313
  7.4 12.1 %collective-permute-start = (s32[2,16]{1,0:T(2,128)S(1)}, s32[2,16]{1,0:T(2,128)S(1)}, u32[]{:S(2)}, u32[]{:S(2)}) collective-permute-start(s32[2,16]{1,0:T(2,128)S(1)} %concatenate.15), channel_id=1, source_target_pairs={{0,4},{2,6},{4,0},{6,2},{8,12},{10,14},{12,8},{14,10},{16,20},{18,... | collective-permute-start | bytes 392 | tf_op jit(solution)/shard_map/table/ppermute | solution.py:263
  11.7 32.8 %collective-permute-start.3 = (bf16[2,256,768]{2,1,0:T(8,128)(2,1)}, bf16[2,256,768]{2,1,0:T(8,128)(2,1)S(1)}, u32[]{:S(2)}, u32[]{:S(2)}) collective-permute-start(bf16[2,256,768]{2,1,0:T(8,128)(2,1)} %pad_maximum_fusion.2), channel_id=1, source_target_pairs={{0,4},{2,6},{4,0},{6,2},{8,12},{10,14},{12,8},{14,10},{16,20},{18,... | collective-permute-start | bytes 2359304 | tf_op jit(solution)/shard_map/far/ppermute | solution.py:263
  12.6 31.8 %collective-permute-start.5 = (bf16[256,1280]{1,0:T(8,128)(2,1)}, bf16[256,1280]{1,0:T(8,128)(2,1)}, u32[]{:S(2)}, u32[]{:S(2)}) collective-permute-start(bf16[256,1280]{1,0:T(8,128)(2,1)} %constant_dynamic-slice_fusion), channel_id=1, source_target_pairs={{0,4},{2,6},{4,0},{6,2},{8,12},{10,14},{12,8},{14,10},{16,20},{18,... | collective-permute-start | bytes 1966088 | tf_op jit(solution)/shard_map/q_far/ppermute | solution.py:263
  19.6 12.8 %collective-permute-start.1 = (bf16[2,64,1280]{2,1,0:T(8,128)(2,1)}, bf16[2,64,1280]{2,1,0:T(8,128)(2,1)}, u32[]{:S(2)}, u32[]{:S(2)}) collective-permute-start(bf16[2,64,1280]{2,1,0:T(8,128)(2,1)} %copy_bitcast_fusion.refs_0_), channel_id=1, source_target_pairs={{0,32},{2,34},{4,36},{6,38},{8,40},{10,42},{12,44},{14,46},{16,48}... | collective-permute-start | bytes 983048 | tf_op jit(solution)/shard_map/text_up/ppermute | solution.py:263
  21.5 10.9 %collective-permute-start.2 = (bf16[2,64,1280]{2,1,0:T(8,128)(2,1)}, bf16[2,64,1280]{2,1,0:T(8,128)(2,1)}, u32[]{:S(2)}, u32[]{:S(2)}) collective-permute-start(bf16[2,64,1280]{2,1,0:T(8,128)(2,1)} %copy_bitcast_fusion.refs_0_), channel_id=1, source_target_pairs={{0,224},{2,226},{4,228},{6,230},{8,232},{10,234},{12,236},{14,238}... | collective-permute-start | bytes 983048 | tf_op jit(solution)/shard_map/text_down/ppermute | solution.py:263
  25.4 19.8 %collective-permute-start.4 = (bf16[2,256,1280]{2,1,0:T(8,128)(2,1)S(1)}, bf16[2,256,1280]{2,1,0:T(8,128)(2,1)S(1)}, u32[]{:S(2)}, u32[]{:S(2)}) collective-permute-start(bf16[2,256,1280]{2,1,0:T(8,128)(2,1)S(1)} %pad_maximum_fusion.refs_0_), channel_id=1, source_target_pairs={{0,248},{2,10},{4,252},{6,14},{8,0},{10,18},{12,4},{14,22},{16,8},... | collective-permute-start | bytes 3932168 | tf_op jit(solution)/shard_map/out_own/ppermute | solution.py:263
  30.6 22.1 %copy-start.19 = (bf16[2,256,512]{2,1,0:T(8,128)(2,1)S(1)}, bf16[2,256,512]{2,1,0:T(8,128)(2,1)}, u32[]{:S(2)}) copy-start(bf16[2,256,512]{2,1,0:T(8,128)(2,1)} %pad_maximum_fusion.3) | copy-start | bytes 1572868
  44.5 32.2 %copy-start.3 = (bf16[2,256,768]{2,1,0:T(8,128)(2,1)}, bf16[2,256,768]{2,1,0:T(8,128)(2,1)S(1)}, u32[]{:S(2)}) copy-start(bf16[2,256,768]{2,1,0:T(8,128)(2,1)S(1)} %collective-permute-done.3.refs_1_.far) | copy-start | bytes 2359300
  45.3 31.4 %copy-start.1 = (bf16[2,256,1280]{2,1,0:T(8,128)(2,1)}, bf16[2,256,1280]{2,1,0:T(8,128)(2,1)S(1)}, u32[]{:S(2)}) copy-start(bf16[2,256,1280]{2,1,0:T(8,128)(2,1)S(1)} %collective-permute-done.4.refs_2_.out_own) | copy-start | bytes 3932164
  45.3 29.5 %collective-permute-start.8 = (bf16[2,256,768]{2,1,0:T(8,128)(2,1)S(1)}, bf16[2,256,768]{2,1,0:T(8,128)(2,1)S(1)}, u32[]{:S(2)}, u32[]{:S(2)}) collective-permute-start(bf16[2,256,768]{2,1,0:T(8,128)(2,1)S(1)} %slice_select_fusion), channel_id=1, source_target_pairs={{0,8},{2,250},{4,12},{6,254},{8,16},{10,2},{12,20},{14,6},{16,24},... | collective-permute-start | bytes 2359304 | tf_op jit(solution)/shard_map/mid/ppermute | solution.py:263
  46.1 28.7 %collective-permute-start.7 = (bf16[2,256,768]{2,1,0:T(8,128)(2,1)S(1)}, bf16[2,256,768]{2,1,0:T(8,128)(2,1)S(1)}, u32[]{:S(2)}, u32[]{:S(2)}) collective-permute-start(bf16[2,256,768]{2,1,0:T(8,128)(2,1)S(1)} %collective-permute-done.3.refs_1_.far), channel_id=1, source_target_pairs={{0,248},{2,10},{4,252},{6,14},{8,0},{10,18},{12,4},{14,22},{16,8},... | collective-permute-start | bytes 2359304 | tf_op jit(solution)/shard_map/out_far/ppermute | solution.py:263
  52.7 22.1 %collective-permute-start.6 = (bf16[2,256,512]{2,1,0:T(8,128)(2,1)S(1)}, bf16[2,256,512]{2,1,0:T(8,128)(2,1)S(1)}, u32[]{:S(2)}, u32[]{:S(2)}) collective-permute-start(bf16[2,256,512]{2,1,0:T(8,128)(2,1)S(1)} %copy-done.19), channel_id=1, source_target_pairs={{0,4},{2,6},{4,0},{6,2},{8,12},{10,14},{12,8},{14,10},{16,20},{18,... | collective-permute-start | bytes 1572872 | tf_op jit(solution)/shard_map/far/ppermute | solution.py:263
  53.3 21.5 %collective-permute-start.10 = (bf16[2,64,1280]{2,1,0:T(8,128)(2,1)}, bf16[2,64,1280]{2,1,0:T(8,128)(2,1)S(1)}, u32[]{:S(2)}, u32[]{:S(2)}) collective-permute-start(bf16[2,64,1280]{2,1,0:T(8,128)(2,1)} %collective-permute-done.2.refs_1_), channel_id=1, source_target_pairs={{0,224},{2,226},{4,228},{6,230},{8,232},{10,234},{12,236},{14,238}... | collective-permute-start | bytes 983048 | tf_op jit(solution)/shard_map/text_down/ppermute | solution.py:263
  55.0 19.8 %collective-permute-start.9 = (bf16[2,64,1280]{2,1,0:T(8,128)(2,1)}, bf16[2,64,1280]{2,1,0:T(8,128)(2,1)S(1)}, u32[]{:S(2)}, u32[]{:S(2)}) collective-permute-start(bf16[2,64,1280]{2,1,0:T(8,128)(2,1)} %collective-permute-done.1.refs_4_), channel_id=1, source_target_pairs={{0,32},{2,34},{4,36},{6,38},{8,40},{10,42},{12,44},{14,46},{16,48}... | collective-permute-start | bytes 983048 | tf_op jit(solution)/shard_map/text_up/ppermute | solution.py:263
  74.8 7.7 %copy-start.9 = (bf16[2,64,1280]{2,1,0:T(8,128)(2,1)}, bf16[2,64,1280]{2,1,0:T(8,128)(2,1)S(1)}, u32[]{:S(2)}) copy-start(bf16[2,64,1280]{2,1,0:T(8,128)(2,1)S(1)} %collective-permute-done.10.refs_2_) | copy-start | bytes 983044
  74.8 26.9 %copy-start.4 = (bf16[2,256,512]{2,1,0:T(8,128)(2,1)}, bf16[2,256,512]{2,1,0:T(8,128)(2,1)S(1)}, u32[]{:S(2)}) copy-start(bf16[2,256,512]{2,1,0:T(8,128)(2,1)S(1)} %collective-permute-done.6.refs_1_.far) | copy-start | bytes 1572868
  76.7 9.0 %collective-permute-start.15 = (bf16[5,2,256,768]{3,2,1,0:T(8,128)(2,1)S(1)}, bf16[5,2,256,768]{3,2,1,0:T(8,128)(2,1)}, u32[]{:S(2)}, u32[]{:S(2)}) collective-permute-start(bf16[5,2,256,768]{3,2,1,0:T(8,128)(2,1)S(1)} %gather_heads.2), channel_id=1, source_target_pairs={{0,2},{2,0},{4,6},{6,4},{8,10},{10,8},{12,14},{14,12},{16,18},{18,... | collective-permute-start | bytes 11796488 | tf_op jit(solution)/shard_map/cc_part/ppermute | solution.py:263
  76.8 24.9 %collective-permute-start.11 = (bf16[2,256,512]{2,1,0:T(8,128)(2,1)S(1)}, bf16[2,256,512]{2,1,0:T(8,128)(2,1)S(1)}, u32[]{:S(2)}, u32[]{:S(2)}) collective-permute-start(bf16[2,256,512]{2,1,0:T(8,128)(2,1)S(1)} %collective-permute-done.6.refs_1_.far), channel_id=1, source_target_pairs={{0,248},{2,10},{4,252},{6,14},{8,0},{10,18},{12,4},{14,22},{16,8},... | collective-permute-start | bytes 1572872 | tf_op jit(solution)/shard_map/out_far/ppermute | solution.py:263
  82.1 19.6 %copy-start.2 = (bf16[2,256,1280]{2,1,0:T(8,128)(2,1)S(1)}, bf16[2,256,1280]{2,1,0:T(8,128)(2,1)}, u32[]{:S(2)}) copy-start(bf16[2,256,1280]{2,1,0:T(8,128)(2,1)} %copy-done.1) | copy-start | bytes 3932164
  82.1 19.6 %collective-permute-start.12 = (bf16[2,256,512]{2,1,0:T(8,128)(2,1)S(1)}, bf16[2,256,512]{2,1,0:T(8,128)(2,1)S(1)}, u32[]{:S(2)}, u32[]{:S(2)}) collective-permute-start(bf16[2,256,512]{2,1,0:T(8,128)(2,1)S(1)} %slice_select_fusion.1), channel_id=1, source_target_pairs={{0,8},{2,250},{4,12},{6,254},{8,16},{10,2},{12,20},{14,6},{16,24},... | collective-permute-start | bytes 1572872 | tf_op jit(solution)/shard_map/mid/ppermute | solution.py:263
  82.2 14.2 %collective-permute-start.13 = (bf16[2,64,1280]{2,1,0:T(8,128)(2,1)S(1)}, bf16[2,64,1280]{2,1,0:T(8,128)(2,1)}, u32[]{:S(2)}, u32[]{:S(2)}) collective-permute-start(bf16[2,64,1280]{2,1,0:T(8,128)(2,1)S(1)} %collective-permute-done.9.refs_5_), channel_id=1, source_target_pairs={{0,32},{2,34},{4,36},{6,38},{8,40},{10,42},{12,44},{14,46},{16,48}... | collective-permute-start | bytes 983048 | tf_op jit(solution)/shard_map/text_up/ppermute | solution.py:263
  82.5 18.5 %collective-permute-start.14 = (bf16[2,64,1280]{2,1,0:T(8,128)(2,1)S(1)}, bf16[2,64,1280]{2,1,0:T(8,128)(2,1)S(1)}, u32[]{:S(2)}, u32[]{:S(2)}) collective-permute-start(bf16[2,64,1280]{2,1,0:T(8,128)(2,1)S(1)} %collective-permute-done.10.refs_2_), channel_id=1, source_target_pairs={{0,224},{2,226},{4,228},{6,230},{8,232},{10,234},{12,236},{14,238}... | collective-permute-start | bytes 983048 | tf_op jit(solution)/shard_map/text_down/ppermute | solution.py:263
  103.0 5.1 %collective-permute-start.17 = (bf16[5,2,256,512]{3,2,1,0:T(8,128)(2,1)S(1)}, bf16[5,2,256,512]{3,2,1,0:T(8,128)(2,1)}, u32[]{:S(2)}, u32[]{:S(2)}) collective-permute-start(bf16[5,2,256,512]{3,2,1,0:T(8,128)(2,1)S(1)} %gather_heads.3), channel_id=1, source_target_pairs={{0,2},{2,0},{4,6},{6,4},{8,10},{10,8},{12,14},{14,12},{16,18},{18,... | collective-permute-start | bytes 7864328 | tf_op jit(solution)/shard_map/cc_part/ppermute | solution.py:263
  105.0 11.2 %copy-start = (bf16[7,2,64,1280]{3,2,1,0:T(8,128)(2,1)}, bf16[7,2,64,1280]{3,2,1,0:T(8,128)(2,1)S(1)}, u32[]{:S(2)}) copy-start(bf16[7,2,64,1280]{3,2,1,0:T(8,128)(2,1)S(1)} %pack.1.near) | copy-start | bytes 6881284
  105.0 12.4 %collective-permute-start.18 = (bf16[7,2,64,1280]{3,2,1,0:T(8,128)(2,1)S(1)}, bf16[7,2,64,1280]{3,2,1,0:T(8,128)(2,1)}, u32[]{:S(2)}, u32[]{:S(2)}) collective-permute-start(bf16[7,2,64,1280]{3,2,1,0:T(8,128)(2,1)S(1)} %pack.1.near), channel_id=1, source_target_pairs={{0,2},{2,0},{4,6},{6,4},{8,10},{10,8},{12,14},{14,12},{16,18},{18,... | collective-permute-start | bytes 6881288 | tf_op jit(solution)/shard_map/cc_text/ppermute | solution.py:263
  105.5 11.9 %collective-permute-start.16 = (bf16[2,64,1280]{2,1,0:T(8,128)(2,1)}, bf16[2,64,1280]{2,1,0:T(8,128)(2,1)S(1)}, u32[]{:S(2)}, u32[]{:S(2)}) collective-permute-start(bf16[2,64,1280]{2,1,0:T(8,128)(2,1)} %collective-permute-done.13.refs_6_), channel_id=1, source_target_pairs={{0,32},{2,34},{4,36},{6,38},{8,40},{10,42},{12,44},{14,46},{16,48}... | collective-permute-start | bytes 983048 | tf_op jit(solution)/shard_map/text_up/ppermute | solution.py:263
  117.4 1.6 %collective-permute-start.19 = (bf16[2,64,1280]{2,1,0:T(8,128)(2,1)S(1)}, bf16[2,64,1280]{2,1,0:T(8,128)(2,1)S(1)}, u32[]{:S(2)}, u32[]{:S(2)}) collective-permute-start(bf16[2,64,1280]{2,1,0:T(8,128)(2,1)S(1)} %collective-permute-done.16.last), channel_id=1, source_target_pairs={{0,2},{2,0},{4,6},{6,4},{8,10},{10,8},{12,14},{14,12},{16,18},{18,... | collective-permute-start | bytes 983048 | tf_op jit(solution)/shard_map/cc_text/ppermute | solution.py:263
  128.7 12.2 %collective-permute-start.20 = (bf16[256,768]{1,0:T(8,128)(2,1)}, bf16[256,768]{1,0:T(8,128)(2,1)S(1)}, u32[]{:S(2)}, u32[]{:S(2)}) collective-permute-start(bf16[256,768]{1,0:T(8,128)(2,1)} %get-tuple-element.73), channel_id=1, source_target_pairs={{0,4},{2,6},{4,0},{6,2},{8,12},{10,14},{12,8},{14,10},{16,20},{18,... | collective-permute-start | bytes 1179656 | tf_op jit(solution)/shard_map/back/ppermute | solution.py:263
  129.2 8.5 %copy-start.20 = (bf16[256,768]{1,0:T(8,128)(2,1)S(1)}, bf16[256,768]{1,0:T(8,128)(2,1)}, u32[]{:S(2)}) copy-start(bf16[256,768]{1,0:T(8,128)(2,1)} %get-tuple-element.71) | copy-start | bytes 1179652
  136.1 9.7 %collective-permute-start.21 = (bf16[256,512]{1,0:T(8,128)(2,1)}, bf16[256,512]{1,0:T(8,128)(2,1)S(1)}, u32[]{:S(2)}, u32[]{:S(2)}) collective-permute-start(bf16[256,512]{1,0:T(8,128)(2,1)} %get-tuple-element.74), channel_id=1, source_target_pairs={{0,4},{2,6},{4,0},{6,2},{8,12},{10,14},{12,8},{14,10},{16,20},{18,... | collective-permute-start | bytes 786440 | tf_op jit(solution)/shard_map/back/ppermute | solution.py:263
  (13 other events, 30.7 us)

commit v3 on v2

--- a/solution.py
+++ b/solution.py
@@ -34,8 +34,8 @@
 CORES = route(lambda r, x, c: (r, x, 1 - c))
 OUTWARD = route(lambda r, x, c: (r + (1 if c else -1), x, c))
 INWARD = route(lambda r, x, c: (r + (-1 if c else 1), x, c))
-ZUP = route(lambda r, x, c: (r + YN, x, c))
-ZDOWN = route(lambda r, x, c: (r - YN, x, c))
+MAJOR = route(lambda r, x, c: (r + (YN if r % YN < 2 else -YN), x, c))
+MINOR = route(lambda r, x, c: (r - (YN if r % YN < 2 else -YN), x, c))
 
 
 def pack_kernel(*refs):
@@ -146,7 +146,8 @@
     q_own, q_far, sums, stats, near, last, cc_near, cc_last, o_own, o_far, keys, values,
 ):
     for core, (most, other) in enumerate(((near, last), (cc_near, cc_last))):
-        for at, plane in enumerate([most.at[i] for i in range(7)] + [other]):
+        planes = [most.at[i] for i in range(6)] + [other.at[i] for i in range(2)]
+        for at, plane in enumerate(planes):
             to = at * BLK + core * 64
             keys[to : to + 64, :] = plane[0]
             values[to : to + 64, :] = plane[1]
@@ -241,7 +242,7 @@
         pl.BlockSpec((TOK, HD), halved(1)),
         pl.BlockSpec((2, TOK, HD), chunk(2)),
         pl.BlockSpec((2, TOK, HD), chunk(2)),
-        *[pl.BlockSpec((7, 2, 64, HD), halved(3)), pl.BlockSpec((2, 64, HD), halved(2))] * 2,
+        *[pl.BlockSpec((n, 2, 64, HD), halved(3)) for n in (6, 2, 6, 2)],
     ]
     out = jax.ShapeDtypeStruct((TOK, heads * HD), jnp.bfloat16)
     out_specs = (pl.BlockSpec((TOK, HD), chunk(1)), pl.BlockSpec((TOK, HD), chunk(1)))
@@ -295,13 +296,12 @@
         position = jnp.argmax(wanted[:, :, None] == offsets[None, None, :], axis=2).astype(jnp.int32)
         valid = (lists >= 0).astype(jnp.int32)
         slots = jnp.where(lists >= 0, position * 2 + lists % 2, 0)
-        ahead = (2 * segments[:, None] + jnp.arange(2)[None, :] - z) % ZN
-        order = (0, 1, 2, 3, 7, 6, 5, 4)
-        text_at = sum(jnp.where(ahead == k, at, 0) for k, at in enumerate(order))
+        ahead = 2 * segments[:, None] + jnp.arange(2)[None, :] - z
+        text_at = jnp.where(row % YN < 2, -ahead, ahead) % ZN
         return (x[None].astype(jnp.int32), slots, valid, text_at.astype(jnp.int32))
 
     firsts = [sum(CHUNKS[:i]) for i in range(len(CHUNKS))]
-    gives = [pair_of(1 - x, f, h) for f, h in zip(firsts, CHUNKS)]
+    give1 = pair_of(1 - x, firsts[0], CHUNKS[0])
     kv_own = pair_of(x)
 
     own_table = jnp.concatenate(
@@ -314,14 +314,18 @@
         spread.reshape(YN * XN, *halves.shape[1:]), "seq", 0, 0, axis_index_groups=PLANES
     )
     plane = jnp.swapaxes(plane, 0, 1).reshape(2, 64, width)
-    far1 = send("far", gives[0], ACROSS)
-    kv_own, plane, far_table = lax.optimization_barrier((kv_own, plane, far_table))
+    far1 = send("far", give1, ACROSS)
+    kv_own, plane, far_table, queries, latent_keys, latent_values = lax.optimization_barrier(
+        (kv_own, plane, far_table, queries, latent_keys, latent_values)
+    )
     scalars = whereabouts(own_table, far_table)
     out_own = send("out_own", kv_own, OUTWARD)
-    q_far = send("q_far", half_of(queries, 1 - x), ACROSS)
-    up1, down1 = send("text_up", plane, ZUP), send("text_down", plane, ZDOWN)
-    give2, up1, down1, far1, out_own, kv_own, q_far, *scalars = lax.optimization_barrier(
-        (gives[1], up1, down1, far1, out_own, kv_own, q_far, *scalars)
+    hop1 = send("text_z", plane, MAJOR)
+    give2, q_give, hop1, far1, out_own, kv_own, *scalars = lax.optimization_barrier(
+        (
+            pair_of(1 - x, firsts[1], CHUNKS[1]), half_of(queries, 1 - x),
+            hop1, far1, out_own, kv_own, *scalars,
+        )
     )
 
     def between(first, heads, far):
@@ -338,26 +342,32 @@
         )
 
     far2 = send("far", give2, ACROSS)
+    q_far = send("q_far", q_give, ACROSS)
     out_far1 = send("out_far", far1, OUTWARD)
     mid1 = send("mid", between(firsts[0], CHUNKS[0], far1), INWARD)
-    up2, down2 = send("text_up", up1, ZUP), send("text_down", down1, ZDOWN)
-    far2, out_far1, mid1, up2, down2 = lax.optimization_barrier((far2, out_far1, mid1, up2, down2))
+    hop2 = send("text_z", hop1, MAJOR)
+    hop3 = send("text_z", hop2, MAJOR)
+    far2, q_far, out_far1, mid1, hop3 = lax.optimization_barrier(
+        (far2, q_far, out_far1, mid1, hop3)
+    )
 
     out_far2 = send("out_far", far2, OUTWARD)
     mid2 = send("mid", between(firsts[1], CHUNKS[1], far2), INWARD)
-    up3, down3 = send("text_up", up2, ZUP), send("text_down", down2, ZDOWN)
+    hop4 = send("text_z", hop3, MAJOR)
+    hop5 = send("text_z", hop4, MAJOR)
     sums1 = attended(0, far1, out_far1, mid1, swapped(0, far1, out_far1, mid1))
-    out_far2, mid2, up3, down3, *sums1 = lax.optimization_barrier(
-        (out_far2, mid2, up3, down3, *sums1)
-    )
-
-    up4 = send("text_up", up3, ZUP)
-    near = pack(plane, down1, down2, down3, up1, up2, up3)
+    out_far2, mid2, hop5, plane, *sums1 = lax.optimization_barrier(
+        (out_far2, mid2, hop5, plane, *sums1)
+    )
+
+    hop6, other = send("text_z", hop5, MAJOR), send("text_z", plane, MINOR)
+    near = pack(plane, hop1, hop2, hop3, hop4, hop5)
     cc_near = send("cc_text", near, CORES)
     sums2 = attended(1, far2, out_far2, mid2, swapped(1, far2, out_far2, mid2))
-    up4, _, _ = lax.optimization_barrier((up4, *sums2))
-    cc_last = send("cc_text", up4, CORES)
-    text = (near, up4, cc_near, cc_last)
+    hop6, other, _, _ = lax.optimization_barrier((hop6, other, *sums2))
+    last = pack(hop6, other)
+    cc_last = send("cc_text", last, CORES)
+    text = (near, last, cc_near, cc_last)
     results = []
     for first, heads, sums in zip(firsts, CHUNKS, (sums1, sums2)):
         mine, theirs = finish(first, heads, scalars, queries, q_far, *sums, *text)

time: 149 us -> 140 us (0.940)
  starting transfers between devices: 40.8 us -> 34.1 us
    ppermute x22, starting transfers between devices: 35.7 us -> 29 us  [send(): return lax.ppermute(block, 'seq', to)]
    ppermute x22, waiting for transfers between devices: 49.4 us -> 47.2 us  [send(): return lax.ppermute(block, 'seq', to)]
    all_to_all x1, waiting for transfers between devices: 0.01 us -> 1.77 us  [on_device(): lax.all_to_all(spread.reshape(YN * XN, *halves.shape[1:]), 'seq', 0, 0, a...]
    another operation x3 -> x4, local copies, waits for them, and re-layouts: 3.31 us -> 4.16 us  [pair_of(): jnp.stack([half_of(a, which, first, heads) for a in (latent_keys, latent_...]
  transfers between devices with their start and end apart: 23 -> 23, of which waited for: 9 -> 11; matrix products, arithmetic and copies ran while one was open for 8% -> 7% of each run, Pallas kernels for 19% -> 19%
where the time goes in v3:
time: 140 us; the launch traced here: 138 us
  waiting for transfers between devices  49 us (35%)
  Pallas kernels  38.9 us (28%)
  starting transfers between devices  34.1 us (24%)
  local copies, waits for them, and re-layouts  10.1 us (7%)
  other arithmetic  5.21 us (4%)
    ppermute x22, waiting for transfers between devices, send(): return lax.ppermute(block, 'seq', to)  47.2 us
    pallas_call x4, Pallas kernels, call(): pl.pallas_call(kernel, out_shape=out_shape, grid_spec=pltpu.PrefetchScala...  34.5 us
    ppermute x22, starting transfers between devices, send(): return lax.ppermute(block, 'seq', to)  29 us
    all_to_all x1, starting transfers between devices, on_device(): lax.all_to_all(spread.reshape(YN * XN, *halves.shape[1:]), 'seq', 0, 0, a...  5.1 us
    another operation x4, local copies, waits for them, and re-layouts, pair_of(): jnp.stack([half_of(a, which, first, heads) for a in (latent_keys, latent_...  4.16 us
    pallas_call x2, Pallas kernels, gather_heads(): pl.pallas_call(gather_kernel, out_shape=jax.ShapeDtypeStruct((len(pairs),...  2.98 us
  transfers between devices with their start and end apart: 23, of which 11 were waited for; matrix products, arithmetic and copies ran while one was open for 7% of the time, Pallas kernels for 19%

profile of v3, /device:TPU:4, one launch (start us, length us, event | category | flops | bytes accessed | tf_op | source)
XLA Modules:
  0.0 138.4 jit_solution(10508266101243275819)
XLA Ops:
  1.7 5.1 %all-to-all-start = ((bf16[8,2,8,1280]{3,2,1,0:T(8,128)(2,1)}), bf16[8,2,8,1280]{3,2,1,0:T(8,128)(2,1)}, u32[]{:S(2)}, u32[]{:S(2)}) async-start(bf16[8,2,8,1280]{3,2,1,0:T(8,128)(2,1)} %bitcast.4), calls=%async_computation | async-start | bytes 655360 | tf_op jit(solution)/shard_map/all_to_all | solution.py:313
  7.5 2.1 %collective-permute-start = (s32[2,16]{1,0:T(2,128)S(1)}, s32[2,16]{1,0:T(2,128)S(1)}, u32[]{:S(2)}, u32[]{:S(2)}) collective-permute-start(s32[2,16]{1,0:T(2,128)S(1)} %concatenate.15), channel_id=1, source_target_pairs={{0,4},{2,6},{4,0},{6,2},{8,12},{10,14},{12,8},{14,10},{16,20},{18,... | collective-permute-start | bytes 392 | tf_op jit(solution)/shard_map/table/ppermute | solution.py:264
  9.6 1.0 dynamic-slice_bitcast_fusion.2
  11.6 1.2 dynamic-slice_bitcast_fusion
  13.1 1.8 %all-to-all-done = bf16[8,2,8,1280]{3,2,1,0:T(8,128)(2,1)} async-done(((bf16[8,2,8,1280]{3,2,1,0:T(8,128)(2,1)}), bf16[8,2,8,1280]{3,2,1,0:T(8,128)(2,1)}, u32[]{:S(2)}, u32[]{:S(2)}) %all-to-all-start) | async-done | bytes 327712 | tf_op jit(solution)/shard_map/all_to_all | solution.py:313
  14.9 1.0 copy_bitcast_fusion.refs_0_
  16.6 6.7 %collective-permute-start.3 = (bf16[2,256,1280]{2,1,0:T(8,128)(2,1)S(1)}, bf16[2,256,1280]{2,1,0:T(8,128)(2,1)S(1)}, u32[]{:S(2)}, u32[]{:S(2)}) collective-permute-start(bf16[2,256,1280]{2,1,0:T(8,128)(2,1)S(1)} %pad_maximum_fusion.refs_0_), channel_id=1, source_target_pairs={{0,248},{2,10},{4,252},{6,14},{8,0},{10,18},{12,4},{14,22},{16,8},... | collective-permute-start | bytes 3932168 | tf_op jit(solution)/shard_map/out_own/ppermute | solution.py:264
  23.3 1.0 dynamic-slice_bitcast_fusion.5
  24.3 1.0 dynamic-slice_bitcast_fusion.4
  27.6 6.2 %collective-permute-done.1.refs_1_ = bf16[2,64,1280]{2,1,0:T(8,128)(2,1)S(1)} collective-permute-done((bf16[2,64,1280]{2,1,0:T(8,128)(2,1)S(1)}, bf16[2,64,1280]{2,1,0:T(8,128)(2,1)S(1)}, u32[]{:S(2)}, u32[]{:S(2)}) %collective-permute-start.1) | collective-permute-done | bytes 327712 | tf_op jit(solution)/shard_map/text_z/ppermute | solution.py:264
  33.7 4.7 %collective-permute-done.3.refs_2_.out_own = bf16[2,256,1280]{2,1,0:T(8,128)(2,1)S(1)} collective-permute-done((bf16[2,256,1280]{2,1,0:T(8,128)(2,1)S(1)}, bf16[2,256,1280]{2,1,0:T(8,128)(2,1)S(1)}, u32[]{:S(2)}, u32[]{:S(2)}) %collective-permute-start.3) | collective-permute-done | bytes 1310752 | tf_op jit(solution)/shard_map/out_own/ppermute | solution.py:264
  38.6 5.9 %collective-permute-start.6 = (bf16[2,256,768]{2,1,0:T(8,128)(2,1)S(1)}, bf16[2,256,768]{2,1,0:T(8,128)(2,1)S(1)}, u32[]{:S(2)}, u32[]{:S(2)}) collective-permute-start(bf16[2,256,768]{2,1,0:T(8,128)(2,1)S(1)} %collective-permute-done.2.refs_1_.far), channel_id=1, source_target_pairs={{0,248},{2,10},{4,252},{6,14},{8,0},{10,18},{12,4},{14,22},{16,8},... | collective-permute-start | bytes 2359304 | tf_op jit(solution)/shard_map/out_far/ppermute | solution.py:264
  44.5 1.5 %collective-permute-start.5 = (bf16[256,1280]{1,0:T(8,128)(2,1)S(1)}, bf16[256,1280]{1,0:T(8,128)(2,1)S(1)}, u32[]{:S(2)}, u32[]{:S(2)}) collective-permute-start(bf16[256,1280]{1,0:T(8,128)(2,1)S(1)} %constant_dynamic-slice_fusion), channel_id=1, source_target_pairs={{0,4},{2,6},{4,0},{6,2},{8,12},{10,14},{12,8},{14,10},{16,20},{18,... | collective-permute-start | bytes 1966088 | tf_op jit(solution)/shard_map/q_far/ppermute | solution.py:264
  46.5 9.4 %collective-permute-done.8.refs_2_ = bf16[2,64,1280]{2,1,0:T(8,128)(2,1)S(1)} collective-permute-done((bf16[2,64,1280]{2,1,0:T(8,128)(2,1)S(1)}, bf16[2,64,1280]{2,1,0:T(8,128)(2,1)S(1)}, u32[]{:S(2)}, u32[]{:S(2)}) %collective-permute-start.8) | collective-permute-done | bytes 327712 | tf_op jit(solution)/shard_map/text_z/ppermute | solution.py:264
  55.9 10.6 %collective-permute-done.4.refs_1_.far = bf16[2,256,512]{2,1,0:T(8,128)(2,1)S(1)} collective-permute-done((bf16[2,256,512]{2,1,0:T(8,128)(2,1)S(1)}, bf16[2,256,512]{2,1,0:T(8,128)(2,1)S(1)}, u32[]{:S(2)}, u32[]{:S(2)}) %collective-permute-start.4) | collective-permute-done | bytes 524320 | tf_op jit(solution)/shard_map/far/ppermute | solution.py:264
  67.4 1.8 %gather_heads.2 = bf16[5,2,256,768]{3,2,1,0:T(8,128)(2,1)S(1)} custom-call(bf16[2,256,1280]{2,1,0:T(8,128)(2,1)S(1)} %pad_maximum_fusion.refs_0_, bf16[2,256,768]{2,1,0:T(8,128)(2,1)S(1)} %collective-permute-done.2.refs_1_.far, bf16[2,256,1280]{2,1,0:T(8,128)(2,1)S(1)} %collective-permute-done.3.refs_2_.out_own, ...), custom_call_target="tpu_custom_call" | custom-call | tf_op jit(solution)/shard_map/gather_heads/pallas_call | solution.py:77
  69.8 5.5 %collective-permute-start.10 = (bf16[2,256,512]{2,1,0:T(8,128)(2,1)S(1)}, bf16[2,256,512]{2,1,0:T(8,128)(2,1)S(1)}, u32[]{:S(2)}, u32[]{:S(2)}) collective-permute-start(bf16[2,256,512]{2,1,0:T(8,128)(2,1)S(1)} %collective-permute-done.4.refs_1_.far), channel_id=1, source_target_pairs={{0,248},{2,10},{4,252},{6,14},{8,0},{10,18},{12,4},{14,22},{16,8},... | collective-permute-start | bytes 1572872 | tf_op jit(solution)/shard_map/out_far/ppermute | solution.py:264
  75.4 5.3 %collective-permute-done.12.refs_4_ = bf16[2,64,1280]{2,1,0:T(8,128)(2,1)S(1)} collective-permute-done((bf16[2,64,1280]{2,1,0:T(8,128)(2,1)S(1)}, bf16[2,64,1280]{2,1,0:T(8,128)(2,1)S(1)}, u32[]{:S(2)}, u32[]{:S(2)}) %collective-permute-start.12) | collective-permute-done | bytes 327712 | tf_op jit(solution)/shard_map/text_z/ppermute | solution.py:264
  80.7 10.7 %latent.2 = (f32[2,256,768]{2,1,0:T(8,128)}, f32[2,256,768]{2,1,0:T(8,128)}) custom-call(s32[1]{0:T(128)} %bitcast.12.half_ref, s32[4,8]{1,0:T(4,128)} %fusion.2.slots_ref, s32[4,8]{1,0:T(4,128)} %get-tuple-element.52.valid_ref, s32[2,2]{1,0:T(2,128)} %and_select_fusion.text_at_ref, bf16[256,2560]{1,0:T(8,128)(2,1)} %q_own.3, bf16[256,1280]{1,0:T(8,128)(2,1)} %copy-done.19, ...), custom_call_target="tpu_custom_call" | custom-call | flops 9663676416 | bytes 12288000 | tf_op jit(solution)/shard_map/latent/pallas_call | solution.py:196
  91.6 1.2 gather_heads.3
  93.1 1.3 pack.2.near
  94.9 2.9 %collective-permute-start.15 = (bf16[2,64,1280]{2,1,0:T(8,128)(2,1)}, bf16[2,64,1280]{2,1,0:T(8,128)(2,1)S(1)}, u32[]{:S(2)}, u32[]{:S(2)}) collective-permute-start(bf16[2,64,1280]{2,1,0:T(8,128)(2,1)} %collective-permute-done.13.refs_5_), channel_id=1, source_target_pairs={{0,32},{2,34},{4,36},{6,38},{8,40},{10,42},{12,44},{14,46},{16,240... | collective-permute-start | bytes 983048 | tf_op jit(solution)/shard_map/text_z/ppermute | solution.py:264
  98.1 8.0 %latent.3 = (f32[2,256,512]{2,1,0:T(8,128)}, f32[2,256,512]{2,1,0:T(8,128)}) custom-call(s32[1]{0:T(128)} %bitcast.12.half_ref, s32[4,8]{1,0:T(4,128)} %fusion.2.slots_ref, s32[4,8]{1,0:T(4,128)} %get-tuple-element.52.valid_ref, s32[2,2]{1,0:T(2,128)} %and_select_fusion.text_at_ref, bf16[256,2560]{1,0:T(8,128)(2,1)} %q_own.3, bf16[256,1280]{1,0:T(8,128)(2,1)} %copy-done.19, ...), custom_call_target="tpu_custom_call" | custom-call | flops 6442450944 | bytes 8192000 | tf_op jit(solution)/shard_map/latent/pallas_call | solution.py:196
  106.4 1.7 %collective-permute-done.16.refs_1_ = bf16[2,64,1280]{2,1,0:T(8,128)(2,1)S(1)} collective-permute-done((bf16[2,64,1280]{2,1,0:T(8,128)(2,1)S(1)}, bf16[2,64,1280]{2,1,0:T(8,128)(2,1)S(1)}, u32[]{:S(2)}, u32[]{:S(2)}) %collective-permute-start.16) | collective-permute-done | bytes 327712 | tf_op jit(solution)/shard_map/text_z/ppermute | solution.py:264
  108.2 2.1 %collective-permute-done.19.cc_last = bf16[2,2,64,1280]{3,2,1,0:T(8,128)(2,1)S(1)} collective-permute-done((bf16[2,2,64,1280]{3,2,1,0:T(8,128)(2,1)S(1)}, bf16[2,2,64,1280]{3,2,1,0:T(8,128)(2,1)S(1)}, u32[]{:S(2)}, u32[]{:S(2)}) %collective-permute-start.19) | collective-permute-done | bytes 655392 | tf_op jit(solution)/shard_map/cc_text/ppermute | solution.py:264
  111.2 8.9 %finish.2 = (bf16[256,768]{1,0:T(8,128)(2,1)}, bf16[256,768]{1,0:T(8,128)(2,1)}) custom-call(s32[1]{0:T(128)} %bitcast.12.half_ref, s32[4,8]{1,0:T(4,128)} %fusion.2.slots_ref, s32[4,8]{1,0:T(4,128)} %get-tuple-element.52.valid_ref, s32[2,2]{1,0:T(2,128)} %and_select_fusion.text_at_ref, bf16[256,2560]{1,0:T(8,128)(2,1)} %q_own.3, ...), custom_call_target="tpu_custom_call" | custom-call | flops 2415919104 | bytes 3072000 | tf_op jit(solution)/shard_map/finish/pallas_call | solution.py:196
  121.0 6.9 %finish.3 = (bf16[256,512]{1,0:T(8,128)(2,1)}, bf16[256,512]{1,0:T(8,128)(2,1)}) custom-call(s32[1]{0:T(128)} %bitcast.12.half_ref, s32[4,8]{1,0:T(4,128)} %fusion.2.slots_ref, s32[4,8]{1,0:T(4,128)} %get-tuple-element.52.valid_ref, s32[2,2]{1,0:T(2,128)} %and_select_fusion.text_at_ref, bf16[256,2560]{1,0:T(8,128)(2,1)} %q_own.3, ...), custom_call_target="tpu_custom_call" | custom-call | flops 1610612736 | bytes 2048000 | tf_op jit(solution)/shard_map/finish/pallas_call | solution.py:196
  127.8 1.2 collective-permute-start.21
  129.1 1.0 constant_dynamic-update-slice_fusion
  130.1 2.2 %collective-permute-done.20 = bf16[256,768]{1,0:T(8,128)(2,1)S(1)} collective-permute-done((bf16[256,768]{1,0:T(8,128)(2,1)}, bf16[256,768]{1,0:T(8,128)(2,1)S(1)}, u32[]{:S(2)}, u32[]{:S(2)}) %collective-permute-start.20) | collective-permute-done | bytes 393248 | tf_op jit(solution)/shard_map/back/ppermute | solution.py:264
  132.3 4.8 %collective-permute-done.21 = bf16[256,512]{1,0:T(8,128)(2,1)S(1)} collective-permute-done((bf16[256,512]{1,0:T(8,128)(2,1)}, bf16[256,512]{1,0:T(8,128)(2,1)S(1)}, u32[]{:S(2)}, u32[]{:S(2)}) %collective-permute-start.21) | collective-permute-done | bytes 262176 | tf_op jit(solution)/shard_map/back/ppermute | solution.py:264
  137.3 1.1 pad_maximum_fusion.1
  (100 shorter events, 11.5 us)
Async XLA Ops:
  1.7 13.2 %all-to-all-start = ((bf16[8,2,8,1280]{3,2,1,0:T(8,128)(2,1)}), bf16[8,2,8,1280]{3,2,1,0:T(8,128)(2,1)}, u32[]{:S(2)}, u32[]{:S(2)}) async-start(bf16[8,2,8,1280]{3,2,1,0:T(8,128)(2,1)} %bitcast.4), calls=%async_computation | async-start | bytes 655360 | tf_op jit(solution)/shard_map/all_to_all | solution.py:313
  7.5 8.4 %collective-permute-start = (s32[2,16]{1,0:T(2,128)S(1)}, s32[2,16]{1,0:T(2,128)S(1)}, u32[]{:S(2)}, u32[]{:S(2)}) collective-permute-start(s32[2,16]{1,0:T(2,128)S(1)} %concatenate.15), channel_id=1, source_target_pairs={{0,4},{2,6},{4,0},{6,2},{8,12},{10,14},{12,8},{14,10},{16,20},{18,... | collective-permute-start | bytes 392 | tf_op jit(solution)/shard_map/table/ppermute | solution.py:264
  11.6 22.2 %collective-permute-start.2 = (bf16[2,256,768]{2,1,0:T(8,128)(2,1)}, bf16[2,256,768]{2,1,0:T(8,128)(2,1)S(1)}, u32[]{:S(2)}, u32[]{:S(2)}) collective-permute-start(bf16[2,256,768]{2,1,0:T(8,128)(2,1)} %pad_maximum_fusion.2), channel_id=1, source_target_pairs={{0,4},{2,6},{4,0},{6,2},{8,12},{10,14},{12,8},{14,10},{16,20},{18,... | collective-permute-start | bytes 2359304 | tf_op jit(solution)/shard_map/far/ppermute | solution.py:264
  16.6 10.9 %copy-start.18 = (bf16[256,2560]{1,0:T(8,128)(2,1)S(1)}, bf16[256,2560]{1,0:T(8,128)(2,1)}, u32[]{:S(2)}) copy-start(bf16[256,2560]{1,0:T(8,128)(2,1)} %q_own.3) | copy-start | bytes 3932164
  16.6 21.8 %collective-permute-start.3 = (bf16[2,256,1280]{2,1,0:T(8,128)(2,1)S(1)}, bf16[2,256,1280]{2,1,0:T(8,128)(2,1)S(1)}, u32[]{:S(2)}, u32[]{:S(2)}) collective-permute-start(bf16[2,256,1280]{2,1,0:T(8,128)(2,1)S(1)} %pad_maximum_fusion.refs_0_), channel_id=1, source_target_pairs={{0,248},{2,10},{4,252},{6,14},{8,0},{10,18},{12,4},{14,22},{16,8},... | collective-permute-start | bytes 3932168 | tf_op jit(solution)/shard_map/out_own/ppermute | solution.py:264
  25.4 8.4 %collective-permute-start.1 = (bf16[2,64,1280]{2,1,0:T(8,128)(2,1)S(1)}, bf16[2,64,1280]{2,1,0:T(8,128)(2,1)S(1)}, u32[]{:S(2)}, u32[]{:S(2)}) collective-permute-start(bf16[2,64,1280]{2,1,0:T(8,128)(2,1)S(1)} %copy_bitcast_fusion.refs_0_), channel_id=1, source_target_pairs={{0,32},{2,34},{4,36},{6,38},{8,40},{10,42},{12,44},{14,46},{16,240... | collective-permute-start | bytes 983048 | tf_op jit(solution)/shard_map/text_z/ppermute | solution.py:264
  33.7 35.5 %copy-start.10 = (bf16[2,64,1280]{2,1,0:T(8,128)(2,1)}, bf16[2,64,1280]{2,1,0:T(8,128)(2,1)S(1)}, u32[]{:S(2)}) copy-start(bf16[2,64,1280]{2,1,0:T(8,128)(2,1)S(1)} %collective-permute-done.1.refs_1_) | copy-start | bytes 983044
  33.7 35.5 %copy-start.4 = (bf16[2,256,768]{2,1,0:T(8,128)(2,1)}, bf16[2,256,768]{2,1,0:T(8,128)(2,1)S(1)}, u32[]{:S(2)}) copy-start(bf16[2,256,768]{2,1,0:T(8,128)(2,1)S(1)} %collective-permute-done.2.refs_1_.far) | copy-start | bytes 2359300
  38.4 30.8 %copy-start.2 = (bf16[2,256,1280]{2,1,0:T(8,128)(2,1)}, bf16[2,256,1280]{2,1,0:T(8,128)(2,1)S(1)}, u32[]{:S(2)}) copy-start(bf16[2,256,1280]{2,1,0:T(8,128)(2,1)S(1)} %collective-permute-done.3.refs_2_.out_own) | copy-start | bytes 3932164
  38.5 28.0 %collective-permute-start.7 = (bf16[2,256,768]{2,1,0:T(8,128)(2,1)S(1)}, bf16[2,256,768]{2,1,0:T(8,128)(2,1)S(1)}, u32[]{:S(2)}, u32[]{:S(2)}) collective-permute-start(bf16[2,256,768]{2,1,0:T(8,128)(2,1)S(1)} %slice_select_fusion), channel_id=1, source_target_pairs={{0,8},{2,250},{4,12},{6,254},{8,16},{10,2},{12,20},{14,6},{16,24},... | collective-permute-start | bytes 2359304 | tf_op jit(solution)/shard_map/mid/ppermute | solution.py:264
  38.6 28.8 %collective-permute-start.6 = (bf16[2,256,768]{2,1,0:T(8,128)(2,1)S(1)}, bf16[2,256,768]{2,1,0:T(8,128)(2,1)S(1)}, u32[]{:S(2)}, u32[]{:S(2)}) collective-permute-start(bf16[2,256,768]{2,1,0:T(8,128)(2,1)S(1)} %collective-permute-done.2.refs_1_.far), channel_id=1, source_target_pairs={{0,248},{2,10},{4,252},{6,14},{8,0},{10,18},{12,4},{14,22},{16,8},... | collective-permute-start | bytes 2359304 | tf_op jit(solution)/shard_map/out_far/ppermute | solution.py:264
  44.5 11.5 %collective-permute-start.8 = (bf16[2,64,1280]{2,1,0:T(8,128)(2,1)S(1)}, bf16[2,64,1280]{2,1,0:T(8,128)(2,1)S(1)}, u32[]{:S(2)}, u32[]{:S(2)}) collective-permute-start(bf16[2,64,1280]{2,1,0:T(8,128)(2,1)S(1)} %collective-permute-done.1.refs_1_), channel_id=1, source_target_pairs={{0,32},{2,34},{4,36},{6,38},{8,40},{10,42},{12,44},{14,46},{16,240... | collective-permute-start | bytes 983048 | tf_op jit(solution)/shard_map/text_z/ppermute | solution.py:264
  44.5 22.1 %collective-permute-start.5 = (bf16[256,1280]{1,0:T(8,128)(2,1)S(1)}, bf16[256,1280]{1,0:T(8,128)(2,1)S(1)}, u32[]{:S(2)}, u32[]{:S(2)}) collective-permute-start(bf16[256,1280]{1,0:T(8,128)(2,1)S(1)} %constant_dynamic-slice_fusion), channel_id=1, source_target_pairs={{0,4},{2,6},{4,0},{6,2},{8,12},{10,14},{12,8},{14,10},{16,20},{18,... | collective-permute-start | bytes 1966088 | tf_op jit(solution)/shard_map/q_far/ppermute | solution.py:264
  46.0 20.6 %collective-permute-start.4 = (bf16[2,256,512]{2,1,0:T(8,128)(2,1)S(1)}, bf16[2,256,512]{2,1,0:T(8,128)(2,1)S(1)}, u32[]{:S(2)}, u32[]{:S(2)}) collective-permute-start(bf16[2,256,512]{2,1,0:T(8,128)(2,1)S(1)} %pad_maximum_fusion.3), channel_id=1, source_target_pairs={{0,4},{2,6},{4,0},{6,2},{8,12},{10,14},{12,8},{14,10},{16,20},{18,... | collective-permute-start | bytes 1572872 | tf_op jit(solution)/shard_map/far/ppermute | solution.py:264
  55.9 13.3 %copy-start.12 = (bf16[2,64,1280]{2,1,0:T(8,128)(2,1)}, bf16[2,64,1280]{2,1,0:T(8,128)(2,1)S(1)}, u32[]{:S(2)}) copy-start(bf16[2,64,1280]{2,1,0:T(8,128)(2,1)S(1)} %collective-permute-done.8.refs_2_) | copy-start | bytes 983044
  55.9 10.6 %collective-permute-start.9 = (bf16[2,64,1280]{2,1,0:T(8,128)(2,1)S(1)}, bf16[2,64,1280]{2,1,0:T(8,128)(2,1)S(1)}, u32[]{:S(2)}, u32[]{:S(2)}) collective-permute-start(bf16[2,64,1280]{2,1,0:T(8,128)(2,1)S(1)} %collective-permute-done.8.refs_2_), channel_id=1, source_target_pairs={{0,32},{2,34},{4,36},{6,38},{8,40},{10,42},{12,44},{14,46},{16,240... | collective-permute-start | bytes 983048 | tf_op jit(solution)/shard_map/text_z/ppermute | solution.py:264
  66.5 25.0 %copy-start.5 = (bf16[2,256,512]{2,1,0:T(8,128)(2,1)}, bf16[2,256,512]{2,1,0:T(8,128)(2,1)S(1)}, u32[]{:S(2)}) copy-start(bf16[2,256,512]{2,1,0:T(8,128)(2,1)S(1)} %collective-permute-done.4.refs_1_.far) | copy-start | bytes 1572868
  69.3 11.5 %collective-permute-start.14 = (bf16[5,2,256,768]{3,2,1,0:T(8,128)(2,1)S(1)}, bf16[5,2,256,768]{3,2,1,0:T(8,128)(2,1)}, u32[]{:S(2)}, u32[]{:S(2)}) collective-permute-start(bf16[5,2,256,768]{3,2,1,0:T(8,128)(2,1)S(1)} %gather_heads.2), channel_id=1, source_target_pairs={{0,2},{2,0},{4,6},{6,4},{8,10},{10,8},{12,14},{14,12},{16,18},{18,... | collective-permute-start | bytes 11796488 | tf_op jit(solution)/shard_map/cc_part/ppermute | solution.py:264
  69.4 11.3 %collective-permute-start.12 = (bf16[2,64,1280]{2,1,0:T(8,128)(2,1)S(1)}, bf16[2,64,1280]{2,1,0:T(8,128)(2,1)S(1)}, u32[]{:S(2)}, u32[]{:S(2)}) collective-permute-start(bf16[2,64,1280]{2,1,0:T(8,128)(2,1)S(1)} %collective-permute-done.9.refs_3_), channel_id=1, source_target_pairs={{0,32},{2,34},{4,36},{6,38},{8,40},{10,42},{12,44},{14,46},{16,240... | collective-permute-start | bytes 983048 | tf_op jit(solution)/shard_map/text_z/ppermute | solution.py:264
  69.8 21.7 %collective-permute-start.10 = (bf16[2,256,512]{2,1,0:T(8,128)(2,1)S(1)}, bf16[2,256,512]{2,1,0:T(8,128)(2,1)S(1)}, u32[]{:S(2)}, u32[]{:S(2)}) collective-permute-start(bf16[2,256,512]{2,1,0:T(8,128)(2,1)S(1)} %collective-permute-done.4.refs_1_.far), channel_id=1, source_target_pairs={{0,248},{2,10},{4,252},{6,14},{8,0},{10,18},{12,4},{14,22},{16,8},... | collective-permute-start | bytes 1572872 | tf_op jit(solution)/shard_map/out_far/ppermute | solution.py:264
  75.3 16.2 %copy-start.3 = (bf16[2,256,1280]{2,1,0:T(8,128)(2,1)S(1)}, bf16[2,256,1280]{2,1,0:T(8,128)(2,1)}, u32[]{:S(2)}) copy-start(bf16[2,256,1280]{2,1,0:T(8,128)(2,1)} %copy-done.2) | copy-start | bytes 3932164
  75.4 16.1 %collective-permute-start.11 = (bf16[2,256,512]{2,1,0:T(8,128)(2,1)S(1)}, bf16[2,256,512]{2,1,0:T(8,128)(2,1)S(1)}, u32[]{:S(2)}, u32[]{:S(2)}) collective-permute-start(bf16[2,256,512]{2,1,0:T(8,128)(2,1)S(1)} %slice_select_fusion.1), channel_id=1, source_target_pairs={{0,8},{2,250},{4,12},{6,254},{8,16},{10,2},{12,20},{14,6},{16,24},... | collective-permute-start | bytes 1572872 | tf_op jit(solution)/shard_map/mid/ppermute | solution.py:264
  80.7 10.7 %copy-start.16 = (bf16[2,64,1280]{2,1,0:T(8,128)(2,1)}, bf16[2,64,1280]{2,1,0:T(8,128)(2,1)S(1)}, u32[]{:S(2)}) copy-start(bf16[2,64,1280]{2,1,0:T(8,128)(2,1)S(1)} %collective-permute-done.12.refs_4_) | copy-start | bytes 983044
  80.7 10.8 %collective-permute-start.13 = (bf16[2,64,1280]{2,1,0:T(8,128)(2,1)S(1)}, bf16[2,64,1280]{2,1,0:T(8,128)(2,1)}, u32[]{:S(2)}, u32[]{:S(2)}) collective-permute-start(bf16[2,64,1280]{2,1,0:T(8,128)(2,1)S(1)} %collective-permute-done.12.refs_4_), channel_id=1, source_target_pairs={{0,32},{2,34},{4,36},{6,38},{8,40},{10,42},{12,44},{14,46},{16,240... | collective-permute-start | bytes 983048 | tf_op jit(solution)/shard_map/text_z/ppermute | solution.py:264
  92.8 5.3 %collective-permute-start.17 = (bf16[5,2,256,512]{3,2,1,0:T(8,128)(2,1)S(1)}, bf16[5,2,256,512]{3,2,1,0:T(8,128)(2,1)}, u32[]{:S(2)}, u32[]{:S(2)}) collective-permute-start(bf16[5,2,256,512]{3,2,1,0:T(8,128)(2,1)S(1)} %gather_heads.3), channel_id=1, source_target_pairs={{0,2},{2,0},{4,6},{6,4},{8,10},{10,8},{12,14},{14,12},{16,18},{18,... | collective-permute-start | bytes 7864328 | tf_op jit(solution)/shard_map/cc_part/ppermute | solution.py:264
  94.5 11.7 %copy-start = (bf16[6,2,64,1280]{3,2,1,0:T(8,128)(2,1)}, bf16[6,2,64,1280]{3,2,1,0:T(8,128)(2,1)S(1)}, u32[]{:S(2)}) copy-start(bf16[6,2,64,1280]{3,2,1,0:T(8,128)(2,1)S(1)} %pack.2.near) | copy-start | bytes 5898244
  94.5 13.8 %collective-permute-start.18 = (bf16[6,2,64,1280]{3,2,1,0:T(8,128)(2,1)S(1)}, bf16[6,2,64,1280]{3,2,1,0:T(8,128)(2,1)}, u32[]{:S(2)}, u32[]{:S(2)}) collective-permute-start(bf16[6,2,64,1280]{3,2,1,0:T(8,128)(2,1)S(1)} %pack.2.near), channel_id=1, source_target_pairs={{0,2},{2,0},{4,6},{6,4},{8,10},{10,8},{12,14},{14,12},{16,18},{18,... | collective-permute-start | bytes 5898248 | tf_op jit(solution)/shard_map/cc_text/ppermute | solution.py:264
  94.9 11.5 %collective-permute-start.15 = (bf16[2,64,1280]{2,1,0:T(8,128)(2,1)}, bf16[2,64,1280]{2,1,0:T(8,128)(2,1)S(1)}, u32[]{:S(2)}, u32[]{:S(2)}) collective-permute-start(bf16[2,64,1280]{2,1,0:T(8,128)(2,1)} %collective-permute-done.13.refs_5_), channel_id=1, source_target_pairs={{0,32},{2,34},{4,36},{6,38},{8,40},{10,42},{12,44},{14,46},{16,240... | collective-permute-start | bytes 983048 | tf_op jit(solution)/shard_map/text_z/ppermute | solution.py:264
  97.8 10.3 %collective-permute-start.16 = (bf16[2,64,1280]{2,1,0:T(8,128)(2,1)S(1)}, bf16[2,64,1280]{2,1,0:T(8,128)(2,1)S(1)}, u32[]{:S(2)}, u32[]{:S(2)}) collective-permute-start(bf16[2,64,1280]{2,1,0:T(8,128)(2,1)S(1)} %copy_bitcast_fusion.refs_0_), channel_id=1, source_target_pairs={{0,224},{2,226},{4,228},{6,230},{8,232},{10,234},{12,236},{14,238}... | collective-permute-start | bytes 983048 | tf_op jit(solution)/shard_map/text_z/ppermute | solution.py:264
  108.1 2.2 %collective-permute-start.19 = (bf16[2,2,64,1280]{3,2,1,0:T(8,128)(2,1)S(1)}, bf16[2,2,64,1280]{3,2,1,0:T(8,128)(2,1)S(1)}, u32[]{:S(2)}, u32[]{:S(2)}) collective-permute-start(bf16[2,2,64,1280]{3,2,1,0:T(8,128)(2,1)S(1)} %pack.3.last), channel_id=1, source_target_pairs={{0,2},{2,0},{4,6},{6,4},{8,10},{10,8},{12,14},{14,12},{16,18},{18,... | collective-permute-start | bytes 1966088 | tf_op jit(solution)/shard_map/cc_text/ppermute | solution.py:264
  120.1 12.2 %collective-permute-start.20 = (bf16[256,768]{1,0:T(8,128)(2,1)}, bf16[256,768]{1,0:T(8,128)(2,1)S(1)}, u32[]{:S(2)}, u32[]{:S(2)}) collective-permute-start(bf16[256,768]{1,0:T(8,128)(2,1)} %get-tuple-element.79), channel_id=1, source_target_pairs={{0,4},{2,6},{4,0},{6,2},{8,12},{10,14},{12,8},{14,10},{16,20},{18,... | collective-permute-start | bytes 1179656 | tf_op jit(solution)/shard_map/back/ppermute | solution.py:264
  127.8 9.3 %collective-permute-start.21 = (bf16[256,512]{1,0:T(8,128)(2,1)}, bf16[256,512]{1,0:T(8,128)(2,1)S(1)}, u32[]{:S(2)}, u32[]{:S(2)}) collective-permute-start(bf16[256,512]{1,0:T(8,128)(2,1)} %get-tuple-element.80), channel_id=1, source_target_pairs={{0,4},{2,6},{4,0},{6,2},{8,12},{10,14},{12,8},{14,10},{16,20},{18,... | collective-permute-start | bytes 786440 | tf_op jit(solution)/shard_map/back/ppermute | solution.py:264
  (15 other events, 44.0 us)

commit v4 on v3

--- a/solution.py
+++ b/solution.py
@@ -95,6 +95,7 @@
     return lax.dot_general(query, keys, (((1,), (1,)), ((), ())), preferred_element_type=jnp.float32)
 
 
+GROUP = 2
 UNITS = [
     (tile, slice(block * BLK, (block + 1) * BLK), tile * 2 + block)
     for tile in range(2)
@@ -105,7 +106,7 @@
 def latent_kernel(
     half_ref, slots_ref, valid_ref, text_at_ref,
     q_own, q_far, k_own, v_own, far, out_own, out_far, mid, cc_part,
-    sums, stats, keys, values,
+    sums, tops, totals, keys, values,
 ):
     tiles = [
         (k_own, v_own),
@@ -128,7 +129,6 @@
             parts[s] = jnp.where(valid_ref[row, s] > 0, parts[s], NEG)
         return parts
 
-    left = lax.broadcasted_iota(jnp.int32, (BLK, HD), 1) < HD // 2
     ahead = score(UNITS[0])
     for unit, later in zip(UNITS, UNITS[1:] + [None]):
         parts, ahead = ahead, score(later) if later else None
@@ -138,12 +138,13 @@
         sums[tile, rows, :] = jnp.dot(
             rounded, listed(row, values), preferred_element_type=jnp.float32
         )
-        stats[tile, rows, :] = jnp.where(left, top, total)
+        tops[tile, rows, :] = jnp.broadcast_to(top, (BLK, HD))
+        totals[tile, rows, :] = jnp.broadcast_to(total, (BLK, HD))
 
 
 def text_kernel(
     half_ref, slots_ref, valid_ref, text_at_ref,
-    q_own, q_far, sums, stats, near, last, cc_near, cc_last, o_own, o_far, keys, values,
+    q_own, q_far, sums, tops, totals, near, last, cc_near, cc_last, o_own, o_far, keys, values,
 ):
     for core, (most, other) in enumerate(((near, last), (cc_near, cc_last))):
         planes = [most.at[i] for i in range(6)] + [other.at[i] for i in range(2)]
@@ -152,39 +153,42 @@
             keys[to : to + 64, :] = plane[0]
             values[to : to + 64, :] = plane[1]
 
-    def listed(tile, store):
+    units = [
+        (tile, rows, slice(head * HD, (head + 1) * HD))
+        for head in range(GROUP)
+        for tile, rows, _ in UNITS
+    ]
+
+    def listed(unit, store):
+        tile, _, cols = unit
         starts = [pl.multiple_of(text_at_ref[tile, i] * BLK, BLK) for i in range(2)]
-        return jnp.concatenate([store[pl.ds(at, BLK), :] for at in starts], axis=0)
+        return jnp.concatenate([store[pl.ds(at, BLK), cols] for at in starts], axis=0)
 
     scores = [
-        scored((q_own, q_far)[tile][rows, :], listed(tile, keys)) for tile, rows, row in UNITS
+        scored((q_own, q_far)[unit[0]][unit[1], unit[2]], listed(unit, keys)) for unit in units
     ]
     parts = [[score[:, :BLK], score[:, BLK:]] for score in scores]
-    before = [stats[tile, rows, :1] for tile, rows, row in UNITS]
-    ends = slice(HD // 2, HD // 2 + 1)
-    totals_before = [stats[tile, rows, ends] for tile, rows, row in UNITS]
-    tops = [
-        jnp.maximum(old, jnp.max(jnp.maximum(*part), axis=1, keepdims=True))
-        for old, part in zip(before, parts)
-    ]
-    softs = [softened(part, top) for part, top in zip(parts, tops)]
-    fades = [jnp.exp2((old - top) * C2) for old, top in zip(before, tops)]
+    highest = [
+        jnp.maximum(tops[unit], jnp.max(jnp.maximum(*part), axis=1, keepdims=True))
+        for unit, part in zip(units, parts)
+    ]
+    softs = [softened(part, top) for part, top in zip(parts, highest)]
     mixes = [
-        jnp.dot(rounded, listed(tile, values), preferred_element_type=jnp.float32)
-        for (rounded, _), (tile, rows, row) in zip(softs, UNITS)
-    ]
-    for i, (tile, rows, row) in enumerate(UNITS):
-        total = totals_before[i] * fades[i] + softs[i][1]
-        mixed = (sums[tile, rows, :] * fades[i] + mixes[i]) / total
-        (o_own, o_far)[tile][rows, :] = mixed.astype(jnp.bfloat16)
-
-
-def specs_of(first):
+        jnp.dot(rounded, listed(unit, values), preferred_element_type=jnp.float32)
+        for (rounded, _), unit in zip(softs, units)
+    ]
+    for unit, top, (_, total), mixed in zip(units, highest, softs, mixes):
+        fade = jnp.exp2((tops[unit] - top) * C2)
+        mixed = (sums[unit] * fade + mixed) / (totals[unit] * fade + total)
+        (o_own, o_far)[unit[0]][unit[1], unit[2]] = mixed.astype(jnp.bfloat16)
+
+
+def specs_of(first, group=1):
     def whole(i, half, *_):
-        return (0, half[0] * HALF + first + i)
+        return (0, half[0] * (HALF // group) + first // group + i)
 
     def halved(lead):
-        return lambda i, *_: (0,) * lead + (first + i,)
+        return lambda i, *_: (0,) * lead + (first // group + i,)
 
     def chunk(lead):
         return lambda i, *_: (0,) * lead + (i,)
@@ -192,16 +196,16 @@
     return whole, halved, chunk
 
 
-def call(kernel, name, heads, keys, in_specs, out_shape, out_specs, rows, arguments):
+def call(kernel, name, heads, keys, in_specs, out_shape, out_specs, scratch, arguments):
     return pl.pallas_call(
         kernel,
         out_shape=out_shape,
         grid_spec=pltpu.PrefetchScalarGridSpec(
             num_scalar_prefetch=4,
-            grid=(heads,),
+            grid=(heads * HD // scratch[1],),
             in_specs=in_specs,
             out_specs=out_specs,
-            scratch_shapes=[pltpu.VMEM((rows, HD), jnp.bfloat16)] * 2,
+            scratch_shapes=[pltpu.VMEM(scratch, jnp.bfloat16)] * 2,
         ),
         compiler_params=pltpu.CompilerParams(vmem_limit_bytes=56 * 1024 * 1024),
         cost_estimate=pl.CostEstimate(
@@ -228,26 +232,26 @@
         pl.BlockSpec((5, *pair), chunk(3)),
     ]
     out = jax.ShapeDtypeStruct((2, TOK, heads * HD), jnp.float32)
-    out_specs = (pl.BlockSpec(pair, chunk(2)), pl.BlockSpec(pair, chunk(2)))
+    out_specs = (pl.BlockSpec(pair, chunk(2)),) * 3
     return call(
-        latent_kernel, "latent", heads, 1024, in_specs, (out, out), out_specs, 10 * TOK,
+        latent_kernel, "latent", heads, 1024, in_specs, (out,) * 3, out_specs, (10 * TOK, HD),
         (*scalars, *arrays),
     )
 
 
 def finish(first, heads, scalars, *arrays):
-    whole, halved, chunk = specs_of(first)
+    whole, halved, chunk = specs_of(first, GROUP)
+    wide = GROUP * HD
     in_specs = [
-        pl.BlockSpec((TOK, HD), whole),
-        pl.BlockSpec((TOK, HD), halved(1)),
-        pl.BlockSpec((2, TOK, HD), chunk(2)),
-        pl.BlockSpec((2, TOK, HD), chunk(2)),
-        *[pl.BlockSpec((n, 2, 64, HD), halved(3)) for n in (6, 2, 6, 2)],
+        pl.BlockSpec((TOK, wide), whole),
+        pl.BlockSpec((TOK, wide), halved(1)),
+        *[pl.BlockSpec((2, TOK, wide), chunk(2))] * 3,
+        *[pl.BlockSpec((n, 2, 64, wide), halved(3)) for n in (6, 2, 6, 2)],
     ]
     out = jax.ShapeDtypeStruct((TOK, heads * HD), jnp.bfloat16)
-    out_specs = (pl.BlockSpec((TOK, HD), chunk(1)), pl.BlockSpec((TOK, HD), chunk(1)))
+    out_specs = (pl.BlockSpec((TOK, wide), chunk(1)),) * 2
     return call(
-        text_kernel, "finish", heads, 256, in_specs, (out, out), out_specs, ZN * BLK,
+        text_kernel, "finish", heads, 256, in_specs, (out, out), out_specs, (ZN * BLK, wide),
         (*scalars, *arrays),
     )
 
@@ -364,7 +368,7 @@
     near = pack(plane, hop1, hop2, hop3, hop4, hop5)
     cc_near = send("cc_text", near, CORES)
     sums2 = attended(1, far2, out_far2, mid2, swapped(1, far2, out_far2, mid2))
-    hop6, other, _, _ = lax.optimization_barrier((hop6, other, *sums2))
+    hop6, other, *_ = lax.optimization_barrier((hop6, other, *sums2))
     last = pack(hop6, other)
     cc_last = send("cc_text", last, CORES)
     text = (near, last, cc_near, cc_last)

time: 140 us -> 138 us (0.986)
  Pallas kernels: 38.9 us -> 34.7 us
  waiting for transfers between devices: 49 us -> 50.7 us
    pallas_call x4, Pallas kernels: 34.5 us -> 30.4 us  [call(): pl.pallas_call(kernel, out_shape=out_shape, grid_spec=pltpu.PrefetchScala...]
    ppermute x22, waiting for transfers between devices: 47.2 us -> 49 us  [send(): return lax.ppermute(block, 'seq', to)]
  transfers between devices with their start and end apart: 23 -> 23, of which waited for: 11 -> 11; matrix products, arithmetic and copies ran while one was open for 7% -> 8% of each run, Pallas kernels for 19% -> 18%
where the time goes in v4:
time: 138 us; the launch traced here: 136 us
  waiting for transfers between devices  50.7 us (37%)
  Pallas kernels  34.7 us (25%)
  starting transfers between devices  34.1 us (25%)
  local copies, waits for them, and re-layouts  10.1 us (7%)
  other arithmetic  5.3 us (4%)
    ppermute x22, waiting for transfers between devices, send(): return lax.ppermute(block, 'seq', to)  49 us
    pallas_call x4, Pallas kernels, call(): pl.pallas_call(kernel, out_shape=out_shape, grid_spec=pltpu.PrefetchScala...  30.4 us
    ppermute x22, starting transfers between devices, send(): return lax.ppermute(block, 'seq', to)  29 us
    all_to_all x1, starting transfers between devices, on_device(): lax.all_to_all(spread.reshape(YN * XN, *halves.shape[1:]), 'seq', 0, 0, a...  5.1 us
    another operation x4, local copies, waits for them, and re-layouts, pair_of(): jnp.stack([half_of(a, which, first, heads) for a in (latent_keys, latent_...  4.16 us
    pallas_call x2, Pallas kernels, gather_heads(): pl.pallas_call(gather_kernel, out_shape=jax.ShapeDtypeStruct((len(pairs),...  2.98 us
  transfers between devices with their start and end apart: 23, of which 11 were waited for; matrix products, arithmetic and copies ran while one was open for 8% of the time, Pallas kernels for 18%

profile of v4, /device:TPU:4, one launch (start us, length us, event | category | flops | bytes accessed | tf_op | source)
XLA Modules:
  0.0 136.1 jit_solution(9398973393261652776)
XLA Ops:
  1.7 5.1 %all-to-all-start = ((bf16[8,2,8,1280]{3,2,1,0:T(8,128)(2,1)}), bf16[8,2,8,1280]{3,2,1,0:T(8,128)(2,1)}, u32[]{:S(2)}, u32[]{:S(2)}) async-start(bf16[8,2,8,1280]{3,2,1,0:T(8,128)(2,1)} %bitcast.4), calls=%async_computation | async-start | bytes 655360 | tf_op jit(solution)/shard_map/all_to_all | solution.py:317
  7.5 2.1 %collective-permute-start = (s32[2,16]{1,0:T(2,128)S(1)}, s32[2,16]{1,0:T(2,128)S(1)}, u32[]{:S(2)}, u32[]{:S(2)}) collective-permute-start(s32[2,16]{1,0:T(2,128)S(1)} %concatenate.15), channel_id=1, source_target_pairs={{0,4},{2,6},{4,0},{6,2},{8,12},{10,14},{12,8},{14,10},{16,20},{18,... | collective-permute-start | bytes 392 | tf_op jit(solution)/shard_map/table/ppermute | solution.py:268
  9.6 1.0 dynamic-slice_bitcast_fusion.2
  11.6 1.2 dynamic-slice_bitcast_fusion
  13.1 1.8 %all-to-all-done = bf16[8,2,8,1280]{3,2,1,0:T(8,128)(2,1)} async-done(((bf16[8,2,8,1280]{3,2,1,0:T(8,128)(2,1)}), bf16[8,2,8,1280]{3,2,1,0:T(8,128)(2,1)}, u32[]{:S(2)}, u32[]{:S(2)}) %all-to-all-start) | async-done | bytes 327712 | tf_op jit(solution)/shard_map/all_to_all | solution.py:317
  14.9 1.0 copy_bitcast_fusion.refs_0_
  16.6 6.7 %collective-permute-start.3 = (bf16[2,256,1280]{2,1,0:T(8,128)(2,1)S(1)}, bf16[2,256,1280]{2,1,0:T(8,128)(2,1)S(1)}, u32[]{:S(2)}, u32[]{:S(2)}) collective-permute-start(bf16[2,256,1280]{2,1,0:T(8,128)(2,1)S(1)} %pad_maximum_fusion.refs_0_), channel_id=1, source_target_pairs={{0,248},{2,10},{4,252},{6,14},{8,0},{10,18},{12,4},{14,22},{16,8},... | collective-permute-start | bytes 3932168 | tf_op jit(solution)/shard_map/out_own/ppermute | solution.py:268
  23.3 1.0 dynamic-slice_bitcast_fusion.5
  24.3 1.0 dynamic-slice_bitcast_fusion.4
  27.6 6.1 %collective-permute-done.1.refs_1_ = bf16[2,64,1280]{2,1,0:T(8,128)(2,1)S(1)} collective-permute-done((bf16[2,64,1280]{2,1,0:T(8,128)(2,1)S(1)}, bf16[2,64,1280]{2,1,0:T(8,128)(2,1)S(1)}, u32[]{:S(2)}, u32[]{:S(2)}) %collective-permute-start.1) | collective-permute-done | bytes 327712 | tf_op jit(solution)/shard_map/text_z/ppermute | solution.py:268
  33.7 4.7 %collective-permute-done.3.refs_2_.out_own = bf16[2,256,1280]{2,1,0:T(8,128)(2,1)S(1)} collective-permute-done((bf16[2,256,1280]{2,1,0:T(8,128)(2,1)S(1)}, bf16[2,256,1280]{2,1,0:T(8,128)(2,1)S(1)}, u32[]{:S(2)}, u32[]{:S(2)}) %collective-permute-start.3) | collective-permute-done | bytes 1310752 | tf_op jit(solution)/shard_map/out_own/ppermute | solution.py:268
  38.6 5.9 %collective-permute-start.6 = (bf16[2,256,768]{2,1,0:T(8,128)(2,1)S(1)}, bf16[2,256,768]{2,1,0:T(8,128)(2,1)S(1)}, u32[]{:S(2)}, u32[]{:S(2)}) collective-permute-start(bf16[2,256,768]{2,1,0:T(8,128)(2,1)S(1)} %collective-permute-done.2.refs_1_.far), channel_id=1, source_target_pairs={{0,248},{2,10},{4,252},{6,14},{8,0},{10,18},{12,4},{14,22},{16,8},... | collective-permute-start | bytes 2359304 | tf_op jit(solution)/shard_map/out_far/ppermute | solution.py:268
  44.5 1.5 %collective-permute-start.5 = (bf16[256,1280]{1,0:T(8,128)(2,1)S(1)}, bf16[256,1280]{1,0:T(8,128)(2,1)S(1)}, u32[]{:S(2)}, u32[]{:S(2)}) collective-permute-start(bf16[256,1280]{1,0:T(8,128)(2,1)S(1)} %constant_dynamic-slice_fusion), channel_id=1, source_target_pairs={{0,4},{2,6},{4,0},{6,2},{8,12},{10,14},{12,8},{14,10},{16,20},{18,... | collective-permute-start | bytes 1966088 | tf_op jit(solution)/shard_map/q_far/ppermute | solution.py:268
  46.5 9.4 %collective-permute-done.8.refs_2_ = bf16[2,64,1280]{2,1,0:T(8,128)(2,1)S(1)} collective-permute-done((bf16[2,64,1280]{2,1,0:T(8,128)(2,1)S(1)}, bf16[2,64,1280]{2,1,0:T(8,128)(2,1)S(1)}, u32[]{:S(2)}, u32[]{:S(2)}) %collective-permute-start.8) | collective-permute-done | bytes 327712 | tf_op jit(solution)/shard_map/text_z/ppermute | solution.py:268
  55.9 10.6 %collective-permute-done.4.refs_1_.far = bf16[2,256,512]{2,1,0:T(8,128)(2,1)S(1)} collective-permute-done((bf16[2,256,512]{2,1,0:T(8,128)(2,1)S(1)}, bf16[2,256,512]{2,1,0:T(8,128)(2,1)S(1)}, u32[]{:S(2)}, u32[]{:S(2)}) %collective-permute-start.4) | collective-permute-done | bytes 524320 | tf_op jit(solution)/shard_map/far/ppermute | solution.py:268
  67.4 1.8 %gather_heads.2 = bf16[5,2,256,768]{3,2,1,0:T(8,128)(2,1)S(1)} custom-call(bf16[2,256,1280]{2,1,0:T(8,128)(2,1)S(1)} %pad_maximum_fusion.refs_0_, bf16[2,256,768]{2,1,0:T(8,128)(2,1)S(1)} %collective-permute-done.2.refs_1_.far, bf16[2,256,1280]{2,1,0:T(8,128)(2,1)S(1)} %collective-permute-done.3.refs_2_.out_own, ...), custom_call_target="tpu_custom_call" | custom-call | tf_op jit(solution)/shard_map/gather_heads/pallas_call | solution.py:77
  69.8 5.5 %collective-permute-start.10 = (bf16[2,256,512]{2,1,0:T(8,128)(2,1)S(1)}, bf16[2,256,512]{2,1,0:T(8,128)(2,1)S(1)}, u32[]{:S(2)}, u32[]{:S(2)}) collective-permute-start(bf16[2,256,512]{2,1,0:T(8,128)(2,1)S(1)} %collective-permute-done.4.refs_1_.far), channel_id=1, source_target_pairs={{0,248},{2,10},{4,252},{6,14},{8,0},{10,18},{12,4},{14,22},{16,8},... | collective-permute-start | bytes 1572872 | tf_op jit(solution)/shard_map/out_far/ppermute | solution.py:268
  75.4 5.3 %collective-permute-done.12.refs_4_ = bf16[2,64,1280]{2,1,0:T(8,128)(2,1)S(1)} collective-permute-done((bf16[2,64,1280]{2,1,0:T(8,128)(2,1)S(1)}, bf16[2,64,1280]{2,1,0:T(8,128)(2,1)S(1)}, u32[]{:S(2)}, u32[]{:S(2)}) %collective-permute-start.12) | collective-permute-done | bytes 327712 | tf_op jit(solution)/shard_map/text_z/ppermute | solution.py:268
  80.7 10.7 %latent.2 = (f32[2,256,768]{2,1,0:T(8,128)}, f32[2,256,768]{2,1,0:T(8,128)}, f32[2,256,768]{2,1,0:T(8,128)}) custom-call(s32[1]{0:T(128)} %bitcast.12.half_ref, s32[4,8]{1,0:T(4,128)} %fusion.2.slots_ref, s32[4,8]{1,0:T(4,128)} %get-tuple-element.55.valid_ref, s32[2,2]{1,0:T(2,128)} %and_select_fusion.text_at_ref, bf16[256,2560]{1,0:T(8,128)(2,1)} %q_own.3, ...), custom_call_target="tpu_custom_call" | custom-call | flops 9663676416 | bytes 12288000 | tf_op jit(solution)/shard_map/latent/pallas_call | solution.py:200
  91.6 1.2 gather_heads.3
  93.1 1.3 pack.2.near
  94.9 2.9 %collective-permute-start.15 = (bf16[2,64,1280]{2,1,0:T(8,128)(2,1)}, bf16[2,64,1280]{2,1,0:T(8,128)(2,1)S(1)}, u32[]{:S(2)}, u32[]{:S(2)}) collective-permute-start(bf16[2,64,1280]{2,1,0:T(8,128)(2,1)} %collective-permute-done.13.refs_5_), channel_id=1, source_target_pairs={{0,32},{2,34},{4,36},{6,38},{8,40},{10,42},{12,44},{14,46},{16,240... | collective-permute-start | bytes 983048 | tf_op jit(solution)/shard_map/text_z/ppermute | solution.py:268
  98.1 8.0 %latent.3 = (f32[2,256,512]{2,1,0:T(8,128)}, f32[2,256,512]{2,1,0:T(8,128)}, f32[2,256,512]{2,1,0:T(8,128)}) custom-call(s32[1]{0:T(128)} %bitcast.12.half_ref, s32[4,8]{1,0:T(4,128)} %fusion.2.slots_ref, s32[4,8]{1,0:T(4,128)} %get-tuple-element.55.valid_ref, s32[2,2]{1,0:T(2,128)} %and_select_fusion.text_at_ref, bf16[256,2560]{1,0:T(8,128)(2,1)} %q_own.3, ...), custom_call_target="tpu_custom_call" | custom-call | flops 6442450944 | bytes 8192000 | tf_op jit(solution)/shard_map/latent/pallas_call | solution.py:200
  106.4 1.7 %collective-permute-done.16.refs_1_ = bf16[2,64,1280]{2,1,0:T(8,128)(2,1)S(1)} collective-permute-done((bf16[2,64,1280]{2,1,0:T(8,128)(2,1)S(1)}, bf16[2,64,1280]{2,1,0:T(8,128)(2,1)S(1)}, u32[]{:S(2)}, u32[]{:S(2)}) %collective-permute-start.16) | collective-permute-done | bytes 327712 | tf_op jit(solution)/shard_map/text_z/ppermute | solution.py:268
  108.3 2.1 %collective-permute-done.19.cc_last = bf16[2,2,64,1280]{3,2,1,0:T(8,128)(2,1)S(1)} collective-permute-done((bf16[2,2,64,1280]{3,2,1,0:T(8,128)(2,1)S(1)}, bf16[2,2,64,1280]{3,2,1,0:T(8,128)(2,1)S(1)}, u32[]{:S(2)}, u32[]{:S(2)}) %collective-permute-start.19) | collective-permute-done | bytes 655392 | tf_op jit(solution)/shard_map/cc_text/ppermute | solution.py:268
  111.2 6.6 %finish.2 = (bf16[256,768]{1,0:T(8,128)(2,1)}, bf16[256,768]{1,0:T(8,128)(2,1)}) custom-call(s32[1]{0:T(128)} %bitcast.12.half_ref, s32[4,8]{1,0:T(4,128)} %fusion.2.slots_ref, s32[4,8]{1,0:T(4,128)} %get-tuple-element.55.valid_ref, s32[2,2]{1,0:T(2,128)} %and_select_fusion.text_at_ref, bf16[256,2560]{1,0:T(8,128)(2,1)} %q_own.3, ...), custom_call_target="tpu_custom_call" | custom-call | flops 2415919104 | bytes 3072000 | tf_op jit(solution)/shard_map/finish/pallas_call | solution.py:200
  118.7 5.0 %finish.3 = (bf16[256,512]{1,0:T(8,128)(2,1)}, bf16[256,512]{1,0:T(8,128)(2,1)}) custom-call(s32[1]{0:T(128)} %bitcast.12.half_ref, s32[4,8]{1,0:T(4,128)} %fusion.2.slots_ref, s32[4,8]{1,0:T(4,128)} %get-tuple-element.55.valid_ref, s32[2,2]{1,0:T(2,128)} %and_select_fusion.text_at_ref, bf16[256,2560]{1,0:T(8,128)(2,1)} %q_own.3, ...), custom_call_target="tpu_custom_call" | custom-call | flops 1610612736 | bytes 2048000 | tf_op jit(solution)/shard_map/finish/pallas_call | solution.py:200
  123.6 1.3 collective-permute-start.21
  124.9 1.0 constant_dynamic-update-slice_fusion
  125.9 4.1 %collective-permute-done.20 = bf16[256,768]{1,0:T(8,128)(2,1)S(1)} collective-permute-done((bf16[256,768]{1,0:T(8,128)(2,1)}, bf16[256,768]{1,0:T(8,128)(2,1)S(1)}, u32[]{:S(2)}, u32[]{:S(2)}) %collective-permute-start.20) | collective-permute-done | bytes 393248 | tf_op jit(solution)/shard_map/back/ppermute | solution.py:268
  130.0 4.8 %collective-permute-done.21 = bf16[256,512]{1,0:T(8,128)(2,1)S(1)} collective-permute-done((bf16[256,512]{1,0:T(8,128)(2,1)}, bf16[256,512]{1,0:T(8,128)(2,1)S(1)}, u32[]{:S(2)}, u32[]{:S(2)}) %collective-permute-start.21) | collective-permute-done | bytes 262176 | tf_op jit(solution)/shard_map/back/ppermute | solution.py:268
  135.0 1.1 pad_maximum_fusion.1
  (100 shorter events, 11.6 us)
Async XLA Ops:
  1.7 13.2 %all-to-all-start = ((bf16[8,2,8,1280]{3,2,1,0:T(8,128)(2,1)}), bf16[8,2,8,1280]{3,2,1,0:T(8,128)(2,1)}, u32[]{:S(2)}, u32[]{:S(2)}) async-start(bf16[8,2,8,1280]{3,2,1,0:T(8,128)(2,1)} %bitcast.4), calls=%async_computation | async-start | bytes 655360 | tf_op jit(solution)/shard_map/all_to_all | solution.py:317
  7.5 8.4 %collective-permute-start = (s32[2,16]{1,0:T(2,128)S(1)}, s32[2,16]{1,0:T(2,128)S(1)}, u32[]{:S(2)}, u32[]{:S(2)}) collective-permute-start(s32[2,16]{1,0:T(2,128)S(1)} %concatenate.15), channel_id=1, source_target_pairs={{0,4},{2,6},{4,0},{6,2},{8,12},{10,14},{12,8},{14,10},{16,20},{18,... | collective-permute-start | bytes 392 | tf_op jit(solution)/shard_map/table/ppermute | solution.py:268
  11.6 22.2 %collective-permute-start.2 = (bf16[2,256,768]{2,1,0:T(8,128)(2,1)}, bf16[2,256,768]{2,1,0:T(8,128)(2,1)S(1)}, u32[]{:S(2)}, u32[]{:S(2)}) collective-permute-start(bf16[2,256,768]{2,1,0:T(8,128)(2,1)} %pad_maximum_fusion.2), channel_id=1, source_target_pairs={{0,4},{2,6},{4,0},{6,2},{8,12},{10,14},{12,8},{14,10},{16,20},{18,... | collective-permute-start | bytes 2359304 | tf_op jit(solution)/shard_map/far/ppermute | solution.py:268
  16.6 11.0 %copy-start.18 = (bf16[256,2560]{1,0:T(8,128)(2,1)S(1)}, bf16[256,2560]{1,0:T(8,128)(2,1)}, u32[]{:S(2)}) copy-start(bf16[256,2560]{1,0:T(8,128)(2,1)} %q_own.3) | copy-start | bytes 3932164
  16.6 21.8 %collective-permute-start.3 = (bf16[2,256,1280]{2,1,0:T(8,128)(2,1)S(1)}, bf16[2,256,1280]{2,1,0:T(8,128)(2,1)S(1)}, u32[]{:S(2)}, u32[]{:S(2)}) collective-permute-start(bf16[2,256,1280]{2,1,0:T(8,128)(2,1)S(1)} %pad_maximum_fusion.refs_0_), channel_id=1, source_target_pairs={{0,248},{2,10},{4,252},{6,14},{8,0},{10,18},{12,4},{14,22},{16,8},... | collective-permute-start | bytes 3932168 | tf_op jit(solution)/shard_map/out_own/ppermute | solution.py:268
  25.4 8.4 %collective-permute-start.1 = (bf16[2,64,1280]{2,1,0:T(8,128)(2,1)S(1)}, bf16[2,64,1280]{2,1,0:T(8,128)(2,1)S(1)}, u32[]{:S(2)}, u32[]{:S(2)}) collective-permute-start(bf16[2,64,1280]{2,1,0:T(8,128)(2,1)S(1)} %copy_bitcast_fusion.refs_0_), channel_id=1, source_target_pairs={{0,32},{2,34},{4,36},{6,38},{8,40},{10,42},{12,44},{14,46},{16,240... | collective-permute-start | bytes 983048 | tf_op jit(solution)/shard_map/text_z/ppermute | solution.py:268
  33.7 35.5 %copy-start.10 = (bf16[2,64,1280]{2,1,0:T(8,128)(2,1)}, bf16[2,64,1280]{2,1,0:T(8,128)(2,1)S(1)}, u32[]{:S(2)}) copy-start(bf16[2,64,1280]{2,1,0:T(8,128)(2,1)S(1)} %collective-permute-done.1.refs_1_) | copy-start | bytes 983044
  33.7 35.5 %copy-start.4 = (bf16[2,256,768]{2,1,0:T(8,128)(2,1)}, bf16[2,256,768]{2,1,0:T(8,128)(2,1)S(1)}, u32[]{:S(2)}) copy-start(bf16[2,256,768]{2,1,0:T(8,128)(2,1)S(1)} %collective-permute-done.2.refs_1_.far) | copy-start | bytes 2359300
  38.4 30.8 %copy-start.2 = (bf16[2,256,1280]{2,1,0:T(8,128)(2,1)}, bf16[2,256,1280]{2,1,0:T(8,128)(2,1)S(1)}, u32[]{:S(2)}) copy-start(bf16[2,256,1280]{2,1,0:T(8,128)(2,1)S(1)} %collective-permute-done.3.refs_2_.out_own) | copy-start | bytes 3932164
  38.5 28.0 %collective-permute-start.7 = (bf16[2,256,768]{2,1,0:T(8,128)(2,1)S(1)}, bf16[2,256,768]{2,1,0:T(8,128)(2,1)S(1)}, u32[]{:S(2)}, u32[]{:S(2)}) collective-permute-start(bf16[2,256,768]{2,1,0:T(8,128)(2,1)S(1)} %slice_select_fusion), channel_id=1, source_target_pairs={{0,8},{2,250},{4,12},{6,254},{8,16},{10,2},{12,20},{14,6},{16,24},... | collective-permute-start | bytes 2359304 | tf_op jit(solution)/shard_map/mid/ppermute | solution.py:268
  38.6 28.8 %collective-permute-start.6 = (bf16[2,256,768]{2,1,0:T(8,128)(2,1)S(1)}, bf16[2,256,768]{2,1,0:T(8,128)(2,1)S(1)}, u32[]{:S(2)}, u32[]{:S(2)}) collective-permute-start(bf16[2,256,768]{2,1,0:T(8,128)(2,1)S(1)} %collective-permute-done.2.refs_1_.far), channel_id=1, source_target_pairs={{0,248},{2,10},{4,252},{6,14},{8,0},{10,18},{12,4},{14,22},{16,8},... | collective-permute-start | bytes 2359304 | tf_op jit(solution)/shard_map/out_far/ppermute | solution.py:268
  44.5 11.5 %collective-permute-start.8 = (bf16[2,64,1280]{2,1,0:T(8,128)(2,1)S(1)}, bf16[2,64,1280]{2,1,0:T(8,128)(2,1)S(1)}, u32[]{:S(2)}, u32[]{:S(2)}) collective-permute-start(bf16[2,64,1280]{2,1,0:T(8,128)(2,1)S(1)} %collective-permute-done.1.refs_1_), channel_id=1, source_target_pairs={{0,32},{2,34},{4,36},{6,38},{8,40},{10,42},{12,44},{14,46},{16,240... | collective-permute-start | bytes 983048 | tf_op jit(solution)/shard_map/text_z/ppermute | solution.py:268
  44.5 22.1 %collective-permute-start.5 = (bf16[256,1280]{1,0:T(8,128)(2,1)S(1)}, bf16[256,1280]{1,0:T(8,128)(2,1)S(1)}, u32[]{:S(2)}, u32[]{:S(2)}) collective-permute-start(bf16[256,1280]{1,0:T(8,128)(2,1)S(1)} %constant_dynamic-slice_fusion), channel_id=1, source_target_pairs={{0,4},{2,6},{4,0},{6,2},{8,12},{10,14},{12,8},{14,10},{16,20},{18,... | collective-permute-start | bytes 1966088 | tf_op jit(solution)/shard_map/q_far/ppermute | solution.py:268
  46.0 20.6 %collective-permute-start.4 = (bf16[2,256,512]{2,1,0:T(8,128)(2,1)S(1)}, bf16[2,256,512]{2,1,0:T(8,128)(2,1)S(1)}, u32[]{:S(2)}, u32[]{:S(2)}) collective-permute-start(bf16[2,256,512]{2,1,0:T(8,128)(2,1)S(1)} %pad_maximum_fusion.3), channel_id=1, source_target_pairs={{0,4},{2,6},{4,0},{6,2},{8,12},{10,14},{12,8},{14,10},{16,20},{18,... | collective-permute-start | bytes 1572872 | tf_op jit(solution)/shard_map/far/ppermute | solution.py:268
  55.9 13.3 %copy-start.12 = (bf16[2,64,1280]{2,1,0:T(8,128)(2,1)}, bf16[2,64,1280]{2,1,0:T(8,128)(2,1)S(1)}, u32[]{:S(2)}) copy-start(bf16[2,64,1280]{2,1,0:T(8,128)(2,1)S(1)} %collective-permute-done.8.refs_2_) | copy-start | bytes 983044
  55.9 10.6 %collective-permute-start.9 = (bf16[2,64,1280]{2,1,0:T(8,128)(2,1)S(1)}, bf16[2,64,1280]{2,1,0:T(8,128)(2,1)S(1)}, u32[]{:S(2)}, u32[]{:S(2)}) collective-permute-start(bf16[2,64,1280]{2,1,0:T(8,128)(2,1)S(1)} %collective-permute-done.8.refs_2_), channel_id=1, source_target_pairs={{0,32},{2,34},{4,36},{6,38},{8,40},{10,42},{12,44},{14,46},{16,240... | collective-permute-start | bytes 983048 | tf_op jit(solution)/shard_map/text_z/ppermute | solution.py:268
  66.5 25.0 %copy-start.5 = (bf16[2,256,512]{2,1,0:T(8,128)(2,1)}, bf16[2,256,512]{2,1,0:T(8,128)(2,1)S(1)}, u32[]{:S(2)}) copy-start(bf16[2,256,512]{2,1,0:T(8,128)(2,1)S(1)} %collective-permute-done.4.refs_1_.far) | copy-start | bytes 1572868
  69.3 11.5 %collective-permute-start.14 = (bf16[5,2,256,768]{3,2,1,0:T(8,128)(2,1)S(1)}, bf16[5,2,256,768]{3,2,1,0:T(8,128)(2,1)}, u32[]{:S(2)}, u32[]{:S(2)}) collective-permute-start(bf16[5,2,256,768]{3,2,1,0:T(8,128)(2,1)S(1)} %gather_heads.2), channel_id=1, source_target_pairs={{0,2},{2,0},{4,6},{6,4},{8,10},{10,8},{12,14},{14,12},{16,18},{18,... | collective-permute-start | bytes 11796488 | tf_op jit(solution)/shard_map/cc_part/ppermute | solution.py:268
  69.4 11.3 %collective-permute-start.12 = (bf16[2,64,1280]{2,1,0:T(8,128)(2,1)S(1)}, bf16[2,64,1280]{2,1,0:T(8,128)(2,1)S(1)}, u32[]{:S(2)}, u32[]{:S(2)}) collective-permute-start(bf16[2,64,1280]{2,1,0:T(8,128)(2,1)S(1)} %collective-permute-done.9.refs_3_), channel_id=1, source_target_pairs={{0,32},{2,34},{4,36},{6,38},{8,40},{10,42},{12,44},{14,46},{16,240... | collective-permute-start | bytes 983048 | tf_op jit(solution)/shard_map/text_z/ppermute | solution.py:268
  69.8 21.7 %collective-permute-start.10 = (bf16[2,256,512]{2,1,0:T(8,128)(2,1)S(1)}, bf16[2,256,512]{2,1,0:T(8,128)(2,1)S(1)}, u32[]{:S(2)}, u32[]{:S(2)}) collective-permute-start(bf16[2,256,512]{2,1,0:T(8,128)(2,1)S(1)} %collective-permute-done.4.refs_1_.far), channel_id=1, source_target_pairs={{0,248},{2,10},{4,252},{6,14},{8,0},{10,18},{12,4},{14,22},{16,8},... | collective-permute-start | bytes 1572872 | tf_op jit(solution)/shard_map/out_far/ppermute | solution.py:268
  75.3 16.2 %copy-start.3 = (bf16[2,256,1280]{2,1,0:T(8,128)(2,1)S(1)}, bf16[2,256,1280]{2,1,0:T(8,128)(2,1)}, u32[]{:S(2)}) copy-start(bf16[2,256,1280]{2,1,0:T(8,128)(2,1)} %copy-done.2) | copy-start | bytes 3932164
  75.4 16.1 %collective-permute-start.11 = (bf16[2,256,512]{2,1,0:T(8,128)(2,1)S(1)}, bf16[2,256,512]{2,1,0:T(8,128)(2,1)S(1)}, u32[]{:S(2)}, u32[]{:S(2)}) collective-permute-start(bf16[2,256,512]{2,1,0:T(8,128)(2,1)S(1)} %slice_select_fusion.1), channel_id=1, source_target_pairs={{0,8},{2,250},{4,12},{6,254},{8,16},{10,2},{12,20},{14,6},{16,24},... | collective-permute-start | bytes 1572872 | tf_op jit(solution)/shard_map/mid/ppermute | solution.py:268
  80.7 10.8 %copy-start.16 = (bf16[2,64,1280]{2,1,0:T(8,128)(2,1)}, bf16[2,64,1280]{2,1,0:T(8,128)(2,1)S(1)}, u32[]{:S(2)}) copy-start(bf16[2,64,1280]{2,1,0:T(8,128)(2,1)S(1)} %collective-permute-done.12.refs_4_) | copy-start | bytes 983044
  80.7 10.8 %collective-permute-start.13 = (bf16[2,64,1280]{2,1,0:T(8,128)(2,1)S(1)}, bf16[2,64,1280]{2,1,0:T(8,128)(2,1)}, u32[]{:S(2)}, u32[]{:S(2)}) collective-permute-start(bf16[2,64,1280]{2,1,0:T(8,128)(2,1)S(1)} %collective-permute-done.12.refs_4_), channel_id=1, source_target_pairs={{0,32},{2,34},{4,36},{6,38},{8,40},{10,42},{12,44},{14,46},{16,240... | collective-permute-start | bytes 983048 | tf_op jit(solution)/shard_map/text_z/ppermute | solution.py:268
  92.8 5.3 %collective-permute-start.17 = (bf16[5,2,256,512]{3,2,1,0:T(8,128)(2,1)S(1)}, bf16[5,2,256,512]{3,2,1,0:T(8,128)(2,1)}, u32[]{:S(2)}, u32[]{:S(2)}) collective-permute-start(bf16[5,2,256,512]{3,2,1,0:T(8,128)(2,1)S(1)} %gather_heads.3), channel_id=1, source_target_pairs={{0,2},{2,0},{4,6},{6,4},{8,10},{10,8},{12,14},{14,12},{16,18},{18,... | collective-permute-start | bytes 7864328 | tf_op jit(solution)/shard_map/cc_part/ppermute | solution.py:268
  94.5 11.7 %copy-start = (bf16[6,2,64,1280]{3,2,1,0:T(8,128)(2,1)}, bf16[6,2,64,1280]{3,2,1,0:T(8,128)(2,1)S(1)}, u32[]{:S(2)}) copy-start(bf16[6,2,64,1280]{3,2,1,0:T(8,128)(2,1)S(1)} %pack.2.near) | copy-start | bytes 5898244
  94.5 13.8 %collective-permute-start.18 = (bf16[6,2,64,1280]{3,2,1,0:T(8,128)(2,1)S(1)}, bf16[6,2,64,1280]{3,2,1,0:T(8,128)(2,1)}, u32[]{:S(2)}, u32[]{:S(2)}) collective-permute-start(bf16[6,2,64,1280]{3,2,1,0:T(8,128)(2,1)S(1)} %pack.2.near), channel_id=1, source_target_pairs={{0,2},{2,0},{4,6},{6,4},{8,10},{10,8},{12,14},{14,12},{16,18},{18,... | collective-permute-start | bytes 5898248 | tf_op jit(solution)/shard_map/cc_text/ppermute | solution.py:268
  94.9 11.5 %collective-permute-start.15 = (bf16[2,64,1280]{2,1,0:T(8,128)(2,1)}, bf16[2,64,1280]{2,1,0:T(8,128)(2,1)S(1)}, u32[]{:S(2)}, u32[]{:S(2)}) collective-permute-start(bf16[2,64,1280]{2,1,0:T(8,128)(2,1)} %collective-permute-done.13.refs_5_), channel_id=1, source_target_pairs={{0,32},{2,34},{4,36},{6,38},{8,40},{10,42},{12,44},{14,46},{16,240... | collective-permute-start | bytes 983048 | tf_op jit(solution)/shard_map/text_z/ppermute | solution.py:268
  97.8 10.3 %collective-permute-start.16 = (bf16[2,64,1280]{2,1,0:T(8,128)(2,1)S(1)}, bf16[2,64,1280]{2,1,0:T(8,128)(2,1)S(1)}, u32[]{:S(2)}, u32[]{:S(2)}) collective-permute-start(bf16[2,64,1280]{2,1,0:T(8,128)(2,1)S(1)} %copy_bitcast_fusion.refs_0_), channel_id=1, source_target_pairs={{0,224},{2,226},{4,228},{6,230},{8,232},{10,234},{12,236},{14,238}... | collective-permute-start | bytes 983048 | tf_op jit(solution)/shard_map/text_z/ppermute | solution.py:268
  108.1 2.2 %collective-permute-start.19 = (bf16[2,2,64,1280]{3,2,1,0:T(8,128)(2,1)S(1)}, bf16[2,2,64,1280]{3,2,1,0:T(8,128)(2,1)S(1)}, u32[]{:S(2)}, u32[]{:S(2)}) collective-permute-start(bf16[2,2,64,1280]{3,2,1,0:T(8,128)(2,1)S(1)} %pack.3.last), channel_id=1, source_target_pairs={{0,2},{2,0},{4,6},{6,4},{8,10},{10,8},{12,14},{14,12},{16,18},{18,... | collective-permute-start | bytes 1966088 | tf_op jit(solution)/shard_map/cc_text/ppermute | solution.py:268
  117.8 12.2 %collective-permute-start.20 = (bf16[256,768]{1,0:T(8,128)(2,1)}, bf16[256,768]{1,0:T(8,128)(2,1)S(1)}, u32[]{:S(2)}, u32[]{:S(2)}) collective-permute-start(bf16[256,768]{1,0:T(8,128)(2,1)} %get-tuple-element.85), channel_id=1, source_target_pairs={{0,4},{2,6},{4,0},{6,2},{8,12},{10,14},{12,8},{14,10},{16,20},{18,... | collective-permute-start | bytes 1179656 | tf_op jit(solution)/shard_map/back/ppermute | solution.py:268
  123.6 11.2 %collective-permute-start.21 = (bf16[256,512]{1,0:T(8,128)(2,1)}, bf16[256,512]{1,0:T(8,128)(2,1)S(1)}, u32[]{:S(2)}, u32[]{:S(2)}) collective-permute-start(bf16[256,512]{1,0:T(8,128)(2,1)} %get-tuple-element.86), channel_id=1, source_target_pairs={{0,4},{2,6},{4,0},{6,2},{8,12},{10,14},{12,8},{14,10},{16,20},{18,... | collective-permute-start | bytes 786440 | tf_op jit(solution)/shard_map/back/ppermute | solution.py:268
  (15 other events, 42.1 us)

commit v5 on v4

--- a/solution.py
+++ b/solution.py
@@ -325,9 +325,11 @@
     scalars = whereabouts(own_table, far_table)
     out_own = send("out_own", kv_own, OUTWARD)
     hop1 = send("text_z", plane, MAJOR)
-    give2, q_give, hop1, far1, out_own, kv_own, *scalars = lax.optimization_barrier(
+    far1, q_give = lax.optimization_barrier((far1, half_of(queries, 1 - x)))
+    q_far = send("q_far", q_give, ACROSS)
+    give2, hop1, far1, out_own, kv_own, *scalars = lax.optimization_barrier(
         (
-            pair_of(1 - x, firsts[1], CHUNKS[1]), half_of(queries, 1 - x),
+            pair_of(1 - x, firsts[1], CHUNKS[1]),
             hop1, far1, out_own, kv_own, *scalars,
         )
     )
@@ -346,7 +348,6 @@
         )
 
     far2 = send("far", give2, ACROSS)
-    q_far = send("q_far", q_give, ACROSS)
     out_far1 = send("out_far", far1, OUTWARD)
     mid1 = send("mid", between(firsts[0], CHUNKS[0], far1), INWARD)
     hop2 = send("text_z", hop1, MAJOR)

time: 138 us -> 137 us (level)
  the two profiles are of different devices: /device:TPU:4 before, /device:TPU:24 now
where the time goes in v5:
time: 137 us; the launch traced here: 136 us
  starting transfers between devices  47.9 us (35%)
  waiting for transfers between devices  37.8 us (28%)
  Pallas kernels  34.8 us (25%)
  local copies, waits for them, and re-layouts  9.22 us (7%)
  other arithmetic  5.29 us (4%)
    ppermute x22, starting transfers between devices, send(): return lax.ppermute(block, 'seq', to)  42 us
    ppermute x22, waiting for transfers between devices, send(): return lax.ppermute(block, 'seq', to)  37.8 us
    pallas_call x4, Pallas kernels, call(): pl.pallas_call(kernel, out_shape=out_shape, grid_spec=pltpu.PrefetchScala...  30.4 us
    all_to_all x1, starting transfers between devices, on_device(): lax.all_to_all(spread.reshape(YN * XN, *halves.shape[1:]), 'seq', 0, 0, a...  5.94 us
    another operation x4, local copies, waits for them, and re-layouts, pair_of(): jnp.stack([half_of(a, which, first, heads) for a in (latent_keys, latent_...  4.16 us
    pallas_call x2, Pallas kernels, gather_heads(): pl.pallas_call(gather_kernel, out_shape=jax.ShapeDtypeStruct((len(pairs),...  2.99 us
  transfers between devices with their start and end apart: 23, of which 10 were waited for; matrix products, arithmetic and copies ran while one was open for 8% of the time, Pallas kernels for 18%

profile of v5, /device:TPU:24, one launch (start us, length us, event | category | flops | bytes accessed | tf_op | source)
XLA Modules:
  0.0 136.2 jit_solution(13980853157761713990)
XLA Ops:
  1.7 5.9 %all-to-all-start = ((bf16[8,2,8,1280]{3,2,1,0:T(8,128)(2,1)}), bf16[8,2,8,1280]{3,2,1,0:T(8,128)(2,1)}, u32[]{:S(2)}, u32[]{:S(2)}) async-start(bf16[8,2,8,1280]{3,2,1,0:T(8,128)(2,1)} %bitcast.4), calls=%async_computation | async-start | bytes 655360 | tf_op jit(solution)/shard_map/all_to_all | solution.py:317
  8.3 1.6 %collective-permute-start = (s32[2,16]{1,0:T(2,128)S(1)}, s32[2,16]{1,0:T(2,128)S(1)}, u32[]{:S(2)}, u32[]{:S(2)}) collective-permute-start(s32[2,16]{1,0:T(2,128)S(1)} %concatenate.15), channel_id=1, source_target_pairs={{0,4},{2,6},{4,0},{6,2},{8,12},{10,14},{12,8},{14,10},{16,20},{18,... | collective-permute-start | bytes 392 | tf_op jit(solution)/shard_map/table/ppermute | solution.py:268
  9.8 1.0 dynamic-slice_bitcast_fusion.2
  12.4 1.2 dynamic-slice_bitcast_fusion
  18.5 5.6 %collective-permute-start.1 = (bf16[2,64,1280]{2,1,0:T(8,128)(2,1)S(1)}, bf16[2,64,1280]{2,1,0:T(8,128)(2,1)S(1)}, u32[]{:S(2)}, u32[]{:S(2)}) collective-permute-start(bf16[2,64,1280]{2,1,0:T(8,128)(2,1)S(1)} %copy_bitcast_fusion.refs_0_), channel_id=1, source_target_pairs={{0,32},{2,34},{4,36},{6,38},{8,40},{10,42},{12,44},{14,46},{16,240... | collective-permute-start | bytes 983048 | tf_op jit(solution)/shard_map/text_z/ppermute | solution.py:268
  26.3 3.8 %collective-permute-done.2.refs_1_.far = bf16[2,256,768]{2,1,0:T(8,128)(2,1)S(1)} collective-permute-done((bf16[2,256,768]{2,1,0:T(8,128)(2,1)}, bf16[2,256,768]{2,1,0:T(8,128)(2,1)S(1)}, u32[]{:S(2)}, u32[]{:S(2)}) %collective-permute-start.2) | collective-permute-done | bytes 786464 | tf_op jit(solution)/shard_map/far/ppermute | solution.py:268
  30.2 5.1 %collective-permute-done.3.refs_2_.out_own = bf16[2,256,1280]{2,1,0:T(8,128)(2,1)S(1)} collective-permute-done((bf16[2,256,1280]{2,1,0:T(8,128)(2,1)S(1)}, bf16[2,256,1280]{2,1,0:T(8,128)(2,1)S(1)}, u32[]{:S(2)}, u32[]{:S(2)}) %collective-permute-start.3) | collective-permute-done | bytes 1310752 | tf_op jit(solution)/shard_map/out_own/ppermute | solution.py:268
  36.2 1.3 collective-permute-start.6
  37.5 1.5 %collective-permute-start.5 = (bf16[256,1280]{1,0:T(8,128)(2,1)S(1)}, bf16[256,1280]{1,0:T(8,128)(2,1)S(1)}, u32[]{:S(2)}, u32[]{:S(2)}) collective-permute-start(bf16[256,1280]{1,0:T(8,128)(2,1)S(1)} %constant_dynamic-slice_fusion), channel_id=1, source_target_pairs={{0,4},{2,6},{4,0},{6,2},{8,12},{10,14},{12,8},{14,10},{16,20},{18,... | collective-permute-start | bytes 1966088 | tf_op jit(solution)/shard_map/q_far/ppermute | solution.py:268
  39.0 6.7 %collective-permute-start.8 = (bf16[2,64,1280]{2,1,0:T(8,128)(2,1)S(1)}, bf16[2,64,1280]{2,1,0:T(8,128)(2,1)S(1)}, u32[]{:S(2)}, u32[]{:S(2)}) collective-permute-start(bf16[2,64,1280]{2,1,0:T(8,128)(2,1)S(1)} %collective-permute-done.1.refs_1_), channel_id=1, source_target_pairs={{0,32},{2,34},{4,36},{6,38},{8,40},{10,42},{12,44},{14,46},{16,240... | collective-permute-start | bytes 983048 | tf_op jit(solution)/shard_map/text_z/ppermute | solution.py:268
  46.3 4.0 %collective-permute-done.8.refs_2_ = bf16[2,64,1280]{2,1,0:T(8,128)(2,1)S(1)} collective-permute-done((bf16[2,64,1280]{2,1,0:T(8,128)(2,1)S(1)}, bf16[2,64,1280]{2,1,0:T(8,128)(2,1)S(1)}, u32[]{:S(2)}, u32[]{:S(2)}) %collective-permute-start.8) | collective-permute-done | bytes 327712 | tf_op jit(solution)/shard_map/text_z/ppermute | solution.py:268
  50.3 3.7 %collective-permute-start.9 = (bf16[2,64,1280]{2,1,0:T(8,128)(2,1)S(1)}, bf16[2,64,1280]{2,1,0:T(8,128)(2,1)S(1)}, u32[]{:S(2)}, u32[]{:S(2)}) collective-permute-start(bf16[2,64,1280]{2,1,0:T(8,128)(2,1)S(1)} %collective-permute-done.8.refs_2_), channel_id=1, source_target_pairs={{0,32},{2,34},{4,36},{6,38},{8,40},{10,42},{12,44},{14,46},{16,240... | collective-permute-start | bytes 983048 | tf_op jit(solution)/shard_map/text_z/ppermute | solution.py:268
  54.0 1.2 collective-permute-done.5.q_far
  55.2 8.3 %collective-permute-done.4.refs_1_.far = bf16[2,256,512]{2,1,0:T(8,128)(2,1)S(1)} collective-permute-done((bf16[2,256,512]{2,1,0:T(8,128)(2,1)S(1)}, bf16[2,256,512]{2,1,0:T(8,128)(2,1)S(1)}, u32[]{:S(2)}, u32[]{:S(2)}) %collective-permute-start.4) | collective-permute-done | bytes 524320 | tf_op jit(solution)/shard_map/far/ppermute | solution.py:268
  63.6 1.8 %gather_heads.2 = bf16[5,2,256,768]{3,2,1,0:T(8,128)(2,1)S(1)} custom-call(bf16[2,256,1280]{2,1,0:T(8,128)(2,1)S(1)} %pad_maximum_fusion.refs_0_, bf16[2,256,768]{2,1,0:T(8,128)(2,1)S(1)} %collective-permute-done.2.refs_1_.far, bf16[2,256,1280]{2,1,0:T(8,128)(2,1)S(1)} %collective-permute-done.3.refs_2_.out_own, ...), custom_call_target="tpu_custom_call" | custom-call | tf_op jit(solution)/shard_map/gather_heads/pallas_call | solution.py:77
  65.5 6.0 %collective-permute-start.12 = (bf16[2,64,1280]{2,1,0:T(8,128)(2,1)S(1)}, bf16[2,64,1280]{2,1,0:T(8,128)(2,1)S(1)}, u32[]{:S(2)}, u32[]{:S(2)}) collective-permute-start(bf16[2,64,1280]{2,1,0:T(8,128)(2,1)S(1)} %collective-permute-done.9.refs_3_), channel_id=1, source_target_pairs={{0,32},{2,34},{4,36},{6,38},{8,40},{10,42},{12,44},{14,46},{16,240... | collective-permute-start | bytes 983048 | tf_op jit(solution)/shard_map/text_z/ppermute | solution.py:268
  71.6 4.2 %collective-permute-start.11 = (bf16[2,256,512]{2,1,0:T(8,128)(2,1)S(1)}, bf16[2,256,512]{2,1,0:T(8,128)(2,1)S(1)}, u32[]{:S(2)}, u32[]{:S(2)}) collective-permute-start(bf16[2,256,512]{2,1,0:T(8,128)(2,1)S(1)} %slice_select_fusion.1), channel_id=1, source_target_pairs={{0,8},{2,250},{4,12},{6,254},{8,16},{10,2},{12,20},{14,6},{16,24},... | collective-permute-start | bytes 1572872 | tf_op jit(solution)/shard_map/mid/ppermute | solution.py:268
  75.8 3.3 %collective-permute-done.12.refs_4_ = bf16[2,64,1280]{2,1,0:T(8,128)(2,1)S(1)} collective-permute-done((bf16[2,64,1280]{2,1,0:T(8,128)(2,1)S(1)}, bf16[2,64,1280]{2,1,0:T(8,128)(2,1)S(1)}, u32[]{:S(2)}, u32[]{:S(2)}) %collective-permute-start.12) | collective-permute-done | bytes 327712 | tf_op jit(solution)/shard_map/text_z/ppermute | solution.py:268
  79.1 3.7 %collective-permute-start.13 = (bf16[2,64,1280]{2,1,0:T(8,128)(2,1)S(1)}, bf16[2,64,1280]{2,1,0:T(8,128)(2,1)}, u32[]{:S(2)}, u32[]{:S(2)}) collective-permute-start(bf16[2,64,1280]{2,1,0:T(8,128)(2,1)S(1)} %collective-permute-done.12.refs_4_), channel_id=1, source_target_pairs={{0,32},{2,34},{4,36},{6,38},{8,40},{10,42},{12,44},{14,46},{16,240... | collective-permute-start | bytes 983048 | tf_op jit(solution)/shard_map/text_z/ppermute | solution.py:268
  82.8 10.7 %latent.2 = (f32[2,256,768]{2,1,0:T(8,128)}, f32[2,256,768]{2,1,0:T(8,128)}, f32[2,256,768]{2,1,0:T(8,128)}) custom-call(s32[1]{0:T(128)} %bitcast.12.half_ref, s32[4,8]{1,0:T(4,128)} %fusion.2.slots_ref, s32[4,8]{1,0:T(4,128)} %get-tuple-element.57.valid_ref, s32[2,2]{1,0:T(2,128)} %and_select_fusion.text_at_ref, bf16[256,2560]{1,0:T(8,128)(2,1)} %q_own.3, ...), custom_call_target="tpu_custom_call" | custom-call | flops 9663676416 | bytes 12288000 | tf_op jit(solution)/shard_map/latent/pallas_call | solution.py:200
  93.6 1.2 gather_heads.3
  95.2 1.3 pack.2.near
  96.9 2.0 %collective-permute-start.16 = (bf16[2,64,1280]{2,1,0:T(8,128)(2,1)S(1)}, bf16[2,64,1280]{2,1,0:T(8,128)(2,1)S(1)}, u32[]{:S(2)}, u32[]{:S(2)}) collective-permute-start(bf16[2,64,1280]{2,1,0:T(8,128)(2,1)S(1)} %copy_bitcast_fusion.refs_0_), channel_id=1, source_target_pairs={{0,224},{2,226},{4,228},{6,230},{8,232},{10,234},{12,236},{14,238}... | collective-permute-start | bytes 983048 | tf_op jit(solution)/shard_map/text_z/ppermute | solution.py:268
  99.0 1.1 collective-permute-done.17.cc_part
  100.0 8.0 %latent.3 = (f32[2,256,512]{2,1,0:T(8,128)}, f32[2,256,512]{2,1,0:T(8,128)}, f32[2,256,512]{2,1,0:T(8,128)}) custom-call(s32[1]{0:T(128)} %bitcast.12.half_ref, s32[4,8]{1,0:T(4,128)} %fusion.2.slots_ref, s32[4,8]{1,0:T(4,128)} %get-tuple-element.57.valid_ref, s32[2,2]{1,0:T(2,128)} %and_select_fusion.text_at_ref, bf16[256,2560]{1,0:T(8,128)(2,1)} %q_own.3, ...), custom_call_target="tpu_custom_call" | custom-call | flops 6442450944 | bytes 8192000 | tf_op jit(solution)/shard_map/latent/pallas_call | solution.py:200
  108.4 2.0 %collective-permute-done.19.cc_last = bf16[2,2,64,1280]{3,2,1,0:T(8,128)(2,1)S(1)} collective-permute-done((bf16[2,2,64,1280]{3,2,1,0:T(8,128)(2,1)S(1)}, bf16[2,2,64,1280]{3,2,1,0:T(8,128)(2,1)S(1)}, u32[]{:S(2)}, u32[]{:S(2)}) %collective-permute-start.19) | collective-permute-done | bytes 655392 | tf_op jit(solution)/shard_map/cc_text/ppermute | solution.py:268
  111.2 6.6 %finish.2 = (bf16[256,768]{1,0:T(8,128)(2,1)}, bf16[256,768]{1,0:T(8,128)(2,1)}) custom-call(s32[1]{0:T(128)} %bitcast.12.half_ref, s32[4,8]{1,0:T(4,128)} %fusion.2.slots_ref, s32[4,8]{1,0:T(4,128)} %get-tuple-element.57.valid_ref, s32[2,2]{1,0:T(2,128)} %and_select_fusion.text_at_ref, bf16[256,2560]{1,0:T(8,128)(2,1)} %q_own.3, ...), custom_call_target="tpu_custom_call" | custom-call | flops 2415919104 | bytes 3072000 | tf_op jit(solution)/shard_map/finish/pallas_call | solution.py:200
  117.9 1.5 %collective-permute-start.20 = (bf16[256,768]{1,0:T(8,128)(2,1)}, bf16[256,768]{1,0:T(8,128)(2,1)S(1)}, u32[]{:S(2)}, u32[]{:S(2)}) collective-permute-start(bf16[256,768]{1,0:T(8,128)(2,1)} %get-tuple-element.87), channel_id=1, source_target_pairs={{0,4},{2,6},{4,0},{6,2},{8,12},{10,14},{12,8},{14,10},{16,20},{18,... | collective-permute-start | bytes 1179656 | tf_op jit(solution)/shard_map/back/ppermute | solution.py:268
  119.4 5.0 %finish.3 = (bf16[256,512]{1,0:T(8,128)(2,1)}, bf16[256,512]{1,0:T(8,128)(2,1)}) custom-call(s32[1]{0:T(128)} %bitcast.12.half_ref, s32[4,8]{1,0:T(4,128)} %fusion.2.slots_ref, s32[4,8]{1,0:T(4,128)} %get-tuple-element.57.valid_ref, s32[2,2]{1,0:T(2,128)} %and_select_fusion.text_at_ref, bf16[256,2560]{1,0:T(8,128)(2,1)} %q_own.3, ...), custom_call_target="tpu_custom_call" | custom-call | flops 1610612736 | bytes 2048000 | tf_op jit(solution)/shard_map/finish/pallas_call | solution.py:200
  125.9 4.1 %collective-permute-done.20 = bf16[256,768]{1,0:T(8,128)(2,1)S(1)} collective-permute-done((bf16[256,768]{1,0:T(8,128)(2,1)}, bf16[256,768]{1,0:T(8,128)(2,1)S(1)}, u32[]{:S(2)}, u32[]{:S(2)}) %collective-permute-start.20) | collective-permute-done | bytes 393248 | tf_op jit(solution)/shard_map/back/ppermute | solution.py:268
  130.1 4.8 %collective-permute-done.21 = bf16[256,512]{1,0:T(8,128)(2,1)S(1)} collective-permute-done((bf16[256,512]{1,0:T(8,128)(2,1)}, bf16[256,512]{1,0:T(8,128)(2,1)S(1)}, u32[]{:S(2)}, u32[]{:S(2)}) %collective-permute-start.21) | collective-permute-done | bytes 262176 | tf_op jit(solution)/shard_map/back/ppermute | solution.py:268
  135.0 1.1 pad_maximum_fusion.1
  (100 shorter events, 15.5 us)
Async XLA Ops:
  1.7 12.2 %all-to-all-start = ((bf16[8,2,8,1280]{3,2,1,0:T(8,128)(2,1)}), bf16[8,2,8,1280]{3,2,1,0:T(8,128)(2,1)}, u32[]{:S(2)}, u32[]{:S(2)}) async-start(bf16[8,2,8,1280]{3,2,1,0:T(8,128)(2,1)} %bitcast.4), calls=%async_computation | async-start | bytes 655360 | tf_op jit(solution)/shard_map/all_to_all | solution.py:317
  8.3 6.6 %collective-permute-start = (s32[2,16]{1,0:T(2,128)S(1)}, s32[2,16]{1,0:T(2,128)S(1)}, u32[]{:S(2)}, u32[]{:S(2)}) collective-permute-start(s32[2,16]{1,0:T(2,128)S(1)} %concatenate.15), channel_id=1, source_target_pairs={{0,4},{2,6},{4,0},{6,2},{8,12},{10,14},{12,8},{14,10},{16,20},{18,... | collective-permute-start | bytes 392 | tf_op jit(solution)/shard_map/table/ppermute | solution.py:268
  11.8 18.3 %collective-permute-start.2 = (bf16[2,256,768]{2,1,0:T(8,128)(2,1)}, bf16[2,256,768]{2,1,0:T(8,128)(2,1)S(1)}, u32[]{:S(2)}, u32[]{:S(2)}) collective-permute-start(bf16[2,256,768]{2,1,0:T(8,128)(2,1)} %pad_maximum_fusion.2), channel_id=1, source_target_pairs={{0,4},{2,6},{4,0},{6,2},{8,12},{10,14},{12,8},{14,10},{16,20},{18,... | collective-permute-start | bytes 2359304 | tf_op jit(solution)/shard_map/far/ppermute | solution.py:268
  15.6 10.7 %copy-start.18 = (bf16[256,2560]{1,0:T(8,128)(2,1)S(1)}, bf16[256,2560]{1,0:T(8,128)(2,1)}, u32[]{:S(2)}) copy-start(bf16[256,2560]{1,0:T(8,128)(2,1)} %q_own.3) | copy-start | bytes 3932164
  15.6 19.7 %collective-permute-start.3 = (bf16[2,256,1280]{2,1,0:T(8,128)(2,1)S(1)}, bf16[2,256,1280]{2,1,0:T(8,128)(2,1)S(1)}, u32[]{:S(2)}, u32[]{:S(2)}) collective-permute-start(bf16[2,256,1280]{2,1,0:T(8,128)(2,1)S(1)} %pad_maximum_fusion.refs_0_), channel_id=1, source_target_pairs={{0,248},{2,10},{4,252},{6,14},{8,0},{10,18},{12,4},{14,22},{16,8},... | collective-permute-start | bytes 3932168 | tf_op jit(solution)/shard_map/out_own/ppermute | solution.py:268
  18.5 11.7 %collective-permute-start.1 = (bf16[2,64,1280]{2,1,0:T(8,128)(2,1)S(1)}, bf16[2,64,1280]{2,1,0:T(8,128)(2,1)S(1)}, u32[]{:S(2)}, u32[]{:S(2)}) collective-permute-start(bf16[2,64,1280]{2,1,0:T(8,128)(2,1)S(1)} %copy_bitcast_fusion.refs_0_), channel_id=1, source_target_pairs={{0,32},{2,34},{4,36},{6,38},{8,40},{10,42},{12,44},{14,46},{16,240... | collective-permute-start | bytes 983048 | tf_op jit(solution)/shard_map/text_z/ppermute | solution.py:268
  30.2 35.2 %copy-start.4 = (bf16[2,256,768]{2,1,0:T(8,128)(2,1)}, bf16[2,256,768]{2,1,0:T(8,128)(2,1)S(1)}, u32[]{:S(2)}) copy-start(bf16[2,256,768]{2,1,0:T(8,128)(2,1)S(1)} %collective-permute-done.2.refs_1_.far) | copy-start | bytes 2359300
  30.2 35.2 %copy-start.10 = (bf16[2,64,1280]{2,1,0:T(8,128)(2,1)}, bf16[2,64,1280]{2,1,0:T(8,128)(2,1)S(1)}, u32[]{:S(2)}) copy-start(bf16[2,64,1280]{2,1,0:T(8,128)(2,1)S(1)} %collective-permute-done.1.refs_1_) | copy-start | bytes 983044
  35.3 30.0 %copy-start.2 = (bf16[2,256,1280]{2,1,0:T(8,128)(2,1)}, bf16[2,256,1280]{2,1,0:T(8,128)(2,1)S(1)}, u32[]{:S(2)}) copy-start(bf16[2,256,1280]{2,1,0:T(8,128)(2,1)S(1)} %collective-permute-done.3.refs_2_.out_own) | copy-start | bytes 3932164
  35.4 28.1 %collective-permute-start.7 = (bf16[2,256,768]{2,1,0:T(8,128)(2,1)S(1)}, bf16[2,256,768]{2,1,0:T(8,128)(2,1)S(1)}, u32[]{:S(2)}, u32[]{:S(2)}) collective-permute-start(bf16[2,256,768]{2,1,0:T(8,128)(2,1)S(1)} %slice_select_fusion), channel_id=1, source_target_pairs={{0,8},{2,250},{4,12},{6,254},{8,16},{10,2},{12,20},{14,6},{16,24},... | collective-permute-start | bytes 2359304 | tf_op jit(solution)/shard_map/mid/ppermute | solution.py:268
  36.2 27.3 %collective-permute-start.6 = (bf16[2,256,768]{2,1,0:T(8,128)(2,1)S(1)}, bf16[2,256,768]{2,1,0:T(8,128)(2,1)S(1)}, u32[]{:S(2)}, u32[]{:S(2)}) collective-permute-start(bf16[2,256,768]{2,1,0:T(8,128)(2,1)S(1)} %collective-permute-done.2.refs_1_.far), channel_id=1, source_target_pairs={{0,248},{2,10},{4,252},{6,14},{8,0},{10,18},{12,4},{14,22},{16,8},... | collective-permute-start | bytes 2359304 | tf_op jit(solution)/shard_map/out_far/ppermute | solution.py:268
  37.5 17.7 %collective-permute-start.5 = (bf16[256,1280]{1,0:T(8,128)(2,1)S(1)}, bf16[256,1280]{1,0:T(8,128)(2,1)S(1)}, u32[]{:S(2)}, u32[]{:S(2)}) collective-permute-start(bf16[256,1280]{1,0:T(8,128)(2,1)S(1)} %constant_dynamic-slice_fusion), channel_id=1, source_target_pairs={{0,4},{2,6},{4,0},{6,2},{8,12},{10,14},{12,8},{14,10},{16,20},{18,... | collective-permute-start | bytes 1966088 | tf_op jit(solution)/shard_map/q_far/ppermute | solution.py:268
  39.0 11.3 %collective-permute-start.8 = (bf16[2,64,1280]{2,1,0:T(8,128)(2,1)S(1)}, bf16[2,64,1280]{2,1,0:T(8,128)(2,1)S(1)}, u32[]{:S(2)}, u32[]{:S(2)}) collective-permute-start(bf16[2,64,1280]{2,1,0:T(8,128)(2,1)S(1)} %collective-permute-done.1.refs_1_), channel_id=1, source_target_pairs={{0,32},{2,34},{4,36},{6,38},{8,40},{10,42},{12,44},{14,46},{16,240... | collective-permute-start | bytes 983048 | tf_op jit(solution)/shard_map/text_z/ppermute | solution.py:268
  45.7 17.8 %collective-permute-start.4 = (bf16[2,256,512]{2,1,0:T(8,128)(2,1)S(1)}, bf16[2,256,512]{2,1,0:T(8,128)(2,1)S(1)}, u32[]{:S(2)}, u32[]{:S(2)}) collective-permute-start(bf16[2,256,512]{2,1,0:T(8,128)(2,1)S(1)} %pad_maximum_fusion.3), channel_id=1, source_target_pairs={{0,4},{2,6},{4,0},{6,2},{8,12},{10,14},{12,8},{14,10},{16,20},{18,... | collective-permute-start | bytes 1572872 | tf_op jit(solution)/shard_map/far/ppermute | solution.py:268
  50.3 15.0 %copy-start.12 = (bf16[2,64,1280]{2,1,0:T(8,128)(2,1)}, bf16[2,64,1280]{2,1,0:T(8,128)(2,1)S(1)}, u32[]{:S(2)}) copy-start(bf16[2,64,1280]{2,1,0:T(8,128)(2,1)S(1)} %collective-permute-done.8.refs_2_) | copy-start | bytes 983044
  50.3 13.2 %collective-permute-start.9 = (bf16[2,64,1280]{2,1,0:T(8,128)(2,1)S(1)}, bf16[2,64,1280]{2,1,0:T(8,128)(2,1)S(1)}, u32[]{:S(2)}, u32[]{:S(2)}) collective-permute-start(bf16[2,64,1280]{2,1,0:T(8,128)(2,1)S(1)} %collective-permute-done.8.refs_2_), channel_id=1, source_target_pairs={{0,32},{2,34},{4,36},{6,38},{8,40},{10,42},{12,44},{14,46},{16,240... | collective-permute-start | bytes 983048 | tf_op jit(solution)/shard_map/text_z/ppermute | solution.py:268
  63.5 30.1 %copy-start.5 = (bf16[2,256,512]{2,1,0:T(8,128)(2,1)}, bf16[2,256,512]{2,1,0:T(8,128)(2,1)S(1)}, u32[]{:S(2)}) copy-start(bf16[2,256,512]{2,1,0:T(8,128)(2,1)S(1)} %collective-permute-done.4.refs_1_.far) | copy-start | bytes 1572868
  65.4 17.4 %collective-permute-start.14 = (bf16[5,2,256,768]{3,2,1,0:T(8,128)(2,1)S(1)}, bf16[5,2,256,768]{3,2,1,0:T(8,128)(2,1)}, u32[]{:S(2)}, u32[]{:S(2)}) collective-permute-start(bf16[5,2,256,768]{3,2,1,0:T(8,128)(2,1)S(1)} %gather_heads.2), channel_id=1, source_target_pairs={{0,2},{2,0},{4,6},{6,4},{8,10},{10,8},{12,14},{14,12},{16,18},{18,... | collective-permute-start | bytes 11796488 | tf_op jit(solution)/shard_map/cc_part/ppermute | solution.py:268
  65.5 13.6 %collective-permute-start.12 = (bf16[2,64,1280]{2,1,0:T(8,128)(2,1)S(1)}, bf16[2,64,1280]{2,1,0:T(8,128)(2,1)S(1)}, u32[]{:S(2)}, u32[]{:S(2)}) collective-permute-start(bf16[2,64,1280]{2,1,0:T(8,128)(2,1)S(1)} %collective-permute-done.9.refs_3_), channel_id=1, source_target_pairs={{0,32},{2,34},{4,36},{6,38},{8,40},{10,42},{12,44},{14,46},{16,240... | collective-permute-start | bytes 983048 | tf_op jit(solution)/shard_map/text_z/ppermute | solution.py:268
  71.5 22.0 %collective-permute-start.10 = (bf16[2,256,512]{2,1,0:T(8,128)(2,1)S(1)}, bf16[2,256,512]{2,1,0:T(8,128)(2,1)S(1)}, u32[]{:S(2)}, u32[]{:S(2)}) collective-permute-start(bf16[2,256,512]{2,1,0:T(8,128)(2,1)S(1)} %collective-permute-done.4.refs_1_.far), channel_id=1, source_target_pairs={{0,248},{2,10},{4,252},{6,14},{8,0},{10,18},{12,4},{14,22},{16,8},... | collective-permute-start | bytes 1572872 | tf_op jit(solution)/shard_map/out_far/ppermute | solution.py:268
  71.6 22.0 %copy-start.3 = (bf16[2,256,1280]{2,1,0:T(8,128)(2,1)S(1)}, bf16[2,256,1280]{2,1,0:T(8,128)(2,1)}, u32[]{:S(2)}) copy-start(bf16[2,256,1280]{2,1,0:T(8,128)(2,1)} %copy-done.2) | copy-start | bytes 3932164
  71.6 21.9 %collective-permute-start.11 = (bf16[2,256,512]{2,1,0:T(8,128)(2,1)S(1)}, bf16[2,256,512]{2,1,0:T(8,128)(2,1)S(1)}, u32[]{:S(2)}, u32[]{:S(2)}) collective-permute-start(bf16[2,256,512]{2,1,0:T(8,128)(2,1)S(1)} %slice_select_fusion.1), channel_id=1, source_target_pairs={{0,8},{2,250},{4,12},{6,254},{8,16},{10,2},{12,20},{14,6},{16,24},... | collective-permute-start | bytes 1572872 | tf_op jit(solution)/shard_map/mid/ppermute | solution.py:268
  79.1 14.4 %copy-start.16 = (bf16[2,64,1280]{2,1,0:T(8,128)(2,1)}, bf16[2,64,1280]{2,1,0:T(8,128)(2,1)S(1)}, u32[]{:S(2)}) copy-start(bf16[2,64,1280]{2,1,0:T(8,128)(2,1)S(1)} %collective-permute-done.12.refs_4_) | copy-start | bytes 983044
  79.1 14.5 %collective-permute-start.13 = (bf16[2,64,1280]{2,1,0:T(8,128)(2,1)S(1)}, bf16[2,64,1280]{2,1,0:T(8,128)(2,1)}, u32[]{:S(2)}, u32[]{:S(2)}) collective-permute-start(bf16[2,64,1280]{2,1,0:T(8,128)(2,1)S(1)} %collective-permute-done.12.refs_4_), channel_id=1, source_target_pairs={{0,32},{2,34},{4,36},{6,38},{8,40},{10,42},{12,44},{14,46},{16,240... | collective-permute-start | bytes 983048 | tf_op jit(solution)/shard_map/text_z/ppermute | solution.py:268
  94.9 5.1 %collective-permute-start.17 = (bf16[5,2,256,512]{3,2,1,0:T(8,128)(2,1)S(1)}, bf16[5,2,256,512]{3,2,1,0:T(8,128)(2,1)}, u32[]{:S(2)}, u32[]{:S(2)}) collective-permute-start(bf16[5,2,256,512]{3,2,1,0:T(8,128)(2,1)S(1)} %gather_heads.3), channel_id=1, source_target_pairs={{0,2},{2,0},{4,6},{6,4},{8,10},{10,8},{12,14},{14,12},{16,18},{18,... | collective-permute-start | bytes 7864328 | tf_op jit(solution)/shard_map/cc_part/ppermute | solution.py:268
  96.5 11.5 %copy-start = (bf16[6,2,64,1280]{3,2,1,0:T(8,128)(2,1)}, bf16[6,2,64,1280]{3,2,1,0:T(8,128)(2,1)S(1)}, u32[]{:S(2)}) copy-start(bf16[6,2,64,1280]{3,2,1,0:T(8,128)(2,1)S(1)} %pack.2.near) | copy-start | bytes 5898244
  96.5 11.9 %collective-permute-start.18 = (bf16[6,2,64,1280]{3,2,1,0:T(8,128)(2,1)S(1)}, bf16[6,2,64,1280]{3,2,1,0:T(8,128)(2,1)}, u32[]{:S(2)}, u32[]{:S(2)}) collective-permute-start(bf16[6,2,64,1280]{3,2,1,0:T(8,128)(2,1)S(1)} %pack.2.near), channel_id=1, source_target_pairs={{0,2},{2,0},{4,6},{6,4},{8,10},{10,8},{12,14},{14,12},{16,18},{18,... | collective-permute-start | bytes 5898248 | tf_op jit(solution)/shard_map/cc_text/ppermute | solution.py:268
  96.9 11.1 %collective-permute-start.15 = (bf16[2,64,1280]{2,1,0:T(8,128)(2,1)}, bf16[2,64,1280]{2,1,0:T(8,128)(2,1)S(1)}, u32[]{:S(2)}, u32[]{:S(2)}) collective-permute-start(bf16[2,64,1280]{2,1,0:T(8,128)(2,1)} %collective-permute-done.13.refs_5_), channel_id=1, source_target_pairs={{0,32},{2,34},{4,36},{6,38},{8,40},{10,42},{12,44},{14,46},{16,240... | collective-permute-start | bytes 983048 | tf_op jit(solution)/shard_map/text_z/ppermute | solution.py:268
  96.9 11.1 %collective-permute-start.16 = (bf16[2,64,1280]{2,1,0:T(8,128)(2,1)S(1)}, bf16[2,64,1280]{2,1,0:T(8,128)(2,1)S(1)}, u32[]{:S(2)}, u32[]{:S(2)}) collective-permute-start(bf16[2,64,1280]{2,1,0:T(8,128)(2,1)S(1)} %copy_bitcast_fusion.refs_0_), channel_id=1, source_target_pairs={{0,224},{2,226},{4,228},{6,230},{8,232},{10,234},{12,236},{14,238}... | collective-permute-start | bytes 983048 | tf_op jit(solution)/shard_map/text_z/ppermute | solution.py:268
  108.2 2.2 %collective-permute-start.19 = (bf16[2,2,64,1280]{3,2,1,0:T(8,128)(2,1)S(1)}, bf16[2,2,64,1280]{3,2,1,0:T(8,128)(2,1)S(1)}, u32[]{:S(2)}, u32[]{:S(2)}) collective-permute-start(bf16[2,2,64,1280]{3,2,1,0:T(8,128)(2,1)S(1)} %pack.3.last), channel_id=1, source_target_pairs={{0,2},{2,0},{4,6},{6,4},{8,10},{10,8},{12,14},{14,12},{16,18},{18,... | collective-permute-start | bytes 1966088 | tf_op jit(solution)/shard_map/cc_text/ppermute | solution.py:268
  117.9 12.2 %collective-permute-start.20 = (bf16[256,768]{1,0:T(8,128)(2,1)}, bf16[256,768]{1,0:T(8,128)(2,1)S(1)}, u32[]{:S(2)}, u32[]{:S(2)}) collective-permute-start(bf16[256,768]{1,0:T(8,128)(2,1)} %get-tuple-element.87), channel_id=1, source_target_pairs={{0,4},{2,6},{4,0},{6,2},{8,12},{10,14},{12,8},{14,10},{16,20},{18,... | collective-permute-start | bytes 1179656 | tf_op jit(solution)/shard_map/back/ppermute | solution.py:268
  124.3 10.6 %collective-permute-start.21 = (bf16[256,512]{1,0:T(8,128)(2,1)}, bf16[256,512]{1,0:T(8,128)(2,1)S(1)}, u32[]{:S(2)}, u32[]{:S(2)}) collective-permute-start(bf16[256,512]{1,0:T(8,128)(2,1)} %get-tuple-element.88), channel_id=1, source_target_pairs={{0,4},{2,6},{4,0},{6,2},{8,12},{10,14},{12,8},{14,10},{16,20},{18,... | collective-permute-start | bytes 786440 | tf_op jit(solution)/shard_map/back/ppermute | solution.py:268
  (15 other events, 49.3 us)
